TPU v7x, 512 devices: a whole 4x4x16 slice. The times are simulated.
512 devices in a mesh: expert: 128 (over y, z, x_lo), dp: 4 (over x_hi, core).
Axes of the slice: x: 4 (x_hi: 2, x_lo: 2; x = x_hi * 2 + x_lo), y: 4, z: 16, core: 2. Of those that a mesh axis runs over, the one named last changes fastest.
Arguments:
- tokens: bfloat16 [65536, 1024], P(('expert', 'dp')), may hold values from -6 to 6
- cotangent: bfloat16 [65536, 1024], P(('expert', 'dp')), may hold values from -6 to 6
- route_ids: int32 [65536, 2], P(('expert', 'dp')), may hold values from 0 to 127, all different within a row; in each aligned block of 128 rows (0 to 127, 128 to 255, ...) at most 3 rows name the same one
- gate_prob: bfloat16 [65536, 2], P(('expert', 'dp')), may hold values from 0.099609375 to 0.59765625
- swap_partner: int32 [128], replicated, may hold values from 0 to 127, as said below
- expert_weights: bfloat16 [128, 3, 1024, 384], P('expert', None, 'dp'), may hold values from -0.1875 to 0.1875
- first_moment: float32 [128, 3, 1024, 384], P('expert', None, 'dp'), may hold values from -6 to 6
- second_moment: float32 [128, 3, 1024, 384], P('expert', None, 'dp'), may hold values from 1 to 30
Outputs:
- token_grad: bfloat16 [65536, 1024], P(('expert', 'dp'))
- gate_grad: bfloat16 [65536, 2], P(('expert', 'dp'))
- adam_update: bfloat16 [128, 3, 1024, 384], P('expert', None, 'dp')
Inputs may be any that keep to these rules, and one draw needn't show every extreme that they name: `route_ids`: each row names 2 different experts; among the 128 tokens of one device no expert is named more than 3 times, a bound that some block reaches. `swap_partner`: s[s[e]] = e for every e; exactly 32 pairs of experts trade slots, every other expert keeps its own.
All inputs are finite; a program needn't handle non-finite values.
Results may differ from a plain program's by a relative error of at most 0.013.
Values may be sent and summed in bfloat16 or wider, within the bound.
No kernel may reach another device: no remote copies, remote signals or barrier semaphores. Data moves between devices by JAX's collectives and lax.ppermute only.
A program may use at most 64 MiB of HBM per device.

v0:
```python
import jax
import jax.numpy as jnp
from jax import lax
from jax.sharding import PartitionSpec as P

STEP = 100


BETA_ONE = 0.9
BETA_TWO = 0.95
ADAM_EPS = 1e-08


def silu_parts(pre_act):
    sigmoid_val = jax.nn.sigmoid(pre_act)
    return (pre_act * sigmoid_val, sigmoid_val * (1.0 + pre_act * (1.0 - sigmoid_val)))


def adam_step(gradient, moment_one, moment_two):
    first_new = BETA_ONE * moment_one + (1.0 - BETA_ONE) * gradient
    second_new = BETA_TWO * moment_two + (1.0 - BETA_TWO) * gradient * gradient
    first_hat = first_new / (1.0 - BETA_ONE**STEP)
    second_hat = second_new / (1.0 - BETA_TWO**STEP)
    return (first_hat / (jnp.sqrt(second_hat) + ADAM_EPS)).astype(jnp.bfloat16)


def route_weights(payload, partner):
    groups = lax.axis_size("expert")
    spread = lax.all_to_all(
        payload.reshape(groups, -1), "expert", split_axis=0, concat_axis=0, tiled=True
    )
    routed = lax.all_to_all(
        jnp.take(spread, partner, axis=0), "expert", split_axis=0, concat_axis=0, tiled=True
    )
    return routed.reshape(payload.shape)


def route_moments(moment_one, moment_two, partner):
    groups = lax.axis_size("expert")
    spread_one, spread_two = (
        lax.all_to_all(
            moment_one.reshape(groups, -1).astype(jnp.bfloat16),
            "expert",
            split_axis=0,
            concat_axis=0,
            tiled=True,
        ).astype(jnp.float32),
        lax.all_to_all(
            moment_two.reshape(groups, -1).astype(jnp.bfloat16),
            "expert",
            split_axis=0,
            concat_axis=0,
            tiled=True,
        ).astype(jnp.float32),
    )
    routed_one, routed_two = (
        lax.all_to_all(
            jnp.take(spread_one, partner, axis=0).astype(jnp.bfloat16),
            "expert",
            split_axis=0,
            concat_axis=0,
            tiled=True,
        ).astype(jnp.float32),
        lax.all_to_all(
            jnp.take(spread_two, partner, axis=0).astype(jnp.bfloat16),
            "expert",
            split_axis=0,
            concat_axis=0,
            tiled=True,
        ).astype(jnp.float32),
    )
    return (routed_one.reshape(moment_one.shape), routed_two.reshape(moment_two.shape))


def on_device(
    tokens,
    cotangent,
    route_ids,
    gate_prob,
    swap_partner,
    expert_weights,
    first_moment,
    second_moment,
):
    groups = lax.axis_size("expert")
    tok_count, model_width = tokens.shape
    topk_count = route_ids.shape[1]
    capacity = max(2, 3 * tok_count * topk_count // (2 * groups))
    flat_ids = route_ids.reshape(-1)
    expert_table = jnp.arange(groups, dtype=jnp.int32)
    picked = (flat_ids[:, None] == expert_table[None, :]).astype(jnp.int32)
    target = jnp.sum(picked * swap_partner[None, :], axis=1)
    row_rank = jnp.sum((jnp.cumsum(picked, axis=0) - 1) * picked, axis=1)
    position = target * capacity + row_rank
    buffer_rows = groups * capacity
    out_tokens = (
        jnp.zeros((buffer_rows, model_width), jnp.bfloat16)
        .at[position]
        .set(jnp.repeat(tokens, topk_count, axis=0))
        .reshape(groups, capacity, model_width)
    )
    out_cot = (
        jnp.zeros((buffer_rows, model_width), jnp.bfloat16)
        .at[position]
        .set(jnp.repeat(cotangent, topk_count, axis=0))
        .reshape(groups, capacity, model_width)
    )
    out_prob = (
        jnp.zeros((buffer_rows,), jnp.bfloat16)
        .at[position]
        .set(gate_prob.reshape(-1))
        .reshape(groups, capacity)
    )
    got_tokens, got_cot, got_prob = (
        lax.all_to_all(out_tokens, "expert", split_axis=0, concat_axis=0, tiled=True),
        lax.all_to_all(out_cot, "expert", split_axis=0, concat_axis=0, tiled=True),
        lax.all_to_all(out_prob, "expert", split_axis=0, concat_axis=0, tiled=True),
    )
    held_weights = route_weights(expert_weights, swap_partner)
    held_first, held_second = route_moments(first_moment, second_moment, swap_partner)
    whole_expert = lax.all_gather(held_weights, "dp", axis=2, tiled=True)[0]
    rows_in = got_tokens.reshape(buffer_rows, model_width)
    pre_pair = jnp.einsum(
        "rd,kdf->krf", rows_in, whole_expert[:2], preferred_element_type=jnp.float32
    )
    pre_gate = pre_pair[0]
    pre_up = pre_pair[1]
    silu_gate, silu_slope = silu_parts(pre_gate)
    hidden = (silu_gate * pre_up).astype(jnp.bfloat16)
    output = lax.dot_general(
        hidden, whole_expert[2], (((1,), (1,)), ((), ())), preferred_element_type=jnp.float32
    )
    rows_cot = got_cot.reshape(buffer_rows, model_width)
    gate_term = jnp.sum(output * rows_cot.astype(jnp.float32), axis=1).astype(jnp.bfloat16)
    scaled = (
        got_prob.reshape(-1).astype(jnp.float32)[:, None] * rows_cot.astype(jnp.float32)
    ).astype(jnp.bfloat16)
    d_hidden = jnp.dot(scaled, whole_expert[2], preferred_element_type=jnp.float32)
    d_gate = (d_hidden * pre_up * silu_slope).astype(jnp.bfloat16)
    d_up = (d_hidden * silu_gate).astype(jnp.bfloat16)
    d_pair = jnp.stack([d_gate, d_up])
    d_rows = jnp.einsum(
        "krf,kdf->rd", d_pair, whole_expert[:2], preferred_element_type=jnp.float32
    ).astype(jnp.bfloat16)
    grad_pair = jnp.einsum("rd,krf->kdf", rows_in, d_pair, preferred_element_type=jnp.float32)
    grad_down = lax.dot_general(
        scaled, hidden, (((0,), (0,)), ((), ())), preferred_element_type=jnp.float32
    )
    partial_value = jnp.concatenate([grad_pair, grad_down[None]], axis=0)[None]
    gradient = lax.psum_scatter(
        partial_value.astype(jnp.bfloat16), "dp", scatter_dimension=2, tiled=True
    ).astype(jnp.float32)
    back_rows, back_gate = (
        lax.all_to_all(
            d_rows.reshape(groups, capacity, model_width),
            "expert",
            split_axis=0,
            concat_axis=0,
            tiled=True,
        ),
        lax.all_to_all(
            gate_term.reshape(groups, capacity), "expert", split_axis=0, concat_axis=0, tiled=True
        ),
    )
    picked_rows = back_rows.reshape(buffer_rows, model_width)[position].astype(jnp.float32)
    token_grad = jnp.sum(picked_rows.reshape(tok_count, topk_count, model_width), axis=1).astype(
        jnp.bfloat16
    )
    gate_grad = back_gate.reshape(-1)[position].reshape(tok_count, topk_count)
    update = adam_step(gradient, held_first, held_second)
    return (token_grad, gate_grad, update)


def solution(mesh):
    placed = (
        P(("expert", "dp"), None),
        P(("expert", "dp"), None),
        P(("expert", "dp"), None),
        P(("expert", "dp"), None),
        P(),
        P("expert", None, "dp", None),
        P("expert", None, "dp", None),
        P("expert", None, "dp", None),
    )
    return jax.shard_map(
        on_device,
        mesh=mesh,
        in_specs=placed,
        out_specs=(
            P(("expert", "dp"), None),
            P(("expert", "dp"), None),
            P("expert", None, "dp", None),
        ),
        check_vma=False,
    )
```

profile of v0, /device:TPU:6, one launch (start us, length us, event | category | flops | bytes accessed | tf_op | source)
XLA Modules:
  0.0 534.0 jit_solution(13451851215263210766)
XLA Ops:
  13.7 20.5 %all-to-all-start = ((bf16[128,1,3]{2,1,0:T(2,128)(2,1)}), bf16[128,1,3]{2,1,0:T(2,128)(2,1)S(1)}, u32[]{:S(2)}, u32[]{:S(2)}) async-start(bf16[128,1,3]{2,1,0:T(2,128)(2,1)} %all_to_all.67), calls=%async_computation | async-start | bytes 131072 | tf_op jit(solution)/shard_map/all_to_all | solution.py:117
  40.2 9.0 %all-to-all-done = bf16[128,1,3]{2,1,0:T(2,128)(2,1)S(1)} async-done(((bf16[128,1,3]{2,1,0:T(2,128)(2,1)}), bf16[128,1,3]{2,1,0:T(2,128)(2,1)S(1)}, u32[]{:S(2)}, u32[]{:S(2)}) %all-to-all-start) | async-done | bytes 800 | tf_op jit(solution)/shard_map/all_to_all | solution.py:117
  49.8 8.5 %all-to-all-start.2 = ((bf16[128,2,1152]{2,1,0:T(2,128)(2,1)}), bf16[128,2,1152]{2,1,0:T(2,128)(2,1)S(1)}, u32[]{:S(2)}, u32[]{:S(2)}) async-start(bf16[128,2,1152]{2,1,0:T(2,128)(2,1)} %reshape.386), calls=%async_computation.2 | async-start | bytes 1179648 | tf_op jit(solution)/shard_map/all_to_all | solution.py:29
  58.6 4.2 reduce.9
  63.8 30.4 %all-to-all-done.2 = bf16[128,2,1152]{2,1,0:T(2,128)(2,1)S(1)} async-done(((bf16[128,2,1152]{2,1,0:T(2,128)(2,1)}), bf16[128,2,1152]{2,1,0:T(2,128)(2,1)S(1)}, u32[]{:S(2)}, u32[]{:S(2)}) %all-to-all-start.2) | async-done | bytes 589856 | tf_op jit(solution)/shard_map/all_to_all | solution.py:29
  94.2 6.6 %all-to-all-start.7 = ((bf16[128,2,1152]{2,1,0:T(2,128)(2,1)}), bf16[128,2,1152]{2,1,0:T(2,128)(2,1)S(1)}, u32[]{:S(2)}, u32[]{:S(2)}) async-start(bf16[128,2,1152]{2,1,0:T(2,128)(2,1)} %reshape.394), calls=%async_computation.7 | async-start | bytes 1179648 | tf_op jit(solution)/shard_map/all_to_all | solution.py:41
  101.2 4.2 reduce.10
  106.4 30.6 %all-to-all-done.7 = bf16[128,2,1152]{2,1,0:T(2,128)(2,1)S(1)} async-done(((bf16[128,2,1152]{2,1,0:T(2,128)(2,1)}), bf16[128,2,1152]{2,1,0:T(2,128)(2,1)S(1)}, u32[]{:S(2)}, u32[]{:S(2)}) %all-to-all-start.7) | async-done | bytes 589856 | tf_op jit(solution)/shard_map/all_to_all | solution.py:41
  137.0 7.1 %all-to-all-start.9 = ((bf16[128,2,1152]{2,1,0:T(2,128)(2,1)}), bf16[128,2,1152]{2,1,0:T(2,128)(2,1)S(1)}, u32[]{:S(2)}, u32[]{:S(2)}) async-start(bf16[128,2,1152]{2,1,0:T(2,128)(2,1)} %reshape.390), calls=%async_computation.10 | async-start | bytes 1179648 | tf_op jit(solution)/shard_map/all_to_all | solution.py:48
  147.8 32.4 %all-to-all-done.9 = bf16[128,2,1152]{2,1,0:T(2,128)(2,1)S(1)} async-done(((bf16[128,2,1152]{2,1,0:T(2,128)(2,1)}), bf16[128,2,1152]{2,1,0:T(2,128)(2,1)S(1)}, u32[]{:S(2)}, u32[]{:S(2)}) %all-to-all-start.9) | async-done | bytes 589856 | tf_op jit(solution)/shard_map/all_to_all | solution.py:48
  180.2 6.5 %all-to-all-start.4 = ((bf16[128,3,1024]{2,1,0:T(4,128)(2,1)}), bf16[128,3,1024]{2,1,0:T(4,128)(2,1)S(1)}, u32[]{:S(2)}, u32[]{:S(2)}) async-start(bf16[128,3,1024]{2,1,0:T(4,128)(2,1)} %reshape.292), calls=%async_computation.4 | async-start | bytes 2097152 | tf_op jit(solution)/shard_map/all_to_all | solution.py:115
  193.9 47.5 %all-to-all-done.4 = bf16[128,3,1024]{2,1,0:T(4,128)(2,1)S(1)} async-done(((bf16[128,3,1024]{2,1,0:T(4,128)(2,1)}), bf16[128,3,1024]{2,1,0:T(4,128)(2,1)S(1)}, u32[]{:S(2)}, u32[]{:S(2)}) %all-to-all-start.4) | async-done | bytes 786464 | tf_op jit(solution)/shard_map/all_to_all | solution.py:115
  241.4 7.7 %all-to-all-start.3 = ((bf16[128,2,1152]{2,1,0:T(2,128)(2,1)}), bf16[128,2,1152]{2,1,0:T(2,128)(2,1)S(1)}, u32[]{:S(2)}, u32[]{:S(2)}) async-start(bf16[128,2,1152]{2,1,0:T(2,128)(2,1)} %reshape.388), calls=%async_computation.3 | async-start | bytes 1179648 | tf_op jit(solution)/shard_map/all_to_all | solution.py:32
  254.1 31.1 %all-to-all-done.3 = bf16[128,2,1152]{2,1,0:T(2,128)(2,1)S(1)} async-done(((bf16[128,2,1152]{2,1,0:T(2,128)(2,1)}), bf16[128,2,1152]{2,1,0:T(2,128)(2,1)S(1)}, u32[]{:S(2)}, u32[]{:S(2)}) %all-to-all-start.3) | async-done | bytes 589856 | tf_op jit(solution)/shard_map/all_to_all | solution.py:32
  285.2 6.6 %all-to-all-start.1 = ((bf16[128,3,1024]{2,1,0:T(4,128)(2,1)}), bf16[128,3,1024]{2,1,0:T(4,128)(2,1)S(1)}, u32[]{:S(2)}, u32[]{:S(2)}) async-start(bf16[128,3,1024]{2,1,0:T(4,128)(2,1)} %reshape.289), calls=%async_computation.1 | async-start | bytes 2097152 | tf_op jit(solution)/shard_map/all_to_all | solution.py:116
  304.0 42.4 %all-to-all-done.1 = bf16[128,3,1024]{2,1,0:T(4,128)(2,1)S(1)} async-done(((bf16[128,3,1024]{2,1,0:T(4,128)(2,1)}), bf16[128,3,1024]{2,1,0:T(4,128)(2,1)S(1)}, u32[]{:S(2)}, u32[]{:S(2)}) %all-to-all-start.1) | async-done | bytes 786464 | tf_op jit(solution)/shard_map/all_to_all | solution.py:116
  346.5 8.1 %all-to-all-start.10 = ((bf16[128,2,1152]{2,1,0:T(2,128)(2,1)}), bf16[128,2,1152]{2,1,0:T(2,128)(2,1)}, u32[]{:S(2)}, u32[]{:S(2)}) async-start(bf16[128,2,1152]{2,1,0:T(2,128)(2,1)} %reshape.392), calls=%async_computation.11 | async-start | bytes 1179648 | tf_op jit(solution)/shard_map/all_to_all | solution.py:64
  362.6 27.8 %all-to-all-done.10 = bf16[128,2,1152]{2,1,0:T(2,128)(2,1)} async-done(((bf16[128,2,1152]{2,1,0:T(2,128)(2,1)}), bf16[128,2,1152]{2,1,0:T(2,128)(2,1)}, u32[]{:S(2)}, u32[]{:S(2)}) %all-to-all-start.10) | async-done | bytes 589856 | tf_op jit(solution)/shard_map/all_to_all | solution.py:64
  390.4 6.6 %all-to-all-start.8 = ((bf16[128,2,1152]{2,1,0:T(2,128)(2,1)}), bf16[128,2,1152]{2,1,0:T(2,128)(2,1)S(1)}, u32[]{:S(2)}, u32[]{:S(2)}) async-start(bf16[128,2,1152]{2,1,0:T(2,128)(2,1)} %reshape.396), calls=%async_computation.8 | async-start | bytes 1179648 | tf_op jit(solution)/shard_map/all_to_all | solution.py:57
  408.3 24.9 %all-to-all-done.8 = bf16[128,2,1152]{2,1,0:T(2,128)(2,1)S(1)} async-done(((bf16[128,2,1152]{2,1,0:T(2,128)(2,1)}), bf16[128,2,1152]{2,1,0:T(2,128)(2,1)S(1)}, u32[]{:S(2)}, u32[]{:S(2)}) %all-to-all-start.8) | async-done | bytes 589856 | tf_op jit(solution)/shard_map/all_to_all | solution.py:57
  433.2 6.6 %all-to-all-start.6 = ((bf16[128,1,3]{2,1,0:T(2,128)(2,1)}), bf16[128,1,3]{2,1,0:T(2,128)(2,1)S(1)}, u32[]{:S(2)}, u32[]{:S(2)}) async-start(bf16[128,1,3]{2,1,0:T(2,128)(2,1)} %convert_element_type.182), calls=%async_computation.6 | async-start | bytes 131072 | tf_op jit(solution)/shard_map/all_to_all | solution.py:161
  443.4 11.2 %all-to-all-done.6 = bf16[128,1,3]{2,1,0:T(2,128)(2,1)S(1)} async-done(((bf16[128,1,3]{2,1,0:T(2,128)(2,1)}), bf16[128,1,3]{2,1,0:T(2,128)(2,1)S(1)}, u32[]{:S(2)}, u32[]{:S(2)}) %all-to-all-start.6) | async-done | bytes 800 | tf_op jit(solution)/shard_map/all_to_all | solution.py:161
  454.7 8.0 %all-to-all-start.5 = ((bf16[128,3,1024]{2,1,0:T(4,128)(2,1)}), bf16[128,3,1024]{2,1,0:T(4,128)(2,1)}, u32[]{:S(2)}, u32[]{:S(2)}) async-start(bf16[128,3,1024]{2,1,0:T(4,128)(2,1)} %reshape.294), calls=%async_computation.5 | async-start | bytes 2097152 | tf_op jit(solution)/shard_map/all_to_all | solution.py:154
  484.5 31.3 %all-to-all-done.5 = bf16[128,3,1024]{2,1,0:T(4,128)(2,1)} async-done(((bf16[128,3,1024]{2,1,0:T(4,128)(2,1)}), bf16[128,3,1024]{2,1,0:T(4,128)(2,1)}, u32[]{:S(2)}, u32[]{:S(2)}) %all-to-all-start.5) | async-done | bytes 786464 | tf_op jit(solution)/shard_map/all_to_all | solution.py:154
  (142 shorter events, 99.1 us)
Async XLA Ops:
  7.2 27.0 %copy-start.11 = (bf16[1,3,256,384]{3,2,1,0:T(8,128)(2,1)S(1)}, bf16[1,3,256,384]{3,2,1,0:T(8,128)(2,1)}, u32[]{:S(2)}) copy-start(bf16[1,3,256,384]{3,2,1,0:T(8,128)(2,1)} %param.15) | copy-start | bytes 1769476
  13.7 35.5 %all-to-all-start = ((bf16[128,1,3]{2,1,0:T(2,128)(2,1)}), bf16[128,1,3]{2,1,0:T(2,128)(2,1)S(1)}, u32[]{:S(2)}, u32[]{:S(2)}) async-start(bf16[128,1,3]{2,1,0:T(2,128)(2,1)} %all_to_all.67), calls=%async_computation | async-start | bytes 131072 | tf_op jit(solution)/shard_map/all_to_all | solution.py:117
  39.2 19.0 %copy-start.8 = (f32[1,3,256,384]{3,2,1,0:T(8,128)S(1)}, f32[1,3,256,384]{3,2,1,0:T(8,128)}, u32[]{:S(2)}) copy-start(f32[1,3,256,384]{3,2,1,0:T(8,128)} %param.16) | copy-start | bytes 3538948
  49.8 44.5 %all-to-all-start.2 = ((bf16[128,2,1152]{2,1,0:T(2,128)(2,1)}), bf16[128,2,1152]{2,1,0:T(2,128)(2,1)S(1)}, u32[]{:S(2)}, u32[]{:S(2)}) async-start(bf16[128,2,1152]{2,1,0:T(2,128)(2,1)} %reshape.386), calls=%async_computation.2 | async-start | bytes 1179648 | tf_op jit(solution)/shard_map/all_to_all | solution.py:29
  62.8 38.0 %copy-start.9 = (f32[1,3,256,384]{3,2,1,0:T(8,128)S(1)}, f32[1,3,256,384]{3,2,1,0:T(8,128)}, u32[]{:S(2)}) copy-start(f32[1,3,256,384]{3,2,1,0:T(8,128)} %param.17) | copy-start | bytes 3538948
  94.2 42.8 %all-to-all-start.7 = ((bf16[128,2,1152]{2,1,0:T(2,128)(2,1)}), bf16[128,2,1152]{2,1,0:T(2,128)(2,1)S(1)}, u32[]{:S(2)}, u32[]{:S(2)}) async-start(bf16[128,2,1152]{2,1,0:T(2,128)(2,1)} %reshape.394), calls=%async_computation.7 | async-start | bytes 1179648 | tf_op jit(solution)/shard_map/all_to_all | solution.py:41
  105.4 38.7 %copy-start.12 = (bf16[128,1024]{1,0:T(8,128)(2,1)S(1)}, bf16[128,1024]{1,0:T(8,128)(2,1)}, u32[]{:S(2)}) copy-start(bf16[128,1024]{1,0:T(8,128)(2,1)} %param.10) | copy-start | bytes 786436
  137.0 43.2 %all-to-all-start.9 = ((bf16[128,2,1152]{2,1,0:T(2,128)(2,1)}), bf16[128,2,1152]{2,1,0:T(2,128)(2,1)S(1)}, u32[]{:S(2)}, u32[]{:S(2)}) async-start(bf16[128,2,1152]{2,1,0:T(2,128)(2,1)} %reshape.390), calls=%async_computation.10 | async-start | bytes 1179648 | tf_op jit(solution)/shard_map/all_to_all | solution.py:48
  147.8 38.9 %copy-start.18 = (s32[128]{0:T(128)S(1)}, s32[128]{0:T(128)}, u32[]{:S(2)}) copy-start(s32[128]{0:T(128)} %param.14) | copy-start | bytes 1540
  180.2 61.2 %all-to-all-start.4 = ((bf16[128,3,1024]{2,1,0:T(4,128)(2,1)}), bf16[128,3,1024]{2,1,0:T(4,128)(2,1)S(1)}, u32[]{:S(2)}, u32[]{:S(2)}) async-start(bf16[128,3,1024]{2,1,0:T(4,128)(2,1)} %reshape.292), calls=%async_computation.4 | async-start | bytes 2097152 | tf_op jit(solution)/shard_map/all_to_all | solution.py:115
  193.9 55.3 %copy-start.13 = (bf16[128,1024]{1,0:T(8,128)(2,1)S(1)}, bf16[128,1024]{1,0:T(8,128)(2,1)}, u32[]{:S(2)}) copy-start(bf16[128,1024]{1,0:T(8,128)(2,1)} %param.11) | copy-start | bytes 786436
  241.4 9.0 %copy-start = (bf16[128,3,1024]{2,1,0:T(4,128)(2,1)}, bf16[128,3,1024]{2,1,0:T(4,128)(2,1)S(1)}, u32[]{:S(2)}) copy-start(bf16[128,3,1024]{2,1,0:T(4,128)(2,1)S(1)} %all-to-all-done.4) | copy-start | bytes 2359300
  241.4 43.8 %all-to-all-start.3 = ((bf16[128,2,1152]{2,1,0:T(2,128)(2,1)}), bf16[128,2,1152]{2,1,0:T(2,128)(2,1)S(1)}, u32[]{:S(2)}, u32[]{:S(2)}) async-start(bf16[128,2,1152]{2,1,0:T(2,128)(2,1)} %reshape.388), calls=%async_computation.3 | async-start | bytes 1179648 | tf_op jit(solution)/shard_map/all_to_all | solution.py:32
  285.2 61.3 %all-to-all-start.1 = ((bf16[128,3,1024]{2,1,0:T(4,128)(2,1)}), bf16[128,3,1024]{2,1,0:T(4,128)(2,1)S(1)}, u32[]{:S(2)}, u32[]{:S(2)}) async-start(bf16[128,3,1024]{2,1,0:T(4,128)(2,1)} %reshape.289), calls=%async_computation.1 | async-start | bytes 2097152 | tf_op jit(solution)/shard_map/all_to_all | solution.py:116
  291.8 67.6 %all-gather.2.cloned.1.call-start = ((), (), s32[]{:S(2)}) async-start(), calls=%async_computation.12 | async-start | bytes 2949120 | tf_op jit(solution)/shard_map/all_gather | solution.py:121
  303.0 51.5 %copy-start.15 = (bf16[128,1,3]{2,1,0:T(2,128)(2,1)S(1)}, bf16[128,1,3]{2,1,0:T(2,128)(2,1)}, u32[]{:S(2)}) copy-start(bf16[128,1,3]{2,1,0:T(2,128)(2,1)} %copy-done.14) | copy-start | bytes 2308
  346.5 43.9 %all-to-all-start.10 = ((bf16[128,2,1152]{2,1,0:T(2,128)(2,1)}), bf16[128,2,1152]{2,1,0:T(2,128)(2,1)}, u32[]{:S(2)}, u32[]{:S(2)}) async-start(bf16[128,2,1152]{2,1,0:T(2,128)(2,1)} %reshape.392), calls=%async_computation.11 | async-start | bytes 1179648 | tf_op jit(solution)/shard_map/all_to_all | solution.py:64
  362.6 35.8 %copy-start.2 = (bf16[384,1024]{1,0:T(8,128)(2,1)S(1)}, bf16[384,1024]{1,0:T(8,128)(2,1)}, u32[]{:S(2)}) copy-start(bf16[384,1024]{1,0:T(8,128)(2,1)} %convert_element_type.154) | copy-start | bytes 2359300
  390.4 42.8 %all-to-all-start.8 = ((bf16[128,2,1152]{2,1,0:T(2,128)(2,1)}), bf16[128,2,1152]{2,1,0:T(2,128)(2,1)S(1)}, u32[]{:S(2)}, u32[]{:S(2)}) async-start(bf16[128,2,1152]{2,1,0:T(2,128)(2,1)} %reshape.396), calls=%async_computation.8 | async-start | bytes 1179648 | tf_op jit(solution)/shard_map/all_to_all | solution.py:57
  397.0 126.8 %reduce-scatter.2.cloned.1.call-start = ((), (), s32[]{:S(2)}) async-start(), calls=%async_computation.13 | async-start | bytes 2949120 | tf_op jit(solution)/shard_map/reduce_scatter | solution.py:150
  433.2 8.9 %copy-start.5 = (bf16[128,2,1152]{2,1,0:T(2,128)(2,1)}, bf16[128,2,1152]{2,1,0:T(2,128)(2,1)S(1)}, u32[]{:S(2)}) copy-start(bf16[128,2,1152]{2,1,0:T(2,128)(2,1)S(1)} %all-to-all-done.8) | copy-start | bytes 1769476
  433.2 21.5 %all-to-all-start.6 = ((bf16[128,1,3]{2,1,0:T(2,128)(2,1)}), bf16[128,1,3]{2,1,0:T(2,128)(2,1)S(1)}, u32[]{:S(2)}, u32[]{:S(2)}) async-start(bf16[128,1,3]{2,1,0:T(2,128)(2,1)} %convert_element_type.182), calls=%async_computation.6 | async-start | bytes 131072 | tf_op jit(solution)/shard_map/all_to_all | solution.py:161
  454.7 8.0 %copy-start.16 = (bf16[128,1,3]{2,1,0:T(2,128)(2,1)}, bf16[128,1,3]{2,1,0:T(2,128)(2,1)S(1)}, u32[]{:S(2)}) copy-start(bf16[128,1,3]{2,1,0:T(2,128)(2,1)S(1)} %all-to-all-done.6) | copy-start | bytes 2308
  454.7 61.1 %all-to-all-start.5 = ((bf16[128,3,1024]{2,1,0:T(4,128)(2,1)}), bf16[128,3,1024]{2,1,0:T(4,128)(2,1)}, u32[]{:S(2)}, u32[]{:S(2)}) async-start(bf16[128,3,1024]{2,1,0:T(4,128)(2,1)} %reshape.294), calls=%async_computation.5 | async-start | bytes 2097152 | tf_op jit(solution)/shard_map/all_to_all | solution.py:154
  (10 other events, 22.5 us)
Sparse Core Ops, SparseCore 0:
  297.8 38.7 all-gather.1
  405.1 54.9 reduce-scatter.1
where the time goes:
time: 544 us; the launch traced here: 534 us
  waiting for transfers between devices  319 us (59%)
  starting transfers between devices  92.9 us (17%)
  local copies, waits for them, and re-layouts  60.2 us (11%)
  other arithmetic  36.2 us (7%)
  between operations  15.3 us (3%)
  matrix products  10.9 us (2%)
    all_to_all x1, waiting for transfers between devices, on_device(): lax.all_to_all(out_tokens, 'expert', split_axis=0, concat_axis=0, tiled=T...  47.5 us
    all_to_all x1, waiting for transfers between devices, on_device(): lax.all_to_all(out_cot, 'expert', split_axis=0, concat_axis=0, tiled=True)  42.4 us
    all_to_all x1, waiting for transfers between devices, route_moments(): lax.all_to_all(moment_two.reshape(groups, -1).astype(jnp.bfloat16), 'expe...  32.4 us
    all_to_all x1, waiting for transfers between devices, on_device(): lax.all_to_all(d_rows.reshape(groups, capacity, model_width), 'expert', s...  31.3 us
    all_to_all x1, waiting for transfers between devices, route_weights(): lax.all_to_all(jnp.take(spread, partner, axis=0), 'expert', split_axis=0,...  31.1 us
    all_to_all x1, waiting for transfers between devices, route_moments(): lax.all_to_all(moment_one.reshape(groups, -1).astype(jnp.bfloat16), 'expe...  30.6 us
    all_to_all x1, waiting for transfers between devices, route_weights(): lax.all_to_all(payload.reshape(groups, -1), 'expert', split_axis=0, conca...  30.4 us
    all_to_all x1, waiting for transfers between devices, route_moments(): lax.all_to_all(jnp.take(spread_two, partner, axis=0).astype(jnp.bfloat16)...  27.8 us
  transfers between devices with their start and end apart: 13, of which 11 were waited for; matrix products, arithmetic and copies ran while one was open for 18% of the time, Pallas kernels for 0%

commit v1 on v0

v1 whole, which is shorter than its diff:
```python
import jax
import jax.numpy as jnp
from jax import lax
from jax.sharding import PartitionSpec as P

STEP = 100
BETA_ONE = 0.9
BETA_TWO = 0.95
ADAM_EPS = 1e-08
CAP = 3


def silu_parts(pre_act):
    sigmoid_val = jax.nn.sigmoid(pre_act)
    return (pre_act * sigmoid_val, sigmoid_val * (1.0 + pre_act * (1.0 - sigmoid_val)))


def adam_step(gradient, moment_one, moment_two):
    first_new = BETA_ONE * moment_one + (1.0 - BETA_ONE) * gradient
    second_new = BETA_TWO * moment_two + (1.0 - BETA_TWO) * gradient * gradient
    first_hat = first_new / (1.0 - BETA_ONE**STEP)
    second_hat = second_new / (1.0 - BETA_TWO**STEP)
    return (first_hat / (jnp.sqrt(second_hat) + ADAM_EPS)).astype(jnp.bfloat16)


def exchange(x):
    return lax.all_to_all(x, "expert", split_axis=0, concat_axis=0, tiled=True)


def on_device(
    tokens,
    cotangent,
    route_ids,
    gate_prob,
    swap_partner,
    expert_weights,
    first_moment,
    second_moment,
):
    groups = lax.axis_size("expert")
    tok_count, width = tokens.shape
    rows = groups * CAP
    f32, bf16 = jnp.float32, jnp.bfloat16

    whole = lax.all_gather(expert_weights, "dp", axis=2, tiled=True)[0]

    hot = (route_ids[:, :, None] == jnp.arange(groups, dtype=jnp.int32)).astype(bf16)
    named = hot[:, 0] + hot[:, 1]
    prob_at = hot[:, 0] * gate_prob[:, :1] + hot[:, 1] * gate_prob[:, 1:]
    step = jnp.arange(tok_count, dtype=jnp.int32)
    earlier = (step[None, :] < step[:, None]).astype(bf16)
    rank = jnp.dot(earlier, named, preferred_element_type=f32)
    picks = jnp.stack([jnp.where(rank == r, named, 0) for r in range(CAP)])
    picks_prob = picks * prob_at
    sent_x = jnp.einsum("rte,td->erd", picks, tokens, preferred_element_type=f32)
    sent_q = jnp.einsum("rte,td->erd", picks_prob, cotangent, preferred_element_type=f32)
    sent = jnp.concatenate([sent_x.astype(bf16), sent_q.astype(bf16)], axis=1)
    got = exchange(sent.reshape(groups, 6, 8, 128)).reshape(groups, 6, width)
    rows_in = got[:, :CAP].reshape(rows, width)
    scaled = got[:, CAP:].reshape(rows, width)

    pre_gate = jnp.dot(rows_in, whole[0], preferred_element_type=f32)
    pre_up = jnp.dot(rows_in, whole[1], preferred_element_type=f32)
    d_hidden = jnp.dot(scaled, whole[2], preferred_element_type=f32)
    silu_gate, silu_slope = silu_parts(pre_gate)
    hidden = (silu_gate * pre_up).astype(bf16)
    d_gate = (d_hidden * pre_up * silu_slope).astype(bf16)
    d_up = (d_hidden * silu_gate).astype(bf16)
    over_rows = (((0,), (0,)), ((), ()))
    partial = jnp.stack(
        [
            lax.dot_general(rows_in, d_gate, over_rows, preferred_element_type=f32),
            lax.dot_general(rows_in, d_up, over_rows, preferred_element_type=f32),
            lax.dot_general(scaled, hidden, over_rows, preferred_element_type=f32),
        ]
    ).astype(bf16)
    gradient = lax.psum_scatter(partial, "dp", scatter_dimension=1, tiled=True).astype(f32)

    gate_term = jnp.sum(hidden.astype(f32) * d_hidden, axis=1).astype(bf16)
    transposed = (((1,), (1,)), ((), ()))
    d_rows = (
        lax.dot_general(d_gate, whole[0], transposed, preferred_element_type=f32)
        + lax.dot_general(d_up, whole[1], transposed, preferred_element_type=f32)
    ).astype(bf16)
    returned = jnp.concatenate(
        [
            d_rows.reshape(groups, CAP * width),
            jnp.pad(gate_term.reshape(groups, CAP), ((0, 0), (0, 128 - CAP))),
        ],
        axis=1,
    )
    back = exchange(returned)
    back_rows = back[:, : CAP * width].reshape(groups, CAP, width)
    token_grad = jnp.einsum("rte,erd->td", picks, back_rows, preferred_element_type=f32).astype(bf16)
    back_gate = back[:, CAP * width : CAP * width + CAP].astype(f32)
    gate_at = jnp.sum(picks.astype(f32) * back_gate.T[:, None, :], axis=0)
    gate_grad = jnp.sum(hot.astype(f32) * gate_at[:, None, :], axis=2) / gate_prob.astype(f32)

    update = adam_step(gradient, first_moment[0], second_moment[0])
    spread = exchange(update.reshape(groups, -1))
    routed = exchange(jnp.take(spread, swap_partner, axis=0))
    return (token_grad, gate_grad.astype(bf16), routed.reshape(expert_weights.shape))


def solution(mesh):
    placed = (
        P(("expert", "dp"), None),
        P(("expert", "dp"), None),
        P(("expert", "dp"), None),
        P(("expert", "dp"), None),
        P(),
        P("expert", None, "dp", None),
        P("expert", None, "dp", None),
        P("expert", None, "dp", None),
    )
    return jax.shard_map(
        on_device,
        mesh=mesh,
        in_specs=placed,
        out_specs=(
            P(("expert", "dp"), None),
            P(("expert", "dp"), None),
            P("expert", None, "dp", None),
        ),
        check_vma=False,
    )
```

time: 544 us -> 343 us (0.63); the launches traced: 534 us -> 342 us
  waiting for transfers between devices: 319 us -> 223 us
  starting transfers between devices: 92.9 us -> 52.9 us
  local copies, waits for them, and re-layouts: 60.2 us -> 23.5 us
  other arithmetic: 36.2 us -> 15.6 us
    all_to_all x11 -> x4, waiting for transfers between devices: 319 us -> 177 us  [exchange(): return lax.all_to_all(x, 'expert', split_axis=0, concat_axis=0, tiled=True)]
    reduce_scatter x1, waiting for transfers between devices: 0.01 us -> 45.7 us  [on_device(): lax.psum_scatter(partial, 'dp', scatter_dimension=1, tiled=True).astype(f32)]
    all_to_all x11 -> x4, starting transfers between devices: 92.6 us -> 52.6 us  [exchange(): return lax.all_to_all(x, 'expert', split_axis=0, concat_axis=0, tiled=True)]
    unnamed x59 -> x38, local copies, waits for them, and re-layouts: 24.5 us -> 10.5 us
    convert_element_type x7 -> x2, other arithmetic: 10.5 us -> 1.36 us  [the longest x1 0.83 us: on_device(): (route_ids[:, :, None] == jnp.arange(groups, dtype=jnp.int32)).astype(bf16)]
    gather x6 -> x1, local copies, waits for them, and re-layouts: 8.85 us -> 0.97 us  [on_device(): routed = exchange(jnp.take(spread, swap_partner, axis=0))]
    mul x2 -> x0, other arithmetic: 7.37 us -> none  [the longest x1 3.68 us: adam_step(): second_new = BETA_TWO * moment_two + (1.0 - BETA_TWO) * gradient * gradient]
    scatter x3 -> x0, local copies, waits for them, and re-layouts: 6.48 us -> none  [the longest x1 2.41 us: on_device(): out_cot = jnp.zeros((buffer_rows, model_width), jnp.bfloat16).at[position...]
  transfers between devices with their start and end apart: 13 -> 6, of which waited for: 11 -> 5; matrix products, arithmetic and copies ran while one was open for 18% -> 7% of each run, Pallas kernels for 0% -> 0%
where the time goes in v1:
time: 343 us; the launch traced here: 342 us
  waiting for transfers between devices  223 us (65%)
  starting transfers between devices  52.9 us (15%)
  local copies, waits for them, and re-layouts  23.5 us (7%)
  other arithmetic  15.6 us (5%)
  between operations  14.5 us (4%)
  matrix products  11.8 us (3%)
    all_to_all x4, waiting for transfers between devices, exchange(): return lax.all_to_all(x, 'expert', split_axis=0, concat_axis=0, tiled=True)  177 us
    all_to_all x4, starting transfers between devices, exchange(): return lax.all_to_all(x, 'expert', split_axis=0, concat_axis=0, tiled=True)  52.6 us
    reduce_scatter x1, waiting for transfers between devices, on_device(): lax.psum_scatter(partial, 'dp', scatter_dimension=1, tiled=True).astype(f32)  45.7 us
    unnamed x38, local copies, waits for them, and re-layouts  10.5 us
    all_to_all x4, other arithmetic, exchange(): return lax.all_to_all(x, 'expert', split_axis=0, concat_axis=0, tiled=True)  9.01 us
  transfers between devices with their start and end apart: 6, of which 5 were waited for; matrix products, arithmetic and copies ran while one was open for 7% of the time, Pallas kernels for 0%

profile of v1, /device:TPU:6, one launch (start us, length us, event | category | flops | bytes accessed | tf_op | source)
XLA Modules:
  0.0 341.6 jit_solution(1927664430815054430)
XLA Ops:
  10.7 1.4 copy.40
  12.1 20.5 %all-to-all-start = ((bf16[128,6,8,128]{3,2,1,0:T(8,128)(2,1)}), bf16[128,6,8,128]{3,2,1,0:T(8,128)(2,1)S(1)}, u32[]{:S(2)}, u32[]{:S(2)}) async-start(bf16[128,6,8,128]{3,2,1,0:T(8,128)(2,1)} %copy.40), calls=%async_computation | async-start | bytes 3145728 | tf_op jit(solution)/shard_map/all_to_all | solution.py:27
  33.6 76.4 %all-to-all-done = bf16[128,6,8,128]{3,2,1,0:T(8,128)(2,1)S(1)} async-done(((bf16[128,6,8,128]{3,2,1,0:T(8,128)(2,1)}), bf16[128,6,8,128]{3,2,1,0:T(8,128)(2,1)S(1)}, u32[]{:S(2)}, u32[]{:S(2)}) %all-to-all-start) | async-done | bytes 1572896 | tf_op jit(solution)/shard_map/all_to_all | solution.py:27
  115.3 1.8 fusion.18
  117.1 1.8 fusion.20
  118.8 2.0 multiply_reduce_fusion
  123.0 1.7 pad_maximum_fusion
  124.8 45.7 %reduce-scatter.2.cloned.1.call-done = bf16[3,256,384]{2,1,0:T(8,128)(2,1)} async-done(((bf16[3,1024,384]{2,1,0:T(8,128)(2,1)}), bf16[3,256,384]{2,1,0:T(8,128)(2,1)}) %reduce-scatter.2.cloned.1.call-update) | async-done | bytes 589840 | tf_op jit(solution)/shard_map/reduce_scatter | solution.py:77
  170.5 1.9 fusion.14
  173.2 4.2 %reduce.2 = bf16[128,2304]{1,0:T(8,128)(2,1)S(1)} reduce(bf16[128,1,2304]{2,1,0:T(2,128)(2,1)S(1)} %all_to_all.31, bf16[]{:T(256)} %broadcast.67), dimensions={1}, to_apply=%all_to_all.31.reduce_sub_computation | reduce | bytes 1179650 | tf_op jit(solution)/shard_map/all_to_all | solution.py:27
  178.3 18.1 %all-to-all-start.2 = ((bf16[128,2,1152]{2,1,0:T(2,128)(2,1)}), bf16[128,2,1152]{2,1,0:T(2,128)(2,1)}, u32[]{:S(2)}, u32[]{:S(2)}) async-start(bf16[128,2,1152]{2,1,0:T(2,128)(2,1)} %reshape.140), calls=%async_computation.3 | async-start | bytes 1179648 | tf_op jit(solution)/shard_map/all_to_all | solution.py:27
  197.9 1.6 add_convert_fusion
  200.3 1.2 reduce.1
  201.5 1.9 reshape.138
  203.4 29.5 %all-to-all-done.2 = bf16[128,2,1152]{2,1,0:T(2,128)(2,1)} async-done(((bf16[128,2,1152]{2,1,0:T(2,128)(2,1)}), bf16[128,2,1152]{2,1,0:T(2,128)(2,1)}, u32[]{:S(2)}, u32[]{:S(2)}) %all-to-all-start.2) | async-done | bytes 589856 | tf_op jit(solution)/shard_map/all_to_all | solution.py:27
  232.8 6.5 %all-to-all-start.1 = ((bf16[128,2,1600]{2,1,0:T(2,128)(2,1)}), bf16[128,2,1600]{2,1,0:T(2,128)(2,1)S(1)}, u32[]{:S(2)}, u32[]{:S(2)}) async-start(bf16[128,2,1600]{2,1,0:T(2,128)(2,1)} %reshape.138), calls=%async_computation.1 | async-start | bytes 1703936 | tf_op jit(solution)/shard_map/all_to_all | solution.py:27
  239.4 3.9 %reshape.141 = bf16[128,1,2304]{2,1,0:T(2,128)(2,1)S(1)} reshape(bf16[128,2,1152]{2,1,0:T(2,128)(2,1)} %all-to-all-done.2) | data formatting | bytes 1179648
  246.5 39.3 %all-to-all-done.1 = bf16[128,2,1600]{2,1,0:T(2,128)(2,1)S(1)} async-done(((bf16[128,2,1600]{2,1,0:T(2,128)(2,1)}), bf16[128,2,1600]{2,1,0:T(2,128)(2,1)S(1)}, u32[]{:S(2)}, u32[]{:S(2)}) %all-to-all-start.1) | async-done | bytes 819232 | tf_op jit(solution)/shard_map/all_to_all | solution.py:27
  285.7 7.5 %all-to-all-start.3 = ((bf16[128,2,1152]{2,1,0:T(2,128)(2,1)}), bf16[128,2,1152]{2,1,0:T(2,128)(2,1)S(1)}, u32[]{:S(2)}, u32[]{:S(2)}) async-start(bf16[128,2,1152]{2,1,0:T(2,128)(2,1)} %reshape.142), calls=%async_computation.4 | async-start | bytes 1179648 | tf_op jit(solution)/shard_map/all_to_all | solution.py:27
  293.3 1.2 reshape.139
  294.5 1.2 copy.45
  297.7 31.7 %all-to-all-done.3 = bf16[128,2,1152]{2,1,0:T(2,128)(2,1)S(1)} async-done(((bf16[128,2,1152]{2,1,0:T(2,128)(2,1)}), bf16[128,2,1152]{2,1,0:T(2,128)(2,1)S(1)}, u32[]{:S(2)}, u32[]{:S(2)}) %all-to-all-start.3) | async-done | bytes 589856 | tf_op jit(solution)/shard_map/all_to_all | solution.py:27
  329.8 3.6 %reduce = bf16[128,2304]{1,0:T(8,128)(2,1)S(1)} reduce(bf16[128,1,2304]{2,1,0:T(2,128)(2,1)S(1)} %reshape.143, bf16[]{:T(256)} %constant.52), dimensions={1}, to_apply=%all_to_all.30.reduce_sub_computation | reduce | bytes 1179650 | tf_op jit(solution)/shard_map/all_to_all | solution.py:27
  333.4 1.3 reshape.124
  (74 shorter events, 21.4 us)
Async XLA Ops:
  7.2 1.9 copy-start
  7.2 2.5 copy-start.10
  9.0 0.6 copy-start.6
  9.0 0.6 copy-start.8
  12.1 97.9 %all-to-all-start = ((bf16[128,6,8,128]{3,2,1,0:T(8,128)(2,1)}), bf16[128,6,8,128]{3,2,1,0:T(8,128)(2,1)S(1)}, u32[]{:S(2)}, u32[]{:S(2)}) async-start(bf16[128,6,8,128]{3,2,1,0:T(8,128)(2,1)} %copy.40), calls=%async_computation | async-start | bytes 3145728 | tf_op jit(solution)/shard_map/all_to_all | solution.py:27
  32.6 82.7 %all-gather.2.cloned.1.call-start = ((), (), s32[]{:S(2)}) async-start(), calls=%async_computation.5 | async-start | bytes 2949120 | tf_op jit(solution)/shard_map/all_gather | solution.py:45
  33.3 137.1 %reduce-scatter.2.cloned.1.call-start = ((), (), s32[]{:S(2)}) async-start(), calls=%async_computation.6 | async-start | bytes 2949120 | tf_op jit(solution)/shard_map/reduce_scatter | solution.py:77
  112.1 1.6 copy-start.2
  120.8 1.5 copy-start.5
  124.7 45.7 %copy-start.3 = (f32[1,3,256,384]{3,2,1,0:T(8,128)S(1)}, f32[1,3,256,384]{3,2,1,0:T(8,128)}, u32[]{:S(2)}) copy-start(f32[1,3,256,384]{3,2,1,0:T(8,128)} %param.15) | copy-start | bytes 3538948
  124.7 45.7 %copy-start.4 = (f32[1,3,256,384]{3,2,1,0:T(8,128)S(1)}, f32[1,3,256,384]{3,2,1,0:T(8,128)}, u32[]{:S(2)}) copy-start(f32[1,3,256,384]{3,2,1,0:T(8,128)} %param.14) | copy-start | bytes 3538948
  177.4 19.9 %copy-start.1 = (bf16[1,3,1024,384]{3,2,1,0:T(8,128)(2,1)S(1)}, bf16[1,3,1024,384]{3,2,1,0:T(8,128)(2,1)}, u32[]{:S(2)}) copy-start(bf16[1,3,1024,384]{3,2,1,0:T(8,128)(2,1)} %all-gather.2.cloned.1.call-done) | copy-start | bytes 7077892
  178.3 54.5 %all-to-all-start.2 = ((bf16[128,2,1152]{2,1,0:T(2,128)(2,1)}), bf16[128,2,1152]{2,1,0:T(2,128)(2,1)}, u32[]{:S(2)}, u32[]{:S(2)}) async-start(bf16[128,2,1152]{2,1,0:T(2,128)(2,1)} %reshape.140), calls=%async_computation.3 | async-start | bytes 1179648 | tf_op jit(solution)/shard_map/all_to_all | solution.py:27
  199.5 0.8 copy-start.11
  201.5 37.9 %copy-start.14 = (s32[128]{0:T(128)S(1)}, s32[128]{0:T(128)}, u32[]{:S(2)}) copy-start(s32[128]{0:T(128)} %param.12) | copy-start | bytes 1540
  232.8 52.9 %all-to-all-start.1 = ((bf16[128,2,1600]{2,1,0:T(2,128)(2,1)}), bf16[128,2,1600]{2,1,0:T(2,128)(2,1)S(1)}, u32[]{:S(2)}, u32[]{:S(2)}) async-start(bf16[128,2,1600]{2,1,0:T(2,128)(2,1)} %reshape.138), calls=%async_computation.1 | async-start | bytes 1703936 | tf_op jit(solution)/shard_map/all_to_all | solution.py:27
  285.7 43.6 %all-to-all-start.3 = ((bf16[128,2,1152]{2,1,0:T(2,128)(2,1)}), bf16[128,2,1152]{2,1,0:T(2,128)(2,1)S(1)}, u32[]{:S(2)}, u32[]{:S(2)}) async-start(bf16[128,2,1152]{2,1,0:T(2,128)(2,1)} %reshape.142), calls=%async_computation.4 | async-start | bytes 1179648 | tf_op jit(solution)/shard_map/all_to_all | solution.py:27
  294.5 1.3 copy-start.7
  294.5 1.3 copy-start.9
  294.5 1.4 copy-start.13
  294.5 1.5 copy-start.12
Sparse Core Ops, SparseCore 0:
  35.5 39.5 all-gather.1
  124.9 45.5 reduce-scatter.1

commit v2 on v1

--- a/solution.py
+++ b/solution.py
@@ -66,16 +66,6 @@
     hidden = (silu_gate * pre_up).astype(bf16)
     d_gate = (d_hidden * pre_up * silu_slope).astype(bf16)
     d_up = (d_hidden * silu_gate).astype(bf16)
-    over_rows = (((0,), (0,)), ((), ()))
-    partial = jnp.stack(
-        [
-            lax.dot_general(rows_in, d_gate, over_rows, preferred_element_type=f32),
-            lax.dot_general(rows_in, d_up, over_rows, preferred_element_type=f32),
-            lax.dot_general(scaled, hidden, over_rows, preferred_element_type=f32),
-        ]
-    ).astype(bf16)
-    gradient = lax.psum_scatter(partial, "dp", scatter_dimension=1, tiled=True).astype(f32)
-
     gate_term = jnp.sum(hidden.astype(f32) * d_hidden, axis=1).astype(bf16)
     transposed = (((1,), (1,)), ((), ()))
     d_rows = (
@@ -89,7 +79,22 @@
         ],
         axis=1,
     )
+    rows_in, scaled, d_gate, d_up, hidden, returned = lax.optimization_barrier(
+        (rows_in, scaled, d_gate, d_up, hidden, returned)
+    )
     back = exchange(returned)
+    over_rows = (((0,), (0,)), ((), ()))
+    partial = jnp.stack(
+        [
+            lax.dot_general(rows_in, d_gate, over_rows, preferred_element_type=f32),
+            lax.dot_general(rows_in, d_up, over_rows, preferred_element_type=f32),
+            lax.dot_general(scaled, hidden, over_rows, preferred_element_type=f32),
+        ]
+    ).astype(bf16)
+    gradient = lax.psum_scatter(partial, "dp", scatter_dimension=1, tiled=True).astype(f32)
+
+    back, gradient = lax.optimization_barrier((back, gradient))
+
     back_rows = back[:, : CAP * width].reshape(groups, CAP, width)
     token_grad = jnp.einsum("rte,erd->td", picks, back_rows, preferred_element_type=f32).astype(bf16)
     back_gate = back[:, CAP * width : CAP * width + CAP].astype(f32)

time: 343 us -> 301 us (0.88)
  waiting for transfers between devices: 223 us -> 148 us
  blocking collectives: 0 us -> 54.1 us
  starting transfers between devices: 52.9 us -> 35 us
  local copies, waits for them, and re-layouts: 23.5 us -> 19.1 us
    all_to_all x0 -> x1, blocking collectives: none -> 54.1 us  [exchange(): return lax.all_to_all(x, 'expert', split_axis=0, concat_axis=0, tiled=True)]
    reduce_scatter x1, waiting for transfers between devices: 45.7 us -> 0.02 us  [on_device(): lax.psum_scatter(partial, 'dp', scatter_dimension=1, tiled=True).astype(f32)]
    all_to_all x4 -> x3, waiting for transfers between devices: 177 us -> 147 us  [exchange(): return lax.all_to_all(x, 'expert', split_axis=0, concat_axis=0, tiled=True)]
    all_to_all x4 -> x3, starting transfers between devices: 52.6 us -> 34.7 us  [exchange(): return lax.all_to_all(x, 'expert', split_axis=0, concat_axis=0, tiled=True)]
    unnamed x38 -> x30, local copies, waits for them, and re-layouts: 10.5 us -> 5.9 us
    all_to_all x4 -> x3, other arithmetic: 9.01 us -> 8.95 us  [exchange(): return lax.all_to_all(x, 'expert', split_axis=0, concat_axis=0, tiled=True)]
  transfers between devices with their start and end apart: 6 -> 5, of which waited for: 5 -> 3; matrix products, arithmetic and copies ran while one was open for 7% -> 4% of each run, Pallas kernels for 0% -> 0%
where the time goes in v2:
time: 301 us; the launch traced here: 299 us
  waiting for transfers between devices  148 us (49%)
  blocking collectives  54.1 us (18%)
  starting transfers between devices  35 us (12%)
  local copies, waits for them, and re-layouts  19.1 us (6%)
  other arithmetic  18.1 us (6%)
  between operations  14.5 us (5%)
  matrix products  10.6 us (4%)
    all_to_all x3, waiting for transfers between devices, exchange(): return lax.all_to_all(x, 'expert', split_axis=0, concat_axis=0, tiled=True)  147 us
    all_to_all x1, blocking collectives, exchange(): return lax.all_to_all(x, 'expert', split_axis=0, concat_axis=0, tiled=True)  54.1 us
    all_to_all x3, starting transfers between devices, exchange(): return lax.all_to_all(x, 'expert', split_axis=0, concat_axis=0, tiled=True)  34.7 us
    all_to_all x3, other arithmetic, exchange(): return lax.all_to_all(x, 'expert', split_axis=0, concat_axis=0, tiled=True)  8.95 us
  transfers between devices with their start and end apart: 5, of which 3 were waited for; matrix products, arithmetic and copies ran while one was open for 4% of the time, Pallas kernels for 0%

profile of v2, /device:TPU:6, one launch (start us, length us, event | category | flops | bytes accessed | tf_op | source)
XLA Modules:
  0.0 299.5 jit_solution(4885477487453948049)
XLA Ops:
  10.6 1.4 copy.40
  12.0 20.5 %all-to-all-start = ((bf16[128,6,8,128]{3,2,1,0:T(8,128)(2,1)}), bf16[128,6,8,128]{3,2,1,0:T(8,128)(2,1)S(1)}, u32[]{:S(2)}, u32[]{:S(2)}) async-start(bf16[128,6,8,128]{3,2,1,0:T(8,128)(2,1)} %copy.40), calls=%async_computation | async-start | bytes 3145728 | tf_op jit(solution)/shard_map/all_to_all | solution.py:27
  33.5 76.4 %all-to-all-done = bf16[128,6,8,128]{3,2,1,0:T(8,128)(2,1)S(1)} async-done(((bf16[128,6,8,128]{3,2,1,0:T(8,128)(2,1)}), bf16[128,6,8,128]{3,2,1,0:T(8,128)(2,1)S(1)}, u32[]{:S(2)}, u32[]{:S(2)}) %all-to-all-start) | async-done | bytes 1572896 | tf_op jit(solution)/shard_map/all_to_all | solution.py:27
  109.9 1.1 copy.41
  115.3 1.9 fusion.16
  117.2 1.7 fusion.18
  118.9 1.6 multiply_reduce_fusion
  121.8 1.3 reshape.122
  123.2 1.2 fusion.14
  126.6 1.7 pad_maximum_fusion
  128.9 1.2 reduce.1
  131.0 54.1 %all_to_all.36 = bf16[128,2,1600]{2,1,0:T(2,128)(2,1)S(1)} all-to-all(bf16[128,2,1600]{2,1,0:T(2,128)(2,1)S(1)} %reshape.138), channel_id=1, replica_groups=mesh['expert'=128,'dp'=4] {'expert'}, dimensions={0} | all-to-all | bytes 1638400 | tf_op jit(solution)/shard_map/all_to_all | solution.py:27
  185.1 1.2 reshape.139
  186.3 1.2 copy.45
  187.5 1.2 convert_element_type.79
  188.9 2.1 fusion.13
  191.3 4.2 %reduce.2 = bf16[128,2304]{1,0:T(8,128)(2,1)S(1)} reduce(bf16[128,1,2304]{2,1,0:T(2,128)(2,1)S(1)} %all_to_all.31, bf16[]{:T(256)} %broadcast.67), dimensions={1}, to_apply=%all_to_all.31.reduce_sub_computation | reduce | bytes 1179650 | tf_op jit(solution)/shard_map/all_to_all | solution.py:27
  196.5 7.6 %all-to-all-start.2 = ((bf16[128,2,1152]{2,1,0:T(2,128)(2,1)}), bf16[128,2,1152]{2,1,0:T(2,128)(2,1)S(1)}, u32[]{:S(2)}, u32[]{:S(2)}) async-start(bf16[128,2,1152]{2,1,0:T(2,128)(2,1)} %reshape.140), calls=%async_computation.3 | async-start | bytes 1179648 | tf_op jit(solution)/shard_map/all_to_all | solution.py:27
  204.1 36.7 %all-to-all-done.2 = bf16[128,2,1152]{2,1,0:T(2,128)(2,1)S(1)} async-done(((bf16[128,2,1152]{2,1,0:T(2,128)(2,1)}), bf16[128,2,1152]{2,1,0:T(2,128)(2,1)S(1)}, u32[]{:S(2)}, u32[]{:S(2)}) %all-to-all-start.2) | async-done | bytes 589856 | tf_op jit(solution)/shard_map/all_to_all | solution.py:27
  244.5 6.6 %all-to-all-start.3 = ((bf16[128,2,1152]{2,1,0:T(2,128)(2,1)}), bf16[128,2,1152]{2,1,0:T(2,128)(2,1)S(1)}, u32[]{:S(2)}, u32[]{:S(2)}) async-start(bf16[128,2,1152]{2,1,0:T(2,128)(2,1)} %reshape.142), calls=%async_computation.4 | async-start | bytes 1179648 | tf_op jit(solution)/shard_map/all_to_all | solution.py:27
  251.9 1.1 fusion.6
  253.0 34.2 %all-to-all-done.3 = bf16[128,2,1152]{2,1,0:T(2,128)(2,1)S(1)} async-done(((bf16[128,2,1152]{2,1,0:T(2,128)(2,1)}), bf16[128,2,1152]{2,1,0:T(2,128)(2,1)S(1)}, u32[]{:S(2)}, u32[]{:S(2)}) %all-to-all-start.3) | async-done | bytes 589856 | tf_op jit(solution)/shard_map/all_to_all | solution.py:27
  287.8 3.6 %reduce = bf16[128,2304]{1,0:T(8,128)(2,1)S(1)} reduce(bf16[128,1,2304]{2,1,0:T(2,128)(2,1)S(1)} %reshape.143, bf16[]{:T(256)} %constant.52), dimensions={1}, to_apply=%all_to_all.30.reduce_sub_computation | reduce | bytes 1179650 | tf_op jit(solution)/shard_map/all_to_all | solution.py:27
  291.3 1.3 reshape.124
  (66 shorter events, 19.9 us)
Async XLA Ops:
  7.2 1.8 copy-start
  7.2 2.4 copy-start.7
  9.0 0.6 copy-start.4
  12.0 97.9 %all-to-all-start = ((bf16[128,6,8,128]{3,2,1,0:T(8,128)(2,1)}), bf16[128,6,8,128]{3,2,1,0:T(8,128)(2,1)S(1)}, u32[]{:S(2)}, u32[]{:S(2)}) async-start(bf16[128,6,8,128]{3,2,1,0:T(8,128)(2,1)} %copy.40), calls=%async_computation | async-start | bytes 3145728 | tf_op jit(solution)/shard_map/all_to_all | solution.py:27
  32.5 82.7 %all-gather.2.cloned.1.call-start = ((), (), s32[]{:S(2)}) async-start(), calls=%async_computation.5 | async-start | bytes 2949120 | tf_op jit(solution)/shard_map/all_gather | solution.py:45
  33.3 154.2 %reduce-scatter.2.cloned.1.call-start = ((), (), s32[]{:S(2)}) async-start(), calls=%async_computation.6 | async-start | bytes 2949120 | tf_op jit(solution)/shard_map/reduce_scatter | solution.py:94
  112.0 1.6 copy-start.2
  115.2 3.7 %copy-start.1 = (bf16[1,3,1024,384]{3,2,1,0:T(8,128)(2,1)S(1)}, bf16[1,3,1024,384]{3,2,1,0:T(8,128)(2,1)}, u32[]{:S(2)}) copy-start(bf16[1,3,1024,384]{3,2,1,0:T(8,128)(2,1)} %all-gather.2.cloned.1.call-done) | copy-start | bytes 7077892
  124.4 1.4 copy-start.6
  187.5 1.5 copy-start.3
  195.5 8.5 %copy-start.10 = (s32[128]{0:T(128)S(1)}, s32[128]{0:T(128)}, u32[]{:S(2)}) copy-start(s32[128]{0:T(128)} %param.12) | copy-start | bytes 1540
  196.5 44.3 %all-to-all-start.2 = ((bf16[128,2,1152]{2,1,0:T(2,128)(2,1)}), bf16[128,2,1152]{2,1,0:T(2,128)(2,1)S(1)}, u32[]{:S(2)}, u32[]{:S(2)}) async-start(bf16[128,2,1152]{2,1,0:T(2,128)(2,1)} %reshape.140), calls=%async_computation.3 | async-start | bytes 1179648 | tf_op jit(solution)/shard_map/all_to_all | solution.py:27
  244.5 6.7 %copy-start.5 = (bf16[1,128,128]{2,1,0:T(8,128)(2,1)S(1)}, bf16[1,128,128]{2,1,0:T(8,128)(2,1)}, u32[]{:S(2)}) copy-start(bf16[1,128,128]{2,1,0:T(8,128)(2,1)} %copy-done.4) | copy-start | bytes 98308
  244.5 6.8 %copy-start.9 = (s32[128,2]{0,1:T(2,128)S(1)}, s32[128,2]{0,1:T(2,128)}, u32[]{:S(2)}) copy-start(s32[128,2]{0,1:T(2,128)} %param.10) | copy-start | bytes 3076
  244.5 7.0 %copy-start.8 = (bf16[128,2]{0,1:T(2,128)(2,1)S(1)}, bf16[128,2]{0,1:T(2,128)(2,1)}, u32[]{:S(2)}) copy-start(bf16[128,2]{0,1:T(2,128)(2,1)} %param.11) | copy-start | bytes 1540
  244.5 42.8 %all-to-all-start.3 = ((bf16[128,2,1152]{2,1,0:T(2,128)(2,1)}), bf16[128,2,1152]{2,1,0:T(2,128)(2,1)S(1)}, u32[]{:S(2)}, u32[]{:S(2)}) async-start(bf16[128,2,1152]{2,1,0:T(2,128)(2,1)} %reshape.142), calls=%async_computation.4 | async-start | bytes 1179648 | tf_op jit(solution)/shard_map/all_to_all | solution.py:27
Sparse Core Ops, SparseCore 0:
  35.5 39.5 all-gather.1
  128.5 49.1 reduce-scatter.1

commit v3 on v1

v3 whole, which is shorter than its diff:
```python
import jax
import jax.numpy as jnp
from jax import lax
from jax.experimental import pallas as pl
from jax.experimental.pallas import tpu as pltpu
from jax.sharding import PartitionSpec as P

STEP = 100
BETA_ONE = 0.9
BETA_TWO = 0.95
ADAM_EPS = 1e-08
CAP = 3
LANES = 128
f32, bf16 = jnp.float32, jnp.bfloat16

NN = (((1,), (0,)), ((), ()))
NT = (((1,), (1,)), ((), ()))
TN = (((0,), (0,)), ((), ()))


def mul(a, b, dims):
    return lax.dot_general(a, b, dims, preferred_element_type=f32)


def call(body, outs, scratch, flops, moved):
    return pl.pallas_call(
        body,
        out_shape=outs,
        scratch_shapes=scratch,
        compiler_params=pltpu.CompilerParams(vmem_limit_bytes=48 * 2**20),
        cost_estimate=pl.CostEstimate(flops=flops, bytes_accessed=moved, transcendentals=0),
    )


def exchange(x):
    return lax.all_to_all(x, "expert", split_axis=0, concat_axis=0, tiled=True)


def routing(ids, groups):
    tok_count = ids.shape[1]
    expert = lax.broadcasted_iota(jnp.int32, (groups, tok_count), 0)
    hots = [ids[k : k + 1, :] == expert for k in range(2)]
    named = jnp.where(hots[0] | hots[1], 1.0, 0.0)
    before = lax.broadcasted_iota(jnp.int32, (tok_count, tok_count), 0)
    after = lax.broadcasted_iota(jnp.int32, (tok_count, tok_count), 1)
    earlier = jnp.where(before < after, 1.0, 0.0).astype(bf16)
    rank = mul(named.astype(bf16), earlier, NN)
    return hots, [jnp.where(rank == r, named, 0.0) for r in range(CAP)]


def dispatch_body(ids_ref, prob_ref, tok_ref, cot_ref, out_ref, stage):
    groups, _, sub, _ = out_ref.shape
    chunks = sub // 2
    hots, picks = routing(ids_ref[...], groups)
    prob = prob_ref[...].astype(f32)
    prob_at = jnp.where(hots[0], prob[0:1, :], jnp.where(hots[1], prob[1:2, :], 0.0))
    for r in range(CAP):
        x = mul(picks[r].astype(bf16), tok_ref[...], NN)
        q = mul((picks[r] * prob_at).astype(bf16), cot_ref[...], NN)
        for c in range(chunks):
            cols = slice(c * LANES, (c + 1) * LANES)
            stage[pl.ds(c, groups, stride=sub), :] = x[:, cols]
            stage[pl.ds(chunks + c, groups, stride=sub), :] = q[:, cols]
        out_ref[:, r] = stage[...].reshape(groups, sub, LANES).astype(bf16)


def dispatch(ids_t, prob_t, tokens, cotangent, groups):
    sub = 2 * tokens.shape[1] // LANES
    return call(
        dispatch_body,
        jax.ShapeDtypeStruct((groups, CAP, sub, LANES), bf16),
        [pltpu.VMEM((groups * sub, LANES), f32)],
        2 * 2 * CAP * groups * tokens.size,
        4 * 2**20,
    )(ids_t, prob_t, tokens, cotangent)


def rows_body(got_ref, w_ref, x_ref, q_ref, da_ref, du_ref, h_ref, gate_ref, back_ref, stage, stage_back):
    groups, _, sub, _ = got_ref.shape
    chunks = sub // 2
    for r in range(CAP):
        stage[...] = got_ref[:, r].astype(f32).reshape(groups * sub, LANES)
        at = slice(r * groups, (r + 1) * groups)
        for c in range(chunks):
            cols = slice(c * LANES, (c + 1) * LANES)
            x_ref[at, cols] = stage[pl.ds(c, groups, stride=sub), :].astype(bf16)
            q_ref[at, cols] = stage[pl.ds(chunks + c, groups, stride=sub), :].astype(bf16)
    x = x_ref[...]
    a = mul(x, w_ref[0], NN)
    u = mul(x, w_ref[1], NN)
    dh = mul(q_ref[...], w_ref[2], NN)
    sig = jax.nn.sigmoid(a)
    silu = a * sig
    h = (silu * u).astype(bf16)
    da = (dh * u * (sig * (1.0 + a * (1.0 - sig)))).astype(bf16)
    du = (dh * silu).astype(bf16)
    h_ref[...] = h
    da_ref[...] = da
    du_ref[...] = du
    gate = jnp.sum(h.astype(f32) * dh, axis=1, keepdims=True)
    gate_ref[...] = jnp.broadcast_to(gate, gate_ref.shape)
    rows = mul(da, w_ref[0], NT) + mul(du, w_ref[1], NT)
    for r in range(CAP):
        for c in range(chunks):
            stage_back[pl.ds(r * chunks + c, groups, stride=CAP * chunks), :] = rows[
                r * groups : (r + 1) * groups, c * LANES : (c + 1) * LANES
            ]
    back_ref[...] = stage_back[...].reshape(back_ref.shape).astype(bf16)


def rows_products(got, whole):
    groups, _, sub, _ = got.shape
    width, hidden = whole.shape[1:]
    rows, chunks = groups * CAP, sub // 2
    like = jax.ShapeDtypeStruct
    return call(
        rows_body,
        (
            like((rows, width), bf16),
            like((rows, width), bf16),
            like((rows, hidden), bf16),
            like((rows, hidden), bf16),
            like((rows, hidden), bf16),
            like((rows, LANES), f32),
            like((groups, CAP, chunks, LANES), bf16),
        ),
        [
            pltpu.VMEM((groups * sub, LANES), f32),
            pltpu.VMEM((rows * chunks, LANES), f32),
        ],
        10 * rows * width * hidden,
        8 * 2**20,
    )(got, whole)


def grads_body(x_ref, q_ref, da_ref, du_ref, h_ref, out_ref):
    out_ref[0] = mul(x_ref[...], da_ref[...], TN).astype(bf16)
    out_ref[1] = mul(x_ref[...], du_ref[...], TN).astype(bf16)
    out_ref[2] = mul(q_ref[...], h_ref[...], TN).astype(bf16)


def weight_grads(x, q, da, du, h):
    rows, width = x.shape
    hidden = h.shape[1]
    return call(
        grads_body,
        jax.ShapeDtypeStruct((3, width, hidden), bf16),
        [],
        6 * rows * width * hidden,
        6 * 2**20,
    )(x, q, da, du, h)


def adam_body(grad_ref, one_ref, two_ref, gate_ref, out_ref, stage):
    slots, tiles, sub, _ = out_ref.shape
    lines = tiles * sub
    groups = gate_ref.shape[0] // CAP
    parts, blocks = grad_ref.shape[0] // slots, grad_ref.shape[1] // LANES
    for p in range(parts):
        at = slice(p * slots, (p + 1) * slots)
        grad = grad_ref[at, :].astype(f32)
        first_new = BETA_ONE * one_ref[at, :] + (1.0 - BETA_ONE) * grad
        second_new = BETA_TWO * two_ref[at, :] + (1.0 - BETA_TWO) * grad * grad
        first_hat = first_new * (1.0 / (1.0 - BETA_ONE**STEP))
        second_hat = second_new * (1.0 / (1.0 - BETA_TWO**STEP))
        update = first_hat / (jnp.sqrt(second_hat) + ADAM_EPS)
        for b in range(blocks):
            stage[pl.ds(p * blocks + b, slots, stride=lines), :] = update[:, b * LANES : (b + 1) * LANES]
    used = parts * blocks
    for r in range(CAP):
        stage[pl.ds(used + r, slots, stride=lines), :] = gate_ref[r * groups : (r + 1) * groups, :]
    for spare in range(used + CAP, lines):
        stage[pl.ds(spare, slots, stride=lines), :] = jnp.zeros((slots, LANES), f32)
    out_ref[...] = stage[...].reshape(out_ref.shape).astype(bf16)


def adam_update(gradient, moment_one, moment_two, gate, slots):
    lines = -(-(gradient.size // (slots * LANES) + CAP) // 8) * 8
    return call(
        adam_body,
        jax.ShapeDtypeStruct((slots, lines // 8, 8, LANES), bf16),
        [pltpu.VMEM((slots * lines, LANES), f32)],
        12 * gradient.size,
        12 * gradient.size,
    )(gradient, moment_one, moment_two, gate)


def swap_body(partner_ref, in_ref, out_ref):
    def step(d, carry):
        out_ref[d] = in_ref[partner_ref[d]]
        return carry

    lax.fori_loop(0, in_ref.shape[0], step, 0, unroll=8)


def swap_slots(partner, spread):
    vmem = pl.BlockSpec(memory_space=pltpu.VMEM)
    return pl.pallas_call(
        swap_body,
        out_shape=jax.ShapeDtypeStruct(spread.shape, spread.dtype),
        in_specs=[pl.BlockSpec(memory_space=pltpu.SMEM), vmem],
        out_specs=vmem,
        compiler_params=pltpu.CompilerParams(vmem_limit_bytes=48 * 2**20),
        cost_estimate=pl.CostEstimate(flops=0, bytes_accessed=4 * spread.size, transcendentals=0),
    )(partner, spread)


def collect_body(in_ref, out_ref, stage):
    slots, tiles, sub, _ = in_ref.shape
    lines = tiles * sub
    stage[...] = in_ref[...].astype(f32).reshape(slots * lines, LANES)
    parts, blocks = out_ref.shape[0] // slots, out_ref.shape[1] // LANES
    for p in range(parts):
        for b in range(blocks):
            out_ref[p * slots : (p + 1) * slots, b * LANES : (b + 1) * LANES] = stage[
                pl.ds(p * blocks + b, slots, stride=lines), :
            ].astype(bf16)


def collect(routed, shape):
    return call(
        collect_body,
        jax.ShapeDtypeStruct(shape, bf16),
        [pltpu.VMEM((routed.size // LANES, LANES), f32)],
        0,
        4 * routed.size,
    )(routed)


def combine_body(ids_ref, prob_ref, back_ref, gates_ref, tok_ref, gate_ref, stage, rows, gate_stage):
    groups, _, chunks, _ = back_ref.shape
    lines = CAP * chunks
    hots, picks = routing(ids_ref[...], groups)
    stage[...] = back_ref[...].astype(f32).reshape(groups * lines, LANES)
    for r in range(CAP):
        for c in range(chunks):
            rows[r * groups : (r + 1) * groups, c * LANES : (c + 1) * LANES] = stage[
                pl.ds(r * chunks + c, groups, stride=lines), :
            ].astype(bf16)
    tok_ref[...] = mul(jnp.concatenate(picks, axis=0).astype(bf16), rows[...], TN).astype(bf16)
    slots, tiles, sub, _ = gates_ref.shape
    gate_stage[...] = gates_ref[:, tiles - 1].astype(f32).reshape(slots * sub, LANES)
    first = sub - (tiles * sub - GATE_LINE)
    gate_at = sum(picks[r] * gate_stage[pl.ds(first + r, groups, stride=sub), :] for r in range(CAP))
    for k in range(2):
        total = jnp.sum(jnp.where(hots[k], gate_at, 0.0), axis=0, keepdims=True)
        gate_ref[k : k + 1, :] = total / prob_ref[k : k + 1, :].astype(f32)


GATE_LINE = 18


def combine(ids_t, prob_t, back, spread):
    groups, _, chunks, _ = back.shape
    tok_count = ids_t.shape[1]
    width = chunks * LANES
    return call(
        combine_body,
        (
            jax.ShapeDtypeStruct((tok_count, width), bf16),
            jax.ShapeDtypeStruct((2, tok_count), f32),
        ),
        [
            pltpu.VMEM((groups * CAP * chunks, LANES), f32),
            pltpu.VMEM((groups * CAP, width), bf16),
            pltpu.VMEM((spread.shape[0] * 8, LANES), f32),
        ],
        2 * CAP * groups * tok_count * width,
        4 * 2**20,
    )(ids_t, prob_t, back, spread)


def on_device(
    tokens,
    cotangent,
    route_ids,
    gate_prob,
    swap_partner,
    expert_weights,
    first_moment,
    second_moment,
):
    groups = lax.axis_size("expert")
    hidden = expert_weights.shape[3]
    flat = (-1, hidden)
    ids_t, prob_t = route_ids.T, gate_prob.T

    whole = lax.all_gather(expert_weights, "dp", axis=2, tiled=True)[0]
    got = exchange(dispatch(ids_t, prob_t, tokens, cotangent, groups))
    x, q, da, du, h, gate, returned = rows_products(got, whole)
    back = exchange(returned)
    partial = weight_grads(x, q, da, du, h)
    gradient = lax.psum_scatter(partial, "dp", scatter_dimension=1, tiled=True)
    staged = adam_update(
        gradient.reshape(flat), first_moment.reshape(flat), second_moment.reshape(flat), gate, groups
    )
    back, staged = lax.optimization_barrier((back, staged))
    spread = exchange(staged)
    routed = exchange(swap_slots(swap_partner, spread))
    token_grad, gate_grad = combine(ids_t, prob_t, back, spread)
    update = collect(routed, gradient.reshape(flat).shape)
    return (token_grad, gate_grad.T.astype(bf16), update.reshape(expert_weights.shape))


def solution(mesh):
    placed = (
        P(("expert", "dp"), None),
        P(("expert", "dp"), None),
        P(("expert", "dp"), None),
        P(("expert", "dp"), None),
        P(),
        P("expert", None, "dp", None),
        P("expert", None, "dp", None),
        P("expert", None, "dp", None),
    )
    return jax.shard_map(
        on_device,
        mesh=mesh,
        in_specs=placed,
        out_specs=(
            P(("expert", "dp"), None),
            P(("expert", "dp"), None),
            P("expert", None, "dp", None),
        ),
        check_vma=False,
    )
```

time: 343 us -> 297 us (0.87)
  waiting for transfers between devices: 223 us -> 160 us
  blocking collectives: 0 us -> 60.6 us
  Pallas kernels: 0 us -> 17.7 us
  local copies, waits for them, and re-layouts: 23.5 us -> 6.26 us
  starting transfers between devices: 52.9 us -> 36.3 us
  other arithmetic: 15.6 us -> 0.51 us
  matrix products: 11.8 us -> 0 us
    all_to_all x4 -> x3, waiting for transfers between devices: 177 us -> 77.1 us  [exchange(): return lax.all_to_all(x, 'expert', split_axis=0, concat_axis=0, tiled=True)]
    all_to_all x0 -> x1, blocking collectives: none -> 60.6 us  [exchange(): return lax.all_to_all(x, 'expert', split_axis=0, concat_axis=0, tiled=True)]
    all_gather x1, waiting for transfers between devices: 0.02 us -> 41.8 us  [on_device(): whole = lax.all_gather(expert_weights, 'dp', axis=2, tiled=True)[0]]
    pallas_call x0 -> x7, Pallas kernels: none -> 17.7 us  [the longest x1 6.18 us: rows_products(): call(rows_body, (like((rows, width), bf16), like((rows, width), bf16), li...]
    all_to_all x4 -> x3, starting transfers between devices: 52.6 us -> 36.2 us  [exchange(): return lax.all_to_all(x, 'expert', split_axis=0, concat_axis=0, tiled=True)]
    dot_general x12 -> x0, matrix products: 11.8 us -> none  [the longest x1 1.97 us: on_device(): d_hidden = jnp.dot(scaled, whole[2], preferred_element_type=f32)]
    all_to_all x4 -> x0, other arithmetic: 9.01 us -> none  [exchange(): return lax.all_to_all(x, 'expert', split_axis=0, concat_axis=0, tiled=True)]
    reduce_scatter x1, waiting for transfers between devices: 45.7 us -> 40.1 us  [on_device(): gradient = lax.psum_scatter(partial, 'dp', scatter_dimension=1, tiled=True)]
  transfers between devices with their start and end apart: 6 -> 5, of which waited for: 5 -> 4; matrix products, arithmetic and copies ran while one was open for 7% -> 0% of each run, Pallas kernels for 0% -> 1%
where the time goes in v3:
time: 297 us; the launch traced here: 295 us
  waiting for transfers between devices  160 us (54%)
  blocking collectives  60.6 us (20%)
  starting transfers between devices  36.3 us (12%)
  Pallas kernels  17.7 us (6%)
  between operations  14.1 us (5%)
  local copies, waits for them, and re-layouts  6.26 us (2%)
    all_to_all x3, waiting for transfers between devices, exchange(): return lax.all_to_all(x, 'expert', split_axis=0, concat_axis=0, tiled=True)  77.1 us
    all_to_all x1, blocking collectives, exchange(): return lax.all_to_all(x, 'expert', split_axis=0, concat_axis=0, tiled=True)  60.6 us
    all_gather x1, waiting for transfers between devices, on_device(): whole = lax.all_gather(expert_weights, 'dp', axis=2, tiled=True)[0]  41.8 us
    reduce_scatter x1, waiting for transfers between devices, on_device(): gradient = lax.psum_scatter(partial, 'dp', scatter_dimension=1, tiled=True)  40.1 us
    all_to_all x3, starting transfers between devices, exchange(): return lax.all_to_all(x, 'expert', split_axis=0, concat_axis=0, tiled=True)  36.2 us
    unnamed x24, local copies, waits for them, and re-layouts  6.26 us
    pallas_call x1, Pallas kernels, rows_products(): call(rows_body, (like((rows, width), bf16), like((rows, width), bf16), li...  6.18 us
  transfers between devices with their start and end apart: 5, of which 4 were waited for; matrix products, arithmetic and copies ran while one was open for 0% of the time, Pallas kernels for 1%

profile of v3, /device:TPU:6, one launch (start us, length us, event | category | flops | bytes accessed | tf_op | source)
XLA Modules:
  0.0 295.2 jit_solution(6988348873324772459)
XLA Ops:
  7.2 0.9 copy-done.3
  8.1 0.9 copy-done.4
  9.1 0.7 copy-done.7
  9.7 0.7 copy-done.9
  10.4 2.6 shard_map.103
  13.0 20.5 %all-to-all-start = ((bf16[128,3,16,128]{3,2,1,0:T(8,128)(2,1)}), bf16[128,3,16,128]{3,2,1,0:T(8,128)(2,1)S(1)}, u32[]{:S(2)}, u32[]{:S(2)}) async-start(bf16[128,3,16,128]{3,2,1,0:T(8,128)(2,1)} %shard_map.103), calls=%async_computation | async-start | bytes 3145728 | tf_op jit(solution)/shard_map/all_to_all | solution.py:36
  33.6 0.7 all-gather.2.cloned.1.call-update
  34.3 41.8 %all-gather.2.cloned.1.call-done = bf16[1,3,1024,384]{3,2,1,0:T(8,128)(2,1)} async-done(((bf16[1,3,256,384]{3,2,1,0:T(8,128)(2,1)}), bf16[1,3,1024,384]{3,2,1,0:T(8,128)(2,1)}) %all-gather.2.cloned.1.call-update) | async-done | bytes 2359312 | tf_op jit(solution)/shard_map/all_gather | solution.py:288
  76.1 34.8 %all-to-all-done.got_ref = bf16[128,3,16,128]{3,2,1,0:T(8,128)(2,1)S(1)} async-done(((bf16[128,3,16,128]{3,2,1,0:T(8,128)(2,1)}), bf16[128,3,16,128]{3,2,1,0:T(8,128)(2,1)S(1)}, u32[]{:S(2)}, u32[]{:S(2)}) %all-to-all-start) | async-done | bytes 1572896 | tf_op jit(solution)/shard_map/all_to_all | solution.py:36
  110.9 6.2 %shard_map.104 = (bf16[384,1024]{1,0:T(8,128)(2,1)S(1)}, bf16[384,1024]{1,0:T(8,128)(2,1)S(1)}, bf16[384,384]{1,0:T(8,128)(2,1)S(1)}, bf16[384,384]{1,0:T(8,128)...) custom-call(bf16[128,3,16,128]{3,2,1,0:T(8,128)(2,1)S(1)} %all-to-all-done.got_ref, ...), custom_call_target="tpu_custom_call" | custom-call | flops 1509949440 | bytes 8388608 | tf_op jit(solution)/shard_map/pallas_call | solution.py:116
  117.1 0.7 copy-done.5
  117.8 3.1 %shard_map.105 = bf16[3,1024,384]{2,1,0:T(8,128)(2,1)} custom-call(bf16[384,1024]{1,0:T(8,128)(2,1)S(1)} %get-tuple-element.15.x_ref, bf16[384,1024]{1,0:T(8,128)(2,1)S(1)} %get-tuple-element.16.q_ref, bf16[384,384]{1,0:T(8,128)(2,1)S(1)} %get-tuple-element.17.da_ref, bf16[384,384]{1,0:T(8,128)(2,1)S(1)} %get-tuple-element.18.du_ref, ...), custom_call_target="tpu_custom_call" | custom-call | flops 905969664 | bytes 6291456 | tf_op jit(solution)/shard_map/pallas_call | solution.py:145
  120.9 8.2 %all-to-all-start.1 = ((bf16[128,3,8,128]{3,2,1,0:T(8,128)(2,1)}), bf16[128,3,8,128]{3,2,1,0:T(8,128)(2,1)S(1)}, u32[]{:S(2)}, u32[]{:S(2)}) async-start(bf16[128,3,8,128]{3,2,1,0:T(8,128)(2,1)} %get-tuple-element.14), calls=%async_computation.1 | async-start | bytes 1572864 | tf_op jit(solution)/shard_map/all_to_all | solution.py:36
  129.1 40.1 %reduce-scatter.2.cloned.1.call-done = bf16[3,256,384]{2,1,0:T(8,128)(2,1)} async-done(((bf16[3,1024,384]{2,1,0:T(8,128)(2,1)}), bf16[3,256,384]{2,1,0:T(8,128)(2,1)}) %reduce-scatter.2.cloned.1.call-update) | async-done | bytes 589840 | tf_op jit(solution)/shard_map/reduce_scatter | solution.py:293
  169.2 1.3 copy-done.1
  170.5 1.1 copy-done.2
  171.6 1.5 shard_map.106
  173.2 60.6 %all_to_all.20.gates_ref.in_ref = bf16[128,3,8,128]{3,2,1,0:T(8,128)(2,1)S(1)} all-to-all(bf16[128,3,8,128]{3,2,1,0:T(8,128)(2,1)S(1)} %shard_map.106), channel_id=1, replica_groups=mesh['expert'=128,'dp'=4] {'expert'}, dimensions={0} | all-to-all | bytes 1572864 | tf_op jit(solution)/shard_map/all_to_all | solution.py:36
  233.8 1.6 shard_map.108
  235.4 7.5 %all-to-all-start.3 = ((bf16[128,3,8,128]{3,2,1,0:T(8,128)(2,1)}), bf16[128,3,8,128]{3,2,1,0:T(8,128)(2,1)S(1)}, u32[]{:S(2)}, u32[]{:S(2)}) async-start(bf16[128,3,8,128]{3,2,1,0:T(8,128)(2,1)} %shard_map.108), calls=%async_computation.4 | async-start | bytes 1572864 | tf_op jit(solution)/shard_map/all_to_all | solution.py:36
  242.9 1.5 shard_map.107
  244.4 0.5 convert_bitcast_fusion
  244.9 42.3 %all-to-all-done.3.in_ref = bf16[128,3,8,128]{3,2,1,0:T(8,128)(2,1)S(1)} async-done(((bf16[128,3,8,128]{3,2,1,0:T(8,128)(2,1)}), bf16[128,3,8,128]{3,2,1,0:T(8,128)(2,1)S(1)}, u32[]{:S(2)}, u32[]{:S(2)}) %all-to-all-start.3) | async-done | bytes 786464 | tf_op jit(solution)/shard_map/all_to_all | solution.py:36
  287.2 1.1 shard_map.109
  (21 shorter events, 0.1 us)
Async XLA Ops:
  7.2 1.0 copy-start.3
  8.1 0.9 copy-start.4
  9.1 0.7 copy-start.7
  9.7 0.7 copy-start.9
  13.0 97.9 %all-to-all-start = ((bf16[128,3,16,128]{3,2,1,0:T(8,128)(2,1)}), bf16[128,3,16,128]{3,2,1,0:T(8,128)(2,1)S(1)}, u32[]{:S(2)}, u32[]{:S(2)}) async-start(bf16[128,3,16,128]{3,2,1,0:T(8,128)(2,1)} %shard_map.103), calls=%async_computation | async-start | bytes 3145728 | tf_op jit(solution)/shard_map/all_to_all | solution.py:36
  33.6 42.6 %all-gather.2.cloned.1.call-start = ((), (), s32[]{:S(2)}) async-start(), calls=%async_computation.5 | async-start | bytes 2949120 | tf_op jit(solution)/shard_map/all_gather | solution.py:288
  34.3 134.9 %reduce-scatter.2.cloned.1.call-start = ((), (), s32[]{:S(2)}) async-start(), calls=%async_computation.6 | async-start | bytes 2949120 | tf_op jit(solution)/shard_map/reduce_scatter | solution.py:293
  117.1 0.7 copy-start.5
  120.9 48.4 %copy-start = (f32[1,3,256,384]{3,2,1,0:T(8,128)S(1)}, f32[1,3,256,384]{3,2,1,0:T(8,128)}, u32[]{:S(2)}) copy-start(f32[1,3,256,384]{3,2,1,0:T(8,128)} %param.14) | copy-start | bytes 3538948
  120.9 48.4 %copy-start.6 = (f32[384,128]{1,0:T(8,128)S(1)}, f32[384,128]{1,0:T(8,128)}, u32[]{:S(2)}) copy-start(f32[384,128]{1,0:T(8,128)} %copy-done.5) | copy-start | bytes 589828
  120.9 52.2 %all-to-all-start.1 = ((bf16[128,3,8,128]{3,2,1,0:T(8,128)(2,1)}), bf16[128,3,8,128]{3,2,1,0:T(8,128)(2,1)S(1)}, u32[]{:S(2)}, u32[]{:S(2)}) async-start(bf16[128,3,8,128]{3,2,1,0:T(8,128)(2,1)} %get-tuple-element.14), calls=%async_computation.1 | async-start | bytes 1572864 | tf_op jit(solution)/shard_map/all_to_all | solution.py:36
  169.2 1.3 copy-start.1
  170.5 1.1 copy-start.2
  173.1 60.6 %copy-start.11 = (s32[128]{0:T(128)S(1)}, s32[128]{0:T(128)}, u32[]{:S(2)}) copy-start(s32[128]{0:T(128)} %partner_ref.1) | copy-start | bytes 1540
  233.8 9.2 %copy-start.8 = (s32[128,2]{0,1:T(2,128)S(1)}, s32[128,2]{0,1:T(2,128)}, u32[]{:S(2)}) copy-start(s32[128,2]{0,1:T(2,128)} %param.10) | copy-start | bytes 3076
  233.8 9.2 %copy-start.10 = (bf16[128,2]{0,1:T(2,128)(2,1)S(1)}, bf16[128,2]{0,1:T(2,128)(2,1)}, u32[]{:S(2)}) copy-start(bf16[128,2]{0,1:T(2,128)(2,1)} %param.11) | copy-start | bytes 1540
  235.4 51.8 %all-to-all-start.3 = ((bf16[128,3,8,128]{3,2,1,0:T(8,128)(2,1)}), bf16[128,3,8,128]{3,2,1,0:T(8,128)(2,1)S(1)}, u32[]{:S(2)}, u32[]{:S(2)}) async-start(bf16[128,3,8,128]{3,2,1,0:T(8,128)(2,1)} %shard_map.108), calls=%async_computation.4 | async-start | bytes 1572864 | tf_op jit(solution)/shard_map/all_to_all | solution.py:36
Sparse Core Ops, SparseCore 0:
  36.5 39.5 all-gather.1
  121.0 48.1 reduce-scatter.1

commit v4 on v3

v4 whole, which is shorter than its diff:
```python
import functools

import jax
import jax.numpy as jnp
from jax import lax
from jax.experimental import pallas as pl
from jax.experimental.pallas import tpu as pltpu
from jax.sharding import PartitionSpec as P

STEP = 100
BETA_ONE = 0.9
BETA_TWO = 0.95
ADAM_EPS = 1e-08
CAP = 3
LANES = 128
f32, bf16 = jnp.float32, jnp.bfloat16

NN = (((1,), (0,)), ((), ()))
NT = (((1,), (1,)), ((), ()))
TN = (((0,), (0,)), ((), ()))


def mul(a, b, dims):
    return lax.dot_general(a, b, dims, preferred_element_type=f32)


def call(body, outs, scratch, flops, moved):
    return pl.pallas_call(
        body,
        out_shape=outs,
        scratch_shapes=scratch,
        compiler_params=pltpu.CompilerParams(vmem_limit_bytes=48 * 2**20),
        cost_estimate=pl.CostEstimate(flops=flops, bytes_accessed=moved, transcendentals=0),
    )


def exchange(x):
    return lax.all_to_all(x, "expert", split_axis=0, concat_axis=0, tiled=True)


def routing(ids, groups):
    tok_count = ids.shape[1]
    expert = lax.broadcasted_iota(jnp.int32, (groups, tok_count), 0)
    hots = [ids[k : k + 1, :] == expert for k in range(2)]
    named = jnp.where(hots[0] | hots[1], 1.0, 0.0)
    before = lax.broadcasted_iota(jnp.int32, (tok_count, tok_count), 0)
    after = lax.broadcasted_iota(jnp.int32, (tok_count, tok_count), 1)
    earlier = jnp.where(before < after, 1.0, 0.0).astype(bf16)
    rank = mul(named.astype(bf16), earlier, NN)
    return hots, [jnp.where(rank == r, named, 0.0) for r in range(CAP)]


def dispatch_body(ids_ref, prob_ref, tok_ref, cot_ref, out_ref, stage):
    groups, _, sub, _ = out_ref.shape
    chunks = sub // 2
    hots, picks = routing(ids_ref[...], groups)
    prob = prob_ref[...].astype(f32)
    prob_at = jnp.where(hots[0], prob[0:1, :], jnp.where(hots[1], prob[1:2, :], 0.0))
    for r in range(CAP):
        x = mul(picks[r].astype(bf16), tok_ref[...], NN)
        q = mul((picks[r] * prob_at).astype(bf16), cot_ref[...], NN)
        for c in range(chunks):
            cols = slice(c * LANES, (c + 1) * LANES)
            stage[pl.ds(c, groups, stride=sub), :] = x[:, cols]
            stage[pl.ds(chunks + c, groups, stride=sub), :] = q[:, cols]
        out_ref[:, r] = stage[...].reshape(groups, sub, LANES).astype(bf16)


def dispatch(ids_t, prob_t, tokens, cotangent, groups):
    sub = 2 * tokens.shape[1] // LANES
    return call(
        dispatch_body,
        jax.ShapeDtypeStruct((groups, CAP, sub, LANES), bf16),
        [pltpu.VMEM((groups * sub, LANES), f32)],
        2 * 2 * CAP * groups * tokens.size,
        4 * 2**20,
    )(ids_t, prob_t, tokens, cotangent)


def rows_body(got_ref, w_ref, x_ref, q_ref, da_ref, du_ref, h_ref, back_ref, rest_ref, last_ref, stage):
    groups, _, sub, _ = got_ref.shape
    chunks = sub // 2
    for r in range(CAP):
        stage[...] = got_ref[:, r].astype(f32).reshape(groups * sub, LANES)
        at = slice(r * groups, (r + 1) * groups)
        for c in range(chunks):
            cols = slice(c * LANES, (c + 1) * LANES)
            x_ref[at, cols] = stage[pl.ds(c, groups, stride=sub), :].astype(bf16)
            q_ref[at, cols] = stage[pl.ds(chunks + c, groups, stride=sub), :].astype(bf16)
    x = x_ref[...]
    a = mul(x, w_ref[0], NN)
    u = mul(x, w_ref[1], NN)
    dh = mul(q_ref[...], w_ref[2], NN)
    sig = jax.nn.sigmoid(a)
    silu = a * sig
    h = (silu * u).astype(bf16)
    da = (dh * u * (sig * (1.0 + a * (1.0 - sig)))).astype(bf16)
    du = (dh * silu).astype(bf16)
    h_ref[...] = h
    da_ref[...] = da
    du_ref[...] = du
    gate = jnp.sum(h.astype(f32) * dh, axis=1, keepdims=True)
    rows = mul(da, w_ref[0], NT) + mul(du, w_ref[1], NT)
    for r in range(CAP - 1):
        for c in range(chunks):
            stage[pl.ds(r * chunks + c, groups, stride=sub), :] = rows[
                r * groups : (r + 1) * groups, c * LANES : (c + 1) * LANES
            ]
    back_ref[...] = stage[...].reshape(back_ref.shape).astype(bf16)
    first = rest_ref.shape[1]
    left = rows[(CAP - 1) * groups :, :]
    rest_ref[...] = left[:, :first].astype(bf16)
    extra = [left[:, c : c + LANES] for c in range(first, chunks * LANES, LANES)]
    extra += [jnp.broadcast_to(gate[r * groups : (r + 1) * groups], (groups, LANES)) for r in range(CAP)]
    free = first // LANES
    for line in range(8):
        at = line - (8 - free)
        value = extra[at] if 0 <= at < len(extra) else jnp.zeros((groups, LANES), f32)
        stage[pl.ds(line, groups, stride=8), :] = value
    last_ref[...] = stage[: groups * 8, :].reshape(groups, 8, LANES).astype(bf16)


def rows_products(got, whole, free):
    groups, _, sub, _ = got.shape
    width, hidden = whole.shape[1:]
    rows, chunks = groups * CAP, sub // 2
    like = jax.ShapeDtypeStruct
    return call(
        rows_body,
        (
            like((rows, width), bf16),
            like((rows, width), bf16),
            like((rows, hidden), bf16),
            like((rows, hidden), bf16),
            like((rows, hidden), bf16),
            like((groups, CAP - 1, chunks, LANES), bf16),
            like((groups, free * LANES), bf16),
            like((groups, 8, LANES), bf16),
        ),
        [pltpu.VMEM((groups * sub, LANES), f32)],
        10 * rows * width * hidden,
        8 * 2**20,
    )(got, whole)


def grads_body(core_ref, x_ref, q_ref, da_ref, du_ref, h_ref, keep_ref, send_ref):
    halves, _, depth, _ = keep_ref.shape
    for out_ref, core in ((send_ref, 1 - core_ref[0]), (keep_ref, core_ref[0])):
        for half in range(halves):
            cols = pl.ds(pl.multiple_of((half * 2 + core) * depth, depth), depth)
            out_ref[half, 0] = mul(x_ref[:, cols], da_ref[...], TN).astype(bf16)
            out_ref[half, 1] = mul(x_ref[:, cols], du_ref[...], TN).astype(bf16)
            out_ref[half, 2] = mul(q_ref[:, cols], h_ref[...], TN).astype(bf16)


def weight_grads(core, x, q, da, du, h):
    rows, width = x.shape
    hidden = h.shape[1]
    vmem = pl.BlockSpec(memory_space=pltpu.VMEM)
    half = jax.ShapeDtypeStruct((2, 3, width // 4, hidden), bf16)
    return pl.pallas_call(
        grads_body,
        out_shape=(half, half),
        in_specs=[pl.BlockSpec(memory_space=pltpu.SMEM)] + [vmem] * 5,
        out_specs=(vmem, vmem),
        compiler_params=pltpu.CompilerParams(vmem_limit_bytes=48 * 2**20),
        cost_estimate=pl.CostEstimate(
            flops=6 * rows * width * hidden, bytes_accessed=6 * 2**20, transcendentals=0
        ),
    )(core, x, q, da, du, h)


def pair_body(side_ref, keep_ref, got_ref, own_ref, send_ref):
    side = side_ref[0]
    send_ref[...] = (keep_ref[1 - side].astype(f32) + got_ref[1 - side].astype(f32)).astype(bf16)
    own_ref[...] = keep_ref[side].astype(f32) + got_ref[side].astype(f32)


def pair_sum(side, keep, got):
    vmem = pl.BlockSpec(memory_space=pltpu.VMEM)
    return pl.pallas_call(
        pair_body,
        out_shape=(
            jax.ShapeDtypeStruct(keep.shape[1:], f32),
            jax.ShapeDtypeStruct(keep.shape[1:], bf16),
        ),
        in_specs=[pl.BlockSpec(memory_space=pltpu.SMEM), vmem, vmem],
        out_specs=(vmem, vmem),
        compiler_params=pltpu.CompilerParams(vmem_limit_bytes=48 * 2**20),
        cost_estimate=pl.CostEstimate(flops=keep.size, bytes_accessed=5 * keep.size, transcendentals=0),
    )(side, keep, got)


def adam_body(own_ref, other_ref, one_ref, two_ref, rest_ref, out_ref, stage):
    slots, tiles, sub, _ = out_ref.shape
    lines = tiles * sub
    parts, blocks = own_ref.shape[0] // slots, own_ref.shape[1] // LANES
    for p in range(parts):
        at = slice(p * slots, (p + 1) * slots)
        grad = own_ref[at, :] + other_ref[at, :].astype(f32)
        first_new = BETA_ONE * one_ref[at, :] + (1.0 - BETA_ONE) * grad
        second_new = BETA_TWO * two_ref[at, :] + (1.0 - BETA_TWO) * grad * grad
        first_hat = first_new * (1.0 / (1.0 - BETA_ONE**STEP))
        second_hat = second_new * (1.0 / (1.0 - BETA_TWO**STEP))
        update = first_hat / (jnp.sqrt(second_hat) + ADAM_EPS)
        for b in range(blocks):
            stage[pl.ds(p * blocks + b, slots, stride=lines), :] = update[:, b * LANES : (b + 1) * LANES]
    used = parts * blocks
    for c in range(lines - used):
        stage[pl.ds(used + c, slots, stride=lines), :] = rest_ref[:, c * LANES : (c + 1) * LANES].astype(f32)
    out_ref[...] = stage[...].reshape(out_ref.shape).astype(bf16)


def adam_update(own, other, moment_one, moment_two, rest, slots, lines):
    return call(
        adam_body,
        jax.ShapeDtypeStruct((slots, lines // 8, 8, LANES), bf16),
        [pltpu.VMEM((slots * lines, LANES), f32)],
        12 * own.size,
        14 * own.size,
    )(own, other, moment_one, moment_two, rest)


def swap_body(free, partner_ref, in_ref, last_ref, out_ref):
    slots, tiles, sub, _ = in_ref.shape
    update = lax.broadcasted_iota(jnp.int32, (sub, LANES), 0) < sub - free

    def step(d, carry):
        source = partner_ref[d]
        for t in range(tiles - 1):
            out_ref[d, t] = in_ref[source, t]
        moved = in_ref[source, tiles - 1].astype(f32)
        out_ref[d, tiles - 1] = jnp.where(update, moved, last_ref[d].astype(f32)).astype(bf16)
        return carry

    lax.fori_loop(0, slots, step, 0, unroll=8)


def swap_slots(partner, spread, last, free):
    vmem = pl.BlockSpec(memory_space=pltpu.VMEM)
    return pl.pallas_call(
        functools.partial(swap_body, free),
        out_shape=jax.ShapeDtypeStruct(spread.shape, spread.dtype),
        in_specs=[pl.BlockSpec(memory_space=pltpu.SMEM), vmem, vmem],
        out_specs=vmem,
        compiler_params=pltpu.CompilerParams(vmem_limit_bytes=48 * 2**20),
        cost_estimate=pl.CostEstimate(flops=0, bytes_accessed=4 * spread.size, transcendentals=0),
    )(partner, spread, last)


def finish_body(free, ids_ref, prob_ref, back_ref, spread_ref, routed_ref, tok_ref, gate_ref, out_ref, stage, rows):
    groups, ranks, chunks, _ = back_ref.shape
    slots, tiles, sub, _ = routed_ref.shape
    lines = tiles * sub
    parts, blocks = out_ref.shape[0] // slots, out_ref.shape[1] // LANES
    hots, picks = routing(ids_ref[...], groups)
    held = groups * ranks * chunks
    stage[:held, :] = back_ref[...].astype(f32).reshape(held, LANES)
    for r in range(ranks):
        for c in range(chunks):
            rows[r * groups : (r + 1) * groups, c * LANES : (c + 1) * LANES] = stage[
                pl.ds(r * chunks + c, groups, stride=ranks * chunks), :
            ].astype(bf16)
    at = slice(ranks * groups, (ranks + 1) * groups)
    stage[: groups * sub, :] = spread_ref[:, tiles - 1].astype(f32).reshape(groups * sub, LANES)
    for c in range(free):
        rows[at, c * LANES : (c + 1) * LANES] = stage[pl.ds(sub - free + c, groups, stride=sub), :].astype(bf16)
    stage[...] = routed_ref[...].astype(f32).reshape(slots * lines, LANES)
    for p in range(parts):
        for b in range(blocks):
            out_ref[p * slots : (p + 1) * slots, b * LANES : (b + 1) * LANES] = stage[
                pl.ds(p * blocks + b, slots, stride=lines), :
            ].astype(bf16)
    extra = [stage[pl.ds(lines - free + c, groups, stride=lines), :] for c in range(free)]
    for c in range(free, chunks):
        rows[at, c * LANES : (c + 1) * LANES] = extra[c - free].astype(bf16)
    tok_ref[...] = mul(jnp.concatenate(picks, axis=0).astype(bf16), rows[...], TN).astype(bf16)
    gate_at = sum(picks[r] * extra[chunks - free + r] for r in range(CAP))
    for k in range(2):
        total = jnp.sum(jnp.where(hots[k], gate_at, 0.0), axis=0, keepdims=True)
        gate_ref[k : k + 1, :] = total / prob_ref[k : k + 1, :].astype(f32)


def finish(ids_t, prob_t, back, spread, routed, shape, free):
    groups, _, chunks, _ = back.shape
    tok_count = ids_t.shape[1]
    width = chunks * LANES
    return call(
        functools.partial(finish_body, free),
        (
            jax.ShapeDtypeStruct((tok_count, width), bf16),
            jax.ShapeDtypeStruct((2, tok_count), f32),
            jax.ShapeDtypeStruct(shape, bf16),
        ),
        [
            pltpu.VMEM((routed.size // LANES, LANES), f32),
            pltpu.VMEM((groups * CAP, width), bf16),
        ],
        2 * CAP * groups * tok_count * width,
        4 * 2**20,
    )(ids_t, prob_t, back, spread, routed)


def on_device(
    tokens,
    cotangent,
    route_ids,
    gate_prob,
    swap_partner,
    expert_weights,
    first_moment,
    second_moment,
):
    groups = lax.axis_size("expert")
    hidden = expert_weights.shape[3]
    flat = (expert_weights.size // hidden, hidden)
    ids_t, prob_t = route_ids.T, gate_prob.T
    replica = lax.axis_index("dp")
    core, side = (replica % 2).reshape(1), (replica // 2).reshape(1)
    used = expert_weights.size // (groups * LANES)
    lines = -(-used // 8) * 8
    free = lines - used

    whole = lax.all_gather(expert_weights, "dp", axis=2, tiled=True)[0]
    got = exchange(dispatch(ids_t, prob_t, tokens, cotangent, groups))
    x, q, da, du, h, returned, rest, last = rows_products(got, whole, free)
    back = exchange(returned)
    keep, sent = weight_grads(core, x, q, da, du, h)
    own, sent = pair_sum(side, keep, lax.ppermute(sent, "dp", [(0, 1), (1, 0), (2, 3), (3, 2)]))
    other = lax.ppermute(sent, "dp", [(0, 2), (2, 0), (1, 3), (3, 1)])
    staged = adam_update(
        own.reshape(flat),
        other.reshape(flat),
        first_moment.reshape(flat),
        second_moment.reshape(flat),
        rest,
        groups,
        lines,
    )
    back, staged = lax.optimization_barrier((back, staged))
    spread = exchange(staged)
    routed = exchange(swap_slots(swap_partner, spread, last, free))
    token_grad, gate_grad, update = finish(ids_t, prob_t, back, spread, routed, flat, free)
    return (token_grad, gate_grad.T.astype(bf16), update.reshape(expert_weights.shape))


def solution(mesh):
    placed = (
        P(("expert", "dp"), None),
        P(("expert", "dp"), None),
        P(("expert", "dp"), None),
        P(("expert", "dp"), None),
        P(),
        P("expert", None, "dp", None),
        P("expert", None, "dp", None),
        P("expert", None, "dp", None),
    )
    return jax.shard_map(
        on_device,
        mesh=mesh,
        in_specs=placed,
        out_specs=(
            P(("expert", "dp"), None),
            P(("expert", "dp"), None),
            P("expert", None, "dp", None),
        ),
        check_vma=False,
    )
```

time: 297 us -> 284 us (0.956)
  waiting for transfers between devices: 160 us -> 97.4 us
  blocking collectives: 60.6 us -> 111 us
    all_to_all x1 -> x2, blocking collectives: 60.6 us -> 111 us  [exchange(): return lax.all_to_all(x, 'expert', split_axis=0, concat_axis=0, tiled=True)]
    all_to_all x3 -> x2, waiting for transfers between devices: 77.1 us -> 34.8 us  [exchange(): return lax.all_to_all(x, 'expert', split_axis=0, concat_axis=0, tiled=True)]
    reduce_scatter x1 -> x0, waiting for transfers between devices: 40.1 us -> none  [on_device(): gradient = lax.psum_scatter(partial, 'dp', scatter_dimension=1, tiled=True)]
    ppermute x0 -> x2, waiting for transfers between devices: none -> 20.1 us  [the longest x1 16.9 us: on_device(): other = lax.ppermute(sent, 'dp', [(0, 2), (2, 0), (1, 3), (3, 1)])]
    all_to_all x3 -> x2, starting transfers between devices: 36.2 us -> 28.6 us  [exchange(): return lax.all_to_all(x, 'expert', split_axis=0, concat_axis=0, tiled=True)]
    ppermute x0 -> x2, starting transfers between devices: none -> 5.4 us  [the longest x1 3.49 us: on_device(): other = lax.ppermute(sent, 'dp', [(0, 2), (2, 0), (1, 3), (3, 1)])]
    unnamed x24 -> x30, local copies, waits for them, and re-layouts: 6.26 us -> 8.09 us
  transfers between devices with their start and end apart: 5 -> 5, of which waited for: 4 -> 4; matrix products, arithmetic and copies ran while one was open for 0% -> 0% of each run, Pallas kernels for 1% -> 2%
where the time goes in v4:
time: 284 us; the launch traced here: 283 us
  blocking collectives  111 us (39%)
  waiting for transfers between devices  97.4 us (34%)
  starting transfers between devices  34 us (12%)
  Pallas kernels  17.5 us (6%)
  between operations  14.2 us (5%)
  local copies, waits for them, and re-layouts  8.09 us (3%)
    all_to_all x2, blocking collectives, exchange(): return lax.all_to_all(x, 'expert', split_axis=0, concat_axis=0, tiled=True)  111 us
    all_gather x1, waiting for transfers between devices, on_device(): whole = lax.all_gather(expert_weights, 'dp', axis=2, tiled=True)[0]  41.8 us
    all_to_all x2, waiting for transfers between devices, exchange(): return lax.all_to_all(x, 'expert', split_axis=0, concat_axis=0, tiled=True)  34.8 us
    all_to_all x2, starting transfers between devices, exchange(): return lax.all_to_all(x, 'expert', split_axis=0, concat_axis=0, tiled=True)  28.6 us
    ppermute x1, waiting for transfers between devices, on_device(): other = lax.ppermute(sent, 'dp', [(0, 2), (2, 0), (1, 3), (3, 1)])  16.9 us
    unnamed x30, local copies, waits for them, and re-layouts  8.09 us
    pallas_call x1, Pallas kernels, rows_products(): call(rows_body, (like((rows, width), bf16), like((rows, width), bf16), li...  6.17 us
  transfers between devices with their start and end apart: 5, of which 4 were waited for; matrix products, arithmetic and copies ran while one was open for 0% of the time, Pallas kernels for 2%

profile of v4, /device:TPU:6, one launch (start us, length us, event | category | flops | bytes accessed | tf_op | source)
XLA Modules:
  0.0 283.1 jit_solution(8259050183214533220)
XLA Ops:
  7.2 0.9 copy-done.2
  8.1 0.9 copy-done.3
  10.4 2.6 shard_map.103
  13.0 20.5 %all-to-all-start = ((bf16[128,3,16,128]{3,2,1,0:T(8,128)(2,1)}), bf16[128,3,16,128]{3,2,1,0:T(8,128)(2,1)S(1)}, u32[]{:S(2)}, u32[]{:S(2)}) async-start(bf16[128,3,16,128]{3,2,1,0:T(8,128)(2,1)} %shard_map.103), calls=%async_computation | async-start | bytes 3145728 | tf_op jit(solution)/shard_map/all_to_all | solution.py:38
  34.3 41.8 %all-gather.2.cloned.1.call-done = bf16[1,3,1024,384]{3,2,1,0:T(8,128)(2,1)} async-done(((bf16[1,3,256,384]{3,2,1,0:T(8,128)(2,1)}), bf16[1,3,1024,384]{3,2,1,0:T(8,128)(2,1)}) %all-gather.2.cloned.1.call-update) | async-done | bytes 2359312 | tf_op jit(solution)/shard_map/all_gather | solution.py:324
  76.2 34.8 %all-to-all-done.got_ref = bf16[128,3,16,128]{3,2,1,0:T(8,128)(2,1)S(1)} async-done(((bf16[128,3,16,128]{3,2,1,0:T(8,128)(2,1)}), bf16[128,3,16,128]{3,2,1,0:T(8,128)(2,1)S(1)}, u32[]{:S(2)}, u32[]{:S(2)}) %all-to-all-start) | async-done | bytes 1572896 | tf_op jit(solution)/shard_map/all_to_all | solution.py:38
  110.9 6.2 %shard_map.104 = (bf16[384,1024]{1,0:T(8,128)(2,1)S(1)}, bf16[384,1024]{1,0:T(8,128)(2,1)S(1)}, bf16[384,384]{1,0:T(8,128)(2,1)S(1)}, bf16[384,384]{1,0:T(8,128)...) custom-call(bf16[128,3,16,128]{3,2,1,0:T(8,128)(2,1)S(1)} %all-to-al, ...), custom_call_target="tpu_custom_call" | custom-call | flops 1509949440 | bytes 8388608 | tf_op jit(solution)/shard_map/pallas_call | solution.py:128
  117.1 0.9 copy-done.11
  118.0 0.7 copy-done.13
  118.7 8.1 %all-to-all-start.1 = ((bf16[128,2,8,128]{3,2,1,0:T(8,128)(2,1)}), bf16[128,2,8,128]{3,2,1,0:T(8,128)(2,1)S(1)}, u32[]{:S(2)}, u32[]{:S(2)}) async-start(bf16[128,2,8,128]{3,2,1,0:T(8,128)(2,1)} %get-tuple-element.20), calls=%async_computation.1 | async-start | bytes 1048576 | tf_op jit(solution)/shard_map/all_to_all | solution.py:38
  126.8 1.1 copy-done.10
  128.0 1.1 copy-done.12
  129.1 1.0 copy-done.14
  130.1 2.4 shard_map.105
  132.4 1.9 collective-permute-start
  134.3 3.1 %collective-permute-done.got_ref = bf16[2,3,256,384]{3,2,1,0:T(8,128)(2,1)} collective-permute-done((bf16[2,3,256,384]{3,2,1,0:T(8,128)(2,1)}, bf16[2,3,256,384]{3,2,1,0:T(8,128)(2,1)}, u32[]{:S(2)}, u32[]{:S(2)}) %collective-permute-start) | collective-permute-done | bytes 1179680 | tf_op jit(solution)/shard_map/ppermute | solution.py:329
  137.5 1.7 shard_map.106
  139.2 3.5 %collective-permute-start.1 = (bf16[3,256,384]{2,1,0:T(8,128)(2,1)S(1)}, bf16[3,256,384]{2,1,0:T(8,128)(2,1)S(1)}, u32[]{:S(2)}, u32[]{:S(2)}) collective-permute-start(bf16[3,256,384]{2,1,0:T(8,128)(2,1)S(1)} %get-tuple-element.29), channel_id=1, source_target_pairs={{0,2},{2,0},{1,3},{3,1},{4,6},{6,4},{5,7},{7,5},{8,10},{10,8},{9,1... | collective-permute-start | bytes 1769480 | tf_op jit(solution)/shard_map/ppermute | solution.py:330
  142.7 16.9 %collective-permute-done.1 = bf16[3,256,384]{2,1,0:T(8,128)(2,1)S(1)} collective-permute-done((bf16[3,256,384]{2,1,0:T(8,128)(2,1)S(1)}, bf16[3,256,384]{2,1,0:T(8,128)(2,1)S(1)}, u32[]{:S(2)}, u32[]{:S(2)}) %collective-permute-start.1) | collective-permute-done | bytes 589856 | tf_op jit(solution)/shard_map/ppermute | solution.py:330
  159.6 1.6 shard_map.107
  161.3 60.0 %all_to_all.20.in_ref.spread_ref = bf16[128,3,8,128]{3,2,1,0:T(8,128)(2,1)S(1)} all-to-all(bf16[128,3,8,128]{3,2,1,0:T(8,128)(2,1)S(1)} %shard_map.107), channel_id=1, replica_groups=mesh['expert'=128,'dp'=4] {'expert'}, dimensions={0} | all-to-all | bytes 1572864 | tf_op jit(solution)/shard_map/all_to_all | solution.py:38
  221.3 0.8 shard_map.108
  222.1 51.4 %all_to_all.21.routed_ref = bf16[128,3,8,128]{3,2,1,0:T(8,128)(2,1)S(1)} all-to-all(bf16[128,3,8,128]{3,2,1,0:T(8,128)(2,1)S(1)} %shard_map.108), channel_id=1, replica_groups=mesh['expert'=128,'dp'=4] {'expert'}, dimensions={0} | all-to-all | bytes 1572864 | tf_op jit(solution)/shard_map/all_to_all | solution.py:38
  273.5 2.2 shard_map.109
  (27 shorter events, 2.6 us)
Async XLA Ops:
  7.2 1.0 copy-start.2
  8.1 0.9 copy-start.3
  9.1 0.7 copy-start.4
  9.7 0.7 copy-start.6
  13.0 97.9 %all-to-all-start = ((bf16[128,3,16,128]{3,2,1,0:T(8,128)(2,1)}), bf16[128,3,16,128]{3,2,1,0:T(8,128)(2,1)S(1)}, u32[]{:S(2)}, u32[]{:S(2)}) async-start(bf16[128,3,16,128]{3,2,1,0:T(8,128)(2,1)} %shard_map.103), calls=%async_computation | async-start | bytes 3145728 | tf_op jit(solution)/shard_map/all_to_all | solution.py:38
  33.6 42.6 %all-gather.2.cloned.1.call-start = ((), (), s32[]{:S(2)}) async-start(), calls=%async_computation.4 | async-start | bytes 2949120 | tf_op jit(solution)/shard_map/all_gather | solution.py:324
  117.1 0.9 copy-start.11
  118.0 0.7 copy-start.13
  118.7 8.1 %copy-start.9 = (bf16[384,1024]{1,0:T(8,128)(2,1)}, bf16[384,1024]{1,0:T(8,128)(2,1)S(1)}, u32[]{:S(2)}) copy-start(bf16[384,1024]{1,0:T(8,128)(2,1)S(1)} %get-tuple-element.21.x_ref) | copy-start | bytes 2359300
  118.7 42.5 %all-to-all-start.1 = ((bf16[128,2,8,128]{3,2,1,0:T(8,128)(2,1)}), bf16[128,2,8,128]{3,2,1,0:T(8,128)(2,1)S(1)}, u32[]{:S(2)}, u32[]{:S(2)}) async-start(bf16[128,2,8,128]{3,2,1,0:T(8,128)(2,1)} %get-tuple-element.20), calls=%async_computation.1 | async-start | bytes 1048576 | tf_op jit(solution)/shard_map/all_to_all | solution.py:38
  126.8 1.1 copy-start.10
  128.0 1.1 copy-start.12
  129.1 1.0 copy-start.14
  132.4 5.1 %collective-permute-start = (bf16[2,3,256,384]{3,2,1,0:T(8,128)(2,1)}, bf16[2,3,256,384]{3,2,1,0:T(8,128)(2,1)}, u32[]{:S(2)}, u32[]{:S(2)}) collective-permute-start(bf16[2,3,256,384]{3,2,1,0:T(8,128)(2,1)} %get-tuple-element.27), channel_id=1, source_target_pairs={{0,1},{1,0},{2,3},{3,2},{4,5},{5,4},{6,7},{7,6},{8,9},{9,8},{10,11... | collective-permute-start | bytes 3538952 | tf_op jit(solution)/shard_map/ppermute | solution.py:329
  137.5 22.1 %copy-start = (f32[1,3,256,384]{3,2,1,0:T(8,128)S(1)}, f32[1,3,256,384]{3,2,1,0:T(8,128)}, u32[]{:S(2)}) copy-start(f32[1,3,256,384]{3,2,1,0:T(8,128)} %param.14) | copy-start | bytes 3538948
  137.5 22.1 %copy-start.1 = (f32[1,3,256,384]{3,2,1,0:T(8,128)S(1)}, f32[1,3,256,384]{3,2,1,0:T(8,128)}, u32[]{:S(2)}) copy-start(f32[1,3,256,384]{3,2,1,0:T(8,128)} %param.15) | copy-start | bytes 3538948
  139.2 20.4 %collective-permute-start.1 = (bf16[3,256,384]{2,1,0:T(8,128)(2,1)S(1)}, bf16[3,256,384]{2,1,0:T(8,128)(2,1)S(1)}, u32[]{:S(2)}, u32[]{:S(2)}) collective-permute-start(bf16[3,256,384]{2,1,0:T(8,128)(2,1)S(1)} %get-tuple-element.29), channel_id=1, source_target_pairs={{0,2},{2,0},{1,3},{3,1},{4,6},{6,4},{5,7},{7,5},{8,10},{10,8},{9,1... | collective-permute-start | bytes 1769480 | tf_op jit(solution)/shard_map/ppermute | solution.py:330
  161.2 60.1 %copy-start.8 = (s32[128]{0:T(128)S(1)}, s32[128]{0:T(128)}, u32[]{:S(2)}) copy-start(s32[128]{0:T(128)} %partner_ref.1) | copy-start | bytes 1540
  222.1 51.4 %copy-start.5 = (s32[128,2]{0,1:T(2,128)S(1)}, s32[128,2]{0,1:T(2,128)}, u32[]{:S(2)}) copy-start(s32[128,2]{0,1:T(2,128)} %param.10) | copy-start | bytes 3076
  222.1 51.4 %copy-start.7 = (bf16[128,2]{0,1:T(2,128)(2,1)S(1)}, bf16[128,2]{0,1:T(2,128)(2,1)}, u32[]{:S(2)}) copy-start(bf16[128,2]{0,1:T(2,128)(2,1)} %param.11) | copy-start | bytes 1540
Sparse Core Ops, SparseCore 0:
  36.5 39.5 all-gather.1

commit v5 on v3

v5 whole, which is shorter than its diff:
```python
import jax
import jax.numpy as jnp
from jax import lax
from jax.experimental import pallas as pl
from jax.experimental.pallas import tpu as pltpu
from jax.sharding import PartitionSpec as P

STEP = 100
BETA_ONE = 0.9
BETA_TWO = 0.95
ADAM_EPS = 1e-08
CAP = 3
LANES = 128
SLOTS = 128
f32, bf16 = jnp.float32, jnp.bfloat16

NN = (((1,), (0,)), ((), ()))
NT = (((1,), (1,)), ((), ()))
TN = (((0,), (0,)), ((), ()))


def mul(a, b, dims):
    return lax.dot_general(a, b, dims, preferred_element_type=f32)


def call(body, outs, scratch, flops, moved, ins=None, limit=16):
    return pl.pallas_call(
        body,
        out_shape=outs,
        **({} if ins is None else {'in_specs': ins}),
        scratch_shapes=scratch,
        compiler_params=pltpu.CompilerParams(vmem_limit_bytes=limit * 2**20),
        cost_estimate=pl.CostEstimate(flops=flops, bytes_accessed=moved, transcendentals=0),
    )


def exchange(x):
    return lax.all_to_all(x, "expert", split_axis=0, concat_axis=0, tiled=True)


def routing(ids, groups):
    tok_count = ids.shape[1]
    expert = lax.broadcasted_iota(jnp.int32, (groups, tok_count), 0)
    hots = [ids[k : k + 1, :] == expert for k in range(2)]
    named = jnp.where(hots[0] | hots[1], 1.0, 0.0)
    before = lax.broadcasted_iota(jnp.int32, (tok_count, tok_count), 0)
    after = lax.broadcasted_iota(jnp.int32, (tok_count, tok_count), 1)
    earlier = jnp.where(before < after, 1.0, 0.0).astype(bf16)
    rank = mul(named.astype(bf16), earlier, NN)
    return hots, [jnp.where(rank == r, named, 0.0) for r in range(CAP)]


def dispatch_body(ids_hbm, prob_hbm, tok_hbm, cot_hbm, out_ref, ids_ref, prob_ref, tok_ref, cot_ref, stage, sems):
    pairs = ((ids_hbm, ids_ref), (prob_hbm, prob_ref), (tok_hbm, tok_ref), (cot_hbm, cot_ref))
    copies = [pltpu.make_async_copy(src, dst, sems.at[i]) for i, (src, dst) in enumerate(pairs)]
    for copy in copies:
        copy.start()
    groups, _, sub, _ = out_ref.shape
    chunks = sub // 2
    copies[0].wait()
    hots, picks = routing(ids_ref[...], groups)
    copies[1].wait()
    prob = prob_ref[...].astype(f32)
    prob_at = jnp.where(hots[0], prob[0:1, :], jnp.where(hots[1], prob[1:2, :], 0.0))
    copies[2].wait()
    copies[3].wait()
    for r in range(CAP):
        x = mul(picks[r].astype(bf16), tok_ref[...], NN)
        q = mul((picks[r] * prob_at).astype(bf16), cot_ref[...], NN)
        for c in range(chunks):
            cols = slice(c * LANES, (c + 1) * LANES)
            stage[pl.ds(c, groups, stride=sub), :] = x[:, cols]
            stage[pl.ds(chunks + c, groups, stride=sub), :] = q[:, cols]
        out_ref[:, r] = stage[...].reshape(groups, sub, LANES).astype(bf16)


def dispatch(ids_t, prob_t, tokens, cotangent, groups):
    sub = 2 * tokens.shape[1] // LANES
    return call(
        dispatch_body,
        jax.ShapeDtypeStruct((groups, CAP, sub, LANES), bf16),
        [pltpu.VMEM(a.shape, a.dtype) for a in (ids_t, prob_t, tokens, cotangent)]
        + [pltpu.VMEM((groups * sub, LANES), f32), pltpu.SemaphoreType.DMA((4,))],
        2 * 2 * CAP * groups * tokens.size,
        4 * 2**20,
        [pl.BlockSpec(memory_space=pltpu.HBM)] * 4,
    )(ids_t, prob_t, tokens, cotangent)


def expert_body(core_ref, got_ref, w_ref, back_ref, keep_ref, send_ref, x_ref, q_ref, da_ref, du_ref, h_ref, stage, stage_back):
    groups, _, sub, _ = got_ref.shape
    chunks = sub // 2
    for r in range(CAP):
        stage[...] = got_ref[:, r].astype(f32).reshape(groups * sub, LANES)
        at = slice(r * groups, (r + 1) * groups)
        for c in range(chunks):
            cols = slice(c * LANES, (c + 1) * LANES)
            x_ref[at, cols] = stage[pl.ds(c, groups, stride=sub), :].astype(bf16)
            q_ref[at, cols] = stage[pl.ds(chunks + c, groups, stride=sub), :].astype(bf16)
    x = x_ref[...]
    a = mul(x, w_ref[0], NN)
    u = mul(x, w_ref[1], NN)
    dh = mul(q_ref[...], w_ref[2], NN)
    sig = jax.nn.sigmoid(a)
    silu = a * sig
    h = (silu * u).astype(bf16)
    da = (dh * u * (sig * (1.0 + a * (1.0 - sig)))).astype(bf16)
    du = (dh * silu).astype(bf16)
    h_ref[...] = h
    da_ref[...] = da
    du_ref[...] = du
    gate = jnp.sum(h.astype(f32) * dh, axis=1, keepdims=True)
    rows = mul(da, w_ref[0], NT) + mul(du, w_ref[1], NT)
    lines = stage_back.shape[0] // groups
    for r in range(CAP):
        at = slice(r * groups, (r + 1) * groups)
        for c in range(chunks):
            stage_back[pl.ds(r * chunks + c, groups, stride=lines), :] = rows[at, c * LANES : (c + 1) * LANES]
        stage_back[pl.ds(CAP * chunks + r, groups, stride=lines), :] = jnp.broadcast_to(gate[at], (groups, LANES))
    for spare in range(CAP * (chunks + 1), lines):
        stage_back[pl.ds(spare, groups, stride=lines), :] = jnp.zeros((groups, LANES), f32)
    back_ref[...] = stage_back[...].reshape(back_ref.shape).astype(bf16)
    halves, _, depth, _ = keep_ref.shape
    for out_ref, core in ((send_ref, 1 - core_ref[0]), (keep_ref, core_ref[0])):
        for half in range(halves):
            cols = pl.ds(pl.multiple_of((half * 2 + core) * depth, depth), depth)
            out_ref[half, 0] = mul(x_ref[:, cols], da_ref[...], TN).astype(bf16)
            out_ref[half, 1] = mul(x_ref[:, cols], du_ref[...], TN).astype(bf16)
            out_ref[half, 2] = mul(q_ref[:, cols], h_ref[...], TN).astype(bf16)


def expert_step(core, got, whole):
    groups, _, sub, _ = got.shape
    width, hidden = whole.shape[1:]
    rows, chunks = groups * CAP, sub // 2
    lines = -(-CAP * (chunks + 1) // 2) * 2
    like = jax.ShapeDtypeStruct
    half = like((2, 3, width // 4, hidden), bf16)
    vmem = pl.BlockSpec(memory_space=pltpu.VMEM)
    return call(
        expert_body,
        (like((groups * lines // 8, 8, LANES), bf16), half, half),
        [pltpu.VMEM((rows, width), bf16)] * 2
        + [pltpu.VMEM((rows, hidden), bf16)] * 3
        + [pltpu.VMEM((groups * sub, LANES), f32), pltpu.VMEM((groups * lines, LANES), f32)],
        16 * rows * width * hidden,
        12 * 2**20,
        [pl.BlockSpec(memory_space=pltpu.SMEM), vmem, vmem],
        30,
    )(core, got, whole)


def pair_body(side_ref, keep_ref, got_ref, own_ref, send_ref):
    side = side_ref[0]
    send_ref[...] = (keep_ref[1 - side].astype(f32) + got_ref[1 - side].astype(f32)).astype(bf16)
    own_ref[...] = keep_ref[side].astype(f32) + got_ref[side].astype(f32)


def pair_sum(side, keep, got):
    vmem = pl.BlockSpec(memory_space=pltpu.VMEM)
    return pl.pallas_call(
        pair_body,
        out_shape=(
            jax.ShapeDtypeStruct(keep.shape[1:], f32),
            jax.ShapeDtypeStruct(keep.shape[1:], bf16),
        ),
        in_specs=[pl.BlockSpec(memory_space=pltpu.SMEM), vmem, vmem],
        out_specs=(vmem, vmem),
        compiler_params=pltpu.CompilerParams(vmem_limit_bytes=16 * 2**20),
        cost_estimate=pl.CostEstimate(flops=keep.size, bytes_accessed=5 * keep.size, transcendentals=0),
    )(side, keep, got)


def adam_body(own_ref, other_ref, one_ref, two_ref, out_ref, stage):
    blocks = own_ref.shape[1] // LANES
    lines = own_ref.shape[0] * blocks // SLOTS
    for p in range(lines // blocks):
        at = slice(p * SLOTS, (p + 1) * SLOTS)
        grad = own_ref[at, :] + other_ref[at, :].astype(f32)
        first_new = BETA_ONE * one_ref[at, :] + (1.0 - BETA_ONE) * grad
        second_new = BETA_TWO * two_ref[at, :] + (1.0 - BETA_TWO) * grad * grad
        first_hat = first_new * (1.0 / (1.0 - BETA_ONE**STEP))
        second_hat = second_new * (1.0 / (1.0 - BETA_TWO**STEP))
        update = first_hat / (jnp.sqrt(second_hat) + ADAM_EPS)
        for b in range(blocks):
            stage[pl.ds(p * blocks + b, SLOTS, stride=lines), :] = update[:, b * LANES : (b + 1) * LANES]
    out_ref[...] = stage[...].reshape(out_ref.shape).astype(bf16)


def adam_update(own, other, moment_one, moment_two):
    return call(
        adam_body,
        jax.ShapeDtypeStruct((own.size // (8 * LANES), 8, LANES), bf16),
        [pltpu.VMEM((own.size // LANES, LANES), f32)],
        12 * own.size,
        14 * own.size,
    )(own, other, moment_one, moment_two)


def swap_body(partner_ref, in_ref, out_ref):
    def step(d, carry):
        out_ref[d] = in_ref[partner_ref[d]]
        return carry

    lax.fori_loop(0, in_ref.shape[0], step, 0, unroll=8)


def swap_slots(partner, spread):
    vmem = pl.BlockSpec(memory_space=pltpu.VMEM)
    return call(
        swap_body,
        jax.ShapeDtypeStruct(spread.shape, spread.dtype),
        [],
        0,
        4 * spread.size,
        [pl.BlockSpec(memory_space=pltpu.SMEM), vmem],
    )(partner, spread)


def collect_body(in_ref, out_ref, stage):
    stage[...] = in_ref[...].astype(f32).reshape(stage.shape)
    blocks = out_ref.shape[1] // LANES
    lines = stage.shape[0] // SLOTS
    for p in range(lines // blocks):
        for b in range(blocks):
            out_ref[p * SLOTS : (p + 1) * SLOTS, b * LANES : (b + 1) * LANES] = stage[
                pl.ds(p * blocks + b, SLOTS, stride=lines), :
            ].astype(bf16)


def collect(routed, shape):
    return call(
        collect_body,
        jax.ShapeDtypeStruct(shape, bf16),
        [pltpu.VMEM((routed.size // LANES, LANES), f32)],
        0,
        4 * routed.size,
    )(routed)


def combine_body(ids_ref, prob_ref, back_ref, tok_ref, gate_ref, stage, rows):
    groups, chunks = rows.shape[0] // CAP, rows.shape[1] // LANES
    lines = stage.shape[0] // groups
    hots, picks = routing(ids_ref[...], groups)
    stage[...] = back_ref[...].astype(f32).reshape(stage.shape)
    for r in range(CAP):
        for c in range(chunks):
            rows[r * groups : (r + 1) * groups, c * LANES : (c + 1) * LANES] = stage[
                pl.ds(r * chunks + c, groups, stride=lines), :
            ].astype(bf16)
    tok_ref[...] = mul(jnp.concatenate(picks, axis=0).astype(bf16), rows[...], TN).astype(bf16)
    gate_at = sum(picks[r] * stage[pl.ds(CAP * chunks + r, groups, stride=lines), :] for r in range(CAP))
    for k in range(2):
        total = jnp.sum(jnp.where(hots[k], gate_at, 0.0), axis=0, keepdims=True)
        gate_ref[k : k + 1, :] = total / prob_ref[k : k + 1, :].astype(f32)


def combine(ids_t, prob_t, back, width, groups):
    tok_count = ids_t.shape[1]
    return call(
        combine_body,
        (
            jax.ShapeDtypeStruct((tok_count, width), bf16),
            jax.ShapeDtypeStruct((2, tok_count), f32),
        ),
        [
            pltpu.VMEM((back.size // LANES, LANES), f32),
            pltpu.VMEM((groups * CAP, width), bf16),
        ],
        2 * CAP * groups * tok_count * width,
        4 * 2**20,
    )(ids_t, prob_t, back)


def on_device(
    tokens,
    cotangent,
    route_ids,
    gate_prob,
    swap_partner,
    expert_weights,
    first_moment,
    second_moment,
):
    groups = lax.axis_size("expert")
    hidden = expert_weights.shape[3]
    flat = (expert_weights.size // hidden, hidden)
    ids_t, prob_t = route_ids.T, gate_prob.T
    replica = lax.axis_index("dp")
    core, side = (replica % 2).reshape(1), (replica // 2).reshape(1)
    tiles, pairs = (-1, 8, LANES), (groups, -1, 2, LANES)

    whole = lax.all_gather(expert_weights, "dp", axis=2, tiled=True)[0]
    got = exchange(dispatch(ids_t, prob_t, tokens, cotangent, groups))
    returned, keep, sent = expert_step(core, got, whole)
    own, sent = pair_sum(side, keep, lax.ppermute(sent, "dp", [(0, 1), (1, 0), (2, 3), (3, 2)]))
    back = exchange(returned.reshape(pairs))
    other = lax.ppermute(sent, "dp", [(0, 2), (2, 0), (1, 3), (3, 1)])
    staged = adam_update(
        own.reshape(flat), other.reshape(flat), first_moment.reshape(flat), second_moment.reshape(flat)
    )
    back, staged = lax.optimization_barrier((back, staged))
    spread = exchange(staged.reshape(pairs))
    routed = exchange(swap_slots(swap_partner, spread))
    token_grad, gate_grad = combine(ids_t, prob_t, back.reshape(tiles), tokens.shape[1], groups)
    update = collect(routed.reshape(tiles), flat)
    return (token_grad, gate_grad.T.astype(bf16), update.reshape(expert_weights.shape))


def solution(mesh):
    placed = (
        P(("expert", "dp"), None),
        P(("expert", "dp"), None),
        P(("expert", "dp"), None),
        P(("expert", "dp"), None),
        P(),
        P("expert", None, "dp", None),
        P("expert", None, "dp", None),
        P("expert", None, "dp", None),
    )
    return jax.shard_map(
        on_device,
        mesh=mesh,
        in_specs=placed,
        out_specs=(
            P(("expert", "dp"), None),
            P(("expert", "dp"), None),
            P("expert", None, "dp", None),
        ),
        check_vma=False,
    )
```

time: 297 us -> 273 us (0.919)
  blocking collectives: 60.6 us -> 43.5 us
  waiting for transfers between devices: 160 us -> 152 us
  starting transfers between devices: 36.3 us -> 40.6 us
  Pallas kernels: 17.7 us -> 14.7 us
    reduce_scatter x1 -> x0, waiting for transfers between devices: 40.1 us -> none  [on_device(): gradient = lax.psum_scatter(partial, 'dp', scatter_dimension=1, tiled=True)]
    ppermute x0 -> x2, waiting for transfers between devices: none -> 22.6 us  [the longest x1 19.5 us: on_device(): other = lax.ppermute(sent, 'dp', [(0, 2), (2, 0), (1, 3), (3, 1)])]
    all_to_all x1, blocking collectives: 60.6 us -> 43.5 us  [exchange(): return lax.all_to_all(x, 'expert', split_axis=0, concat_axis=0, tiled=True)]
    all_to_all x3, waiting for transfers between devices: 77.1 us -> 87 us  [exchange(): return lax.all_to_all(x, 'expert', split_axis=0, concat_axis=0, tiled=True)]
    ppermute x0 -> x2, starting transfers between devices: none -> 5.41 us  [the longest x1 3.49 us: on_device(): other = lax.ppermute(sent, 'dp', [(0, 2), (2, 0), (1, 3), (3, 1)])]
  transfers between devices with their start and end apart: 5 -> 6, of which waited for: 4 -> 6; matrix products, arithmetic and copies ran while one was open for 0% -> 0% of each run, Pallas kernels for 1% -> 2%
where the time goes in v5:
time: 273 us
  waiting for transfers between devices  152 us (56%)
  blocking collectives  43.5 us (16%)
  starting transfers between devices  40.6 us (15%)
  Pallas kernels  14.7 us (5%)
  between operations  14.2 us (5%)
  local copies, waits for them, and re-layouts  6.88 us (3%)
    all_to_all x3, waiting for transfers between devices, exchange(): return lax.all_to_all(x, 'expert', split_axis=0, concat_axis=0, tiled=True)  87 us
    all_to_all x1, blocking collectives, exchange(): return lax.all_to_all(x, 'expert', split_axis=0, concat_axis=0, tiled=True)  43.5 us
    all_gather x1, waiting for transfers between devices, on_device(): whole = lax.all_gather(expert_weights, 'dp', axis=2, tiled=True)[0]  41.8 us
    all_to_all x3, starting transfers between devices, exchange(): return lax.all_to_all(x, 'expert', split_axis=0, concat_axis=0, tiled=True)  35.2 us
    ppermute x1, waiting for transfers between devices, on_device(): other = lax.ppermute(sent, 'dp', [(0, 2), (2, 0), (1, 3), (3, 1)])  19.5 us
    unnamed x24, local copies, waits for them, and re-layouts  6.88 us
  transfers between devices with their start and end apart: 6, of which 6 were waited for; matrix products, arithmetic and copies ran while one was open for 0% of the time, Pallas kernels for 2%

profile of v5, /device:TPU:6, one launch (start us, length us, event | category | flops | bytes accessed | tf_op | source)
XLA Modules:
  0.0 272.5 jit_solution(14842055436389911478)
XLA Ops:
  7.2 0.9 copy-done.3
  8.1 0.9 copy-done.4
  10.4 2.7 shard_map.103
  13.1 20.5 %all-to-all-start = ((bf16[128,3,16,128]{3,2,1,0:T(8,128)(2,1)}), bf16[128,3,16,128]{3,2,1,0:T(8,128)(2,1)S(1)}, u32[]{:S(2)}, u32[]{:S(2)}) async-start(bf16[128,3,16,128]{3,2,1,0:T(8,128)(2,1)} %shard_map.103), calls=%async_computation | async-start | bytes 3145728 | tf_op jit(solution)/shard_map/all_to_all | solution.py:38
  34.4 41.8 %all-gather.2.cloned.1.call-done = bf16[1,3,1024,384]{3,2,1,0:T(8,128)(2,1)} async-done(((bf16[1,3,256,384]{3,2,1,0:T(8,128)(2,1)}), bf16[1,3,1024,384]{3,2,1,0:T(8,128)(2,1)}) %all-gather.2.cloned.1.call-update) | async-done | bytes 2359312 | tf_op jit(solution)/shard_map/all_gather | solution.py:293
  76.2 34.8 %all-to-all-done.got_ref = bf16[128,3,16,128]{3,2,1,0:T(8,128)(2,1)S(1)} async-done(((bf16[128,3,16,128]{3,2,1,0:T(8,128)(2,1)}), bf16[128,3,16,128]{3,2,1,0:T(8,128)(2,1)S(1)}, u32[]{:S(2)}, u32[]{:S(2)}) %all-to-all-start) | async-done | bytes 1572896 | tf_op jit(solution)/shard_map/all_to_all | solution.py:38
  111.0 1.7 copy-done.10
  112.7 5.2 %shard_map.104 = (bf16[448,8,128]{2,1,0:T(8,128)(2,1)S(1)}, bf16[2,3,256,384]{3,2,1,0:T(8,128)(2,1)S(1)}, bf16[2,3,256,384]{3,2,1,0:T(8,128)(2,1)S(1)}) custom-call(s32[1]{0:T(128)} %bitcast.2.core_ref, bf16[128,3,16,128]{3,2,1,0:T(8,128)(2,1)S(1)} %all-to-all-done.got_ref, bf16[3,1024,384]{2,1,0:T(8,128)(2,1)S(1)} %bitcast.28), custom_call_target="tpu_custom_call" | custom-call | flops 2415919104 | bytes 12582912 | tf_op jit(solution)/shard_map/pallas_call | solution.py:140
  117.8 0.9 copy-done.2
  118.8 1.0 copy-done.11
  119.8 8.1 %all-to-all-start.1 = ((bf16[128,14,2,128]{3,2,1,0:T(2,128)(2,1)}), bf16[128,14,2,128]{3,2,1,0:T(2,128)(2,1)S(1)}, u32[]{:S(2)}, u32[]{:S(2)}) async-start(bf16[128,14,2,128]{3,2,1,0:T(2,128)(2,1)} %bitcast.22), calls=%async_computation.1 | async-start | bytes 1835008 | tf_op jit(solution)/shard_map/all_to_all | solution.py:38
  127.9 1.9 collective-permute-start
  129.8 3.1 %collective-permute-done.got_ref = bf16[2,3,256,384]{3,2,1,0:T(8,128)(2,1)} collective-permute-done((bf16[2,3,256,384]{3,2,1,0:T(8,128)(2,1)}, bf16[2,3,256,384]{3,2,1,0:T(8,128)(2,1)}, u32[]{:S(2)}, u32[]{:S(2)}) %collective-permute-start) | collective-permute-done | bytes 1179680 | tf_op jit(solution)/shard_map/ppermute | solution.py:296
  133.0 1.7 shard_map.105
  134.6 3.5 %collective-permute-start.1 = (bf16[3,256,384]{2,1,0:T(8,128)(2,1)S(1)}, bf16[3,256,384]{2,1,0:T(8,128)(2,1)S(1)}, u32[]{:S(2)}, u32[]{:S(2)}) collective-permute-start(bf16[3,256,384]{2,1,0:T(8,128)(2,1)S(1)} %get-tuple-element.16), channel_id=1, source_target_pairs={{0,2},{2,0},{1,3},{3,1},{4,6},{6,4},{5,7},{7,5},{8,10},{10,8},{9,1... | collective-permute-start | bytes 1769480 | tf_op jit(solution)/shard_map/ppermute | solution.py:298
  138.1 19.5 %collective-permute-done.1 = bf16[3,256,384]{2,1,0:T(8,128)(2,1)S(1)} collective-permute-done((bf16[3,256,384]{2,1,0:T(8,128)(2,1)S(1)}, bf16[3,256,384]{2,1,0:T(8,128)(2,1)S(1)}, u32[]{:S(2)}, u32[]{:S(2)}) %collective-permute-start.1) | collective-permute-done | bytes 589856 | tf_op jit(solution)/shard_map/ppermute | solution.py:298
  157.6 1.4 shard_map.106
  159.0 17.8 %all-to-all-done.1 = bf16[128,14,2,128]{3,2,1,0:T(2,128)(2,1)S(1)} async-done(((bf16[128,14,2,128]{3,2,1,0:T(2,128)(2,1)}), bf16[128,14,2,128]{3,2,1,0:T(2,128)(2,1)S(1)}, u32[]{:S(2)}, u32[]{:S(2)}) %all-to-all-start.1) | async-done | bytes 917536 | tf_op jit(solution)/shard_map/all_to_all | solution.py:38
  176.8 43.5 %all_to_all.20.in_ref = bf16[128,9,2,128]{3,2,1,0:T(2,128)(2,1)S(1)} all-to-all(bf16[128,9,2,128]{3,2,1,0:T(2,128)(2,1)S(1)} %bitcast.17), channel_id=1, replica_groups=mesh['expert'=128,'dp'=4] {'expert'}, dimensions={0} | all-to-all | bytes 1179648 | tf_op jit(solution)/shard_map/all_to_all | solution.py:38
  220.3 1.6 shard_map.108
  221.9 6.6 %all-to-all-start.3 = ((bf16[128,9,2,128]{3,2,1,0:T(2,128)(2,1)}), bf16[128,9,2,128]{3,2,1,0:T(2,128)(2,1)S(1)}, u32[]{:S(2)}, u32[]{:S(2)}) async-start(bf16[128,9,2,128]{3,2,1,0:T(2,128)(2,1)} %shard_map.108), calls=%async_computation.3 | async-start | bytes 1179648 | tf_op jit(solution)/shard_map/all_to_all | solution.py:38
  228.5 1.3 shard_map.107
  230.3 34.4 %all-to-all-done.3 = bf16[128,9,2,128]{3,2,1,0:T(2,128)(2,1)S(1)} async-done(((bf16[128,9,2,128]{3,2,1,0:T(2,128)(2,1)}), bf16[128,9,2,128]{3,2,1,0:T(2,128)(2,1)S(1)}, u32[]{:S(2)}, u32[]{:S(2)}) %all-to-all-start.3) | async-done | bytes 589856 | tf_op jit(solution)/shard_map/all_to_all | solution.py:38
  264.7 1.0 shard_map.109
  (22 shorter events, 2.6 us)
Async XLA Ops:
  7.2 1.0 copy-start.3
  8.1 0.9 copy-start.4
  9.1 0.7 copy-start.5
  9.7 0.7 copy-start.7
  13.1 97.9 %all-to-all-start = ((bf16[128,3,16,128]{3,2,1,0:T(8,128)(2,1)}), bf16[128,3,16,128]{3,2,1,0:T(8,128)(2,1)S(1)}, u32[]{:S(2)}, u32[]{:S(2)}) async-start(bf16[128,3,16,128]{3,2,1,0:T(8,128)(2,1)} %shard_map.103), calls=%async_computation | async-start | bytes 3145728 | tf_op jit(solution)/shard_map/all_to_all | solution.py:38
  33.6 42.6 %all-gather.2.cloned.1.call-start = ((), (), s32[]{:S(2)}) async-start(), calls=%async_computation.4 | async-start | bytes 2949120 | tf_op jit(solution)/shard_map/all_gather | solution.py:293
  111.0 1.7 copy-start.10
  117.8 0.9 copy-start.2
  118.8 1.0 copy-start.11
  119.8 57.0 %all-to-all-start.1 = ((bf16[128,14,2,128]{3,2,1,0:T(2,128)(2,1)}), bf16[128,14,2,128]{3,2,1,0:T(2,128)(2,1)S(1)}, u32[]{:S(2)}, u32[]{:S(2)}) async-start(bf16[128,14,2,128]{3,2,1,0:T(2,128)(2,1)} %bitcast.22), calls=%async_computation.1 | async-start | bytes 1835008 | tf_op jit(solution)/shard_map/all_to_all | solution.py:38
  127.9 5.1 %collective-permute-start = (bf16[2,3,256,384]{3,2,1,0:T(8,128)(2,1)}, bf16[2,3,256,384]{3,2,1,0:T(8,128)(2,1)}, u32[]{:S(2)}, u32[]{:S(2)}) collective-permute-start(bf16[2,3,256,384]{3,2,1,0:T(8,128)(2,1)} %copy-done.11), channel_id=1, source_target_pairs={{0,1},{1,0},{2,3},{3,2},{4,5},{5,4},{6,7},{7,6},{8,9},{9,8},{10,11... | collective-permute-start | bytes 3538952 | tf_op jit(solution)/shard_map/ppermute | solution.py:296
  133.0 24.7 %copy-start = (f32[1,3,256,384]{3,2,1,0:T(8,128)S(1)}, f32[1,3,256,384]{3,2,1,0:T(8,128)}, u32[]{:S(2)}) copy-start(f32[1,3,256,384]{3,2,1,0:T(8,128)} %param.14) | copy-start | bytes 3538948
  133.0 24.7 %copy-start.1 = (f32[1,3,256,384]{3,2,1,0:T(8,128)S(1)}, f32[1,3,256,384]{3,2,1,0:T(8,128)}, u32[]{:S(2)}) copy-start(f32[1,3,256,384]{3,2,1,0:T(8,128)} %param.15) | copy-start | bytes 3538948
  134.6 23.0 %collective-permute-start.1 = (bf16[3,256,384]{2,1,0:T(8,128)(2,1)S(1)}, bf16[3,256,384]{2,1,0:T(8,128)(2,1)S(1)}, u32[]{:S(2)}, u32[]{:S(2)}) collective-permute-start(bf16[3,256,384]{2,1,0:T(8,128)(2,1)S(1)} %get-tuple-element.16), channel_id=1, source_target_pairs={{0,2},{2,0},{1,3},{3,1},{4,6},{6,4},{5,7},{7,5},{8,10},{10,8},{9,1... | collective-permute-start | bytes 1769480 | tf_op jit(solution)/shard_map/ppermute | solution.py:298
  159.0 61.3 %copy-start.9 = (s32[128]{0:T(128)S(1)}, s32[128]{0:T(128)}, u32[]{:S(2)}) copy-start(s32[128]{0:T(128)} %partner_ref.1) | copy-start | bytes 1540
  220.3 8.2 %copy-start.6 = (s32[128,2]{0,1:T(2,128)S(1)}, s32[128,2]{0,1:T(2,128)}, u32[]{:S(2)}) copy-start(s32[128,2]{0,1:T(2,128)} %param.10) | copy-start | bytes 3076
  220.3 8.2 %copy-start.8 = (bf16[128,2]{0,1:T(2,128)(2,1)S(1)}, bf16[128,2]{0,1:T(2,128)(2,1)}, u32[]{:S(2)}) copy-start(bf16[128,2]{0,1:T(2,128)(2,1)} %param.11) | copy-start | bytes 1540
  221.9 42.8 %all-to-all-start.3 = ((bf16[128,9,2,128]{3,2,1,0:T(2,128)(2,1)}), bf16[128,9,2,128]{3,2,1,0:T(2,128)(2,1)S(1)}, u32[]{:S(2)}, u32[]{:S(2)}) async-start(bf16[128,9,2,128]{3,2,1,0:T(2,128)(2,1)} %shard_map.108), calls=%async_computation.3 | async-start | bytes 1179648 | tf_op jit(solution)/shard_map/all_to_all | solution.py:38
Sparse Core Ops, SparseCore 0:
  36.6 39.5 all-gather.1

commit v6 on v5

--- a/solution.py
+++ b/solution.py
@@ -12,6 +12,8 @@
 CAP = 3
 LANES = 128
 SLOTS = 128
+BESIDE = [(0, 1), (1, 0), (2, 3), (3, 2)]
+ACROSS = [(0, 2), (2, 0), (1, 3), (3, 1)]
 f32, bf16 = jnp.float32, jnp.bfloat16
 
 NN = (((1,), (0,)), ((), ()))
@@ -83,11 +85,32 @@
         + [pltpu.VMEM((groups * sub, LANES), f32), pltpu.SemaphoreType.DMA((4,))],
         2 * 2 * CAP * groups * tokens.size,
         4 * 2**20,
-        [pl.BlockSpec(memory_space=pltpu.HBM)] * 4,
+        [pl.BlockSpec(memory_space=pl.ANY)] * 4,
+        60,
     )(ids_t, prob_t, tokens, cotangent)
 
 
-def expert_body(core_ref, got_ref, w_ref, back_ref, keep_ref, send_ref, x_ref, q_ref, da_ref, du_ref, h_ref, stage, stage_back):
+def rows_body(
+    place_ref, got_ref, w0_hbm, w1_hbm, w2_hbm, w3_hbm, back_hbm, x_hbm, q_hbm, da_hbm, du_hbm, h_hbm,
+    w_ref, back_ref, x_ref, q_ref, da_ref, du_ref, h_ref, stage, stage_back, sems,
+):
+    depth = w0_hbm.shape[1]
+    pairs = [
+        (w_hbm, w_ref.at[:, pl.ds(pl.multiple_of(place_ref[i] * depth, depth), depth), :])
+        for i, w_hbm in enumerate((w0_hbm, w1_hbm, w2_hbm, w3_hbm))
+    ]
+    parts = len(pairs)
+    pairs += [
+        (x_ref, x_hbm),
+        (q_ref, q_hbm),
+        (h_ref, h_hbm),
+        (da_ref, da_hbm),
+        (du_ref, du_hbm),
+        (back_ref, back_hbm),
+    ]
+    copies = [pltpu.make_async_copy(src, dst, sems.at[i]) for i, (src, dst) in enumerate(pairs)]
+    for copy in copies[:parts]:
+        copy.start()
     groups, _, sub, _ = got_ref.shape
     chunks = sub // 2
     for r in range(CAP):
@@ -97,6 +120,10 @@
             cols = slice(c * LANES, (c + 1) * LANES)
             x_ref[at, cols] = stage[pl.ds(c, groups, stride=sub), :].astype(bf16)
             q_ref[at, cols] = stage[pl.ds(chunks + c, groups, stride=sub), :].astype(bf16)
+    for copy in copies[:parts]:
+        copy.wait()
+    for copy in copies[parts : parts + 2]:
+        copy.start()
     x = x_ref[...]
     a = mul(x, w_ref[0], NN)
     u = mul(x, w_ref[1], NN)
@@ -109,17 +136,52 @@
     h_ref[...] = h
     da_ref[...] = da
     du_ref[...] = du
+    for copy in copies[parts + 2 : parts + 5]:
+        copy.start()
     gate = jnp.sum(h.astype(f32) * dh, axis=1, keepdims=True)
     rows = mul(da, w_ref[0], NT) + mul(du, w_ref[1], NT)
     lines = stage_back.shape[0] // groups
+    lane = lax.broadcasted_iota(jnp.int32, (groups, LANES), 1)
+    gates = jnp.zeros((groups, LANES), f32)
     for r in range(CAP):
         at = slice(r * groups, (r + 1) * groups)
         for c in range(chunks):
             stage_back[pl.ds(r * chunks + c, groups, stride=lines), :] = rows[at, c * LANES : (c + 1) * LANES]
-        stage_back[pl.ds(CAP * chunks + r, groups, stride=lines), :] = jnp.broadcast_to(gate[at], (groups, LANES))
-    for spare in range(CAP * (chunks + 1), lines):
+        gates = jnp.where(lane == r, gate[at], gates)
+    stage_back[pl.ds(CAP * chunks, groups, stride=lines), :] = gates
+    for spare in range(CAP * chunks + 1, lines):
         stage_back[pl.ds(spare, groups, stride=lines), :] = jnp.zeros((groups, LANES), f32)
     back_ref[...] = stage_back[...].reshape(back_ref.shape).astype(bf16)
+    copies[parts + 5].start()
+    for copy in copies[parts:]:
+        copy.wait()
+
+
+def rows_step(place, got, pieces):
+    groups, _, sub, _ = got.shape
+    three, depth, hidden = pieces[0].shape
+    width = depth * len(pieces)
+    rows, chunks = groups * CAP, sub // 2
+    lines = -(-(CAP * chunks + 1) // 2) * 2
+    made = [(groups * lines // 8, 8, LANES)] + [(rows, width)] * 2 + [(rows, hidden)] * 3
+    anywhere = pl.BlockSpec(memory_space=pl.ANY)
+    return pl.pallas_call(
+        rows_body,
+        out_shape=[jax.ShapeDtypeStruct(s, bf16) for s in made],
+        in_specs=[pl.BlockSpec(memory_space=pltpu.SMEM), pl.BlockSpec(memory_space=pltpu.VMEM)]
+        + [anywhere] * len(pieces),
+        out_specs=[anywhere] * len(made),
+        scratch_shapes=[pltpu.VMEM(s, bf16) for s in [(three, width, hidden)] + made]
+        + [pltpu.VMEM((groups * sub, LANES), f32), pltpu.VMEM((groups * lines, LANES), f32)]
+        + [pltpu.SemaphoreType.DMA((len(pieces) + len(made),))],
+        compiler_params=pltpu.CompilerParams(vmem_limit_bytes=55 * 2**20),
+        cost_estimate=pl.CostEstimate(
+            flops=10 * rows * width * hidden, bytes_accessed=8 * 2**20, transcendentals=0
+        ),
+    )(place, got, *pieces)
+
+
+def grads_body(core_ref, x_ref, q_ref, da_ref, du_ref, h_ref, keep_ref, send_ref):
     halves, _, depth, _ = keep_ref.shape
     for out_ref, core in ((send_ref, 1 - core_ref[0]), (keep_ref, core_ref[0])):
         for half in range(halves):
@@ -129,25 +191,19 @@
             out_ref[half, 2] = mul(q_ref[:, cols], h_ref[...], TN).astype(bf16)
 
 
-def expert_step(core, got, whole):
-    groups, _, sub, _ = got.shape
-    width, hidden = whole.shape[1:]
-    rows, chunks = groups * CAP, sub // 2
-    lines = -(-CAP * (chunks + 1) // 2) * 2
-    like = jax.ShapeDtypeStruct
-    half = like((2, 3, width // 4, hidden), bf16)
+def weight_grads(core, x, q, da, du, h):
+    rows, width = x.shape
+    hidden = h.shape[1]
     vmem = pl.BlockSpec(memory_space=pltpu.VMEM)
-    return call(
-        expert_body,
-        (like((groups * lines // 8, 8, LANES), bf16), half, half),
-        [pltpu.VMEM((rows, width), bf16)] * 2
-        + [pltpu.VMEM((rows, hidden), bf16)] * 3
-        + [pltpu.VMEM((groups * sub, LANES), f32), pltpu.VMEM((groups * lines, LANES), f32)],
-        16 * rows * width * hidden,
-        12 * 2**20,
-        [pl.BlockSpec(memory_space=pltpu.SMEM), vmem, vmem],
-        30,
-    )(core, got, whole)
+    half = jax.ShapeDtypeStruct((2, 3, width // 4, hidden), bf16)
+    return call(
+        grads_body,
+        (half, half),
+        [],
+        6 * rows * width * hidden,
+        6 * 2**20,
+        [pl.BlockSpec(memory_space=pltpu.SMEM)] + [vmem] * 5,
+    )(core, x, q, da, du, h)
 
 
 def pair_body(side_ref, keep_ref, got_ref, own_ref, send_ref):
@@ -249,7 +305,8 @@
                 pl.ds(r * chunks + c, groups, stride=lines), :
             ].astype(bf16)
     tok_ref[...] = mul(jnp.concatenate(picks, axis=0).astype(bf16), rows[...], TN).astype(bf16)
-    gate_at = sum(picks[r] * stage[pl.ds(CAP * chunks + r, groups, stride=lines), :] for r in range(CAP))
+    gates = stage[pl.ds(CAP * chunks, groups, stride=lines), :]
+    gate_at = sum(picks[r] * gates[:, r : r + 1] for r in range(CAP))
     for k in range(2):
         total = jnp.sum(jnp.where(hots[k], gate_at, 0.0), axis=0, keepdims=True)
         gate_ref[k : k + 1, :] = total / prob_ref[k : k + 1, :].astype(f32)
@@ -290,12 +347,18 @@
     core, side = (replica % 2).reshape(1), (replica // 2).reshape(1)
     tiles, pairs = (-1, 8, LANES), (groups, -1, 2, LANES)
 
-    whole = lax.all_gather(expert_weights, "dp", axis=2, tiled=True)[0]
-    got = exchange(dispatch(ids_t, prob_t, tokens, cotangent, groups))
-    returned, keep, sent = expert_step(core, got, whole)
-    own, sent = pair_sum(side, keep, lax.ppermute(sent, "dp", [(0, 1), (1, 0), (2, 3), (3, 2)]))
+    sent = dispatch(ids_t, prob_t, tokens, cotangent, groups)
+    mine, sent = lax.optimization_barrier((expert_weights[0], sent))
+    got = exchange(sent)
+    far = lax.ppermute(mine, "dp", ACROSS)
+    pieces = (mine, far, lax.ppermute(mine, "dp", BESIDE), lax.ppermute(far, "dp", BESIDE))
+    near = side * 2
+    place = jnp.concatenate([near + core, 2 - near + core, near + 1 - core, 3 - near - core])
+    returned, *operands = rows_step(place, got, pieces)
+    keep, sent = weight_grads(core, *operands)
+    own, sent = pair_sum(side, keep, lax.ppermute(sent, "dp", BESIDE))
     back = exchange(returned.reshape(pairs))
-    other = lax.ppermute(sent, "dp", [(0, 2), (2, 0), (1, 3), (3, 1)])
+    other = lax.ppermute(sent, "dp", ACROSS)
     staged = adam_update(
         own.reshape(flat), other.reshape(flat), first_moment.reshape(flat), second_moment.reshape(flat)
     )

time: 273 us -> 254 us (0.930)
  waiting for transfers between devices: 152 us -> 138 us
  between operations: 14.2 us -> 0.85 us
  starting transfers between devices: 40.6 us -> 48.1 us
  local copies, waits for them, and re-layouts: 6.88 us -> 4.1 us
    all_gather x1 -> x0, waiting for transfers between devices: 41.8 us -> none  [on_device(): whole = lax.all_gather(expert_weights, 'dp', axis=2, tiled=True)[0]]
    ppermute x2 -> x5, waiting for transfers between devices: 22.6 us -> 39.7 us  [the longest x1 18.8 us: on_device(): other = lax.ppermute(sent, 'dp', ACROSS)]
    all_to_all x3, waiting for transfers between devices: 87 us -> 98.7 us  [exchange(): return lax.all_to_all(x, 'expert', split_axis=0, concat_axis=0, tiled=True)]
    ppermute x2 -> x5, starting transfers between devices: 5.41 us -> 12.7 us  [the longest x1 3.62 us: on_device(): other = lax.ppermute(sent, 'dp', ACROSS)]
    pallas_call x1 -> x2, Pallas kernels: 5.16 us -> 8.08 us  [the longest x1 6.43 us: rows_step(): pl.pallas_call(rows_body, out_shape=[jax.ShapeDtypeStruct(s, bf16) for s...]
    unnamed x24 -> x28, local copies, waits for them, and re-layouts: 6.88 us -> 4.1 us
  transfers between devices with their start and end apart: 6 -> 8, of which waited for: 6 -> 7; matrix products, arithmetic and copies ran while one was open for 0% -> 0% of each run, Pallas kernels for 2% -> 2%
where the time goes in v6:
time: 254 us; the launch traced here: 253 us
  waiting for transfers between devices  138 us (54%)
  starting transfers between devices  48.1 us (19%)
  blocking collectives  43.4 us (17%)
  Pallas kernels  17.1 us (7%)
  local copies, waits for them, and re-layouts  4.1 us (2%)
    all_to_all x3, waiting for transfers between devices, exchange(): return lax.all_to_all(x, 'expert', split_axis=0, concat_axis=0, tiled=True)  98.7 us
    all_to_all x1, blocking collectives, exchange(): return lax.all_to_all(x, 'expert', split_axis=0, concat_axis=0, tiled=True)  43.4 us
    all_to_all x3, starting transfers between devices, exchange(): return lax.all_to_all(x, 'expert', split_axis=0, concat_axis=0, tiled=True)  35.5 us
    ppermute x1, waiting for transfers between devices, on_device(): other = lax.ppermute(sent, 'dp', ACROSS)  18.8 us
    ppermute x1, waiting for transfers between devices, on_device(): far = lax.ppermute(mine, 'dp', ACROSS)  16.6 us
    pallas_call x1, Pallas kernels, rows_step(): pl.pallas_call(rows_body, out_shape=[jax.ShapeDtypeStruct(s, bf16) for s...  6.43 us
  transfers between devices with their start and end apart: 8, of which 7 were waited for; matrix products, arithmetic and copies ran while one was open for 0% of the time, Pallas kernels for 2%

profile of v6, /device:TPU:6, one launch (start us, length us, event | category | flops | bytes accessed | tf_op | source)
XLA Modules:
  0.0 253.1 jit_solution(4881882412103228253)
XLA Ops:
  0.6 3.5 %shard_map.103 = bf16[128,3,16,128]{3,2,1,0:T(8,128)(2,1)} custom-call(s32[2,128]{1,0:T(2,128)} %bitcast.23, bf16[2,128]{1,0:T(2,128)(2,1)} %bitcast.25, bf16[128,1024]{1,0:T(8,128)(2,1)} %tok_hbm.1, bf16[128,1024]{1,0:T(8,128)(2,1)} %cot_hbm.1), custom_call_target="tpu_custom_call" | custom-call | flops 201326592 | bytes 4194304 | tf_op jit(solution)/shard_map/pallas_call | solution.py:81
  4.2 20.7 %all-to-all-start = ((bf16[128,3,16,128]{3,2,1,0:T(8,128)(2,1)}), bf16[128,3,16,128]{3,2,1,0:T(8,128)(2,1)S(1)}, u32[]{:S(2)}, u32[]{:S(2)}) async-start(bf16[128,3,16,128]{3,2,1,0:T(8,128)(2,1)} %shard_map.103), calls=%async_computation | async-start | bytes 3145728 | tf_op jit(solution)/shard_map/all_to_all | solution.py:40
  24.9 3.3 %collective-permute-start = (bf16[3,256,384]{2,1,0:T(8,128)(2,1)S(1)}, bf16[3,256,384]{2,1,0:T(8,128)(2,1)S(1)}, u32[]{:S(2)}, u32[]{:S(2)}) collective-permute-start(bf16[3,256,384]{2,1,0:T(8,128)(2,1)S(1)} %bitcast.30), channel_id=1, source_target_pairs={{0,2},{2,0},{1,3},{3,1},{4,6},{6,4},{5,7},{7,5},{8,10},{10,8},{9,1... | collective-permute-start | bytes 1769480 | tf_op jit(solution)/shard_map/ppermute | solution.py:353
  28.2 1.9 collective-permute-start.1
  30.1 16.6 %collective-permute-done.w1_hbm = bf16[3,256,384]{2,1,0:T(8,128)(2,1)S(1)} collective-permute-done((bf16[3,256,384]{2,1,0:T(8,128)(2,1)S(1)}, bf16[3,256,384]{2,1,0:T(8,128)(2,1)S(1)}, u32[]{:S(2)}, u32[]{:S(2)}) %collective-permute-start) | collective-permute-done | bytes 589856 | tf_op jit(solution)/shard_map/ppermute | solution.py:353
  46.7 1.9 collective-permute-start.2
  49.3 1.5 collective-permute-done.2.w3_hbm
  50.7 51.5 %all-to-all-done.got_ref = bf16[128,3,16,128]{3,2,1,0:T(8,128)(2,1)S(1)} async-done(((bf16[128,3,16,128]{3,2,1,0:T(8,128)(2,1)}), bf16[128,3,16,128]{3,2,1,0:T(8,128)(2,1)S(1)}, u32[]{:S(2)}, u32[]{:S(2)}) %all-to-all-start) | async-done | bytes 1572896 | tf_op jit(solution)/shard_map/all_to_all | solution.py:40
  102.2 1.2 copy-done.10
  103.4 6.4 %shard_map.104 = (bf16[416,8,128]{2,1,0:T(8,128)(2,1)}, bf16[384,1024]{1,0:T(8,128)(2,1)}, bf16[384,1024]{1,0:T(8,128)(2,1)}, bf16[384,384]{1,0:T(8,128)(2,1)}, ...) custom-call(s32[4]{0:T(128)} %pad_add_fusion.place_ref, bf16[128,3,16,128]{3,2,1,0:T(8,128)(2,1)} %copy-done.10, ...), custom_call_target="tpu_custom_call" | custom-call | flops 1509949440 | bytes 8388608 | tf_op jit(solution)/shard_map/pallas_call | solution.py:168
  109.9 8.2 %all-to-all-start.1 = ((bf16[128,13,2,128]{3,2,1,0:T(2,128)(2,1)}), bf16[128,13,2,128]{3,2,1,0:T(2,128)(2,1)S(1)}, u32[]{:S(2)}, u32[]{:S(2)}) async-start(bf16[128,13,2,128]{3,2,1,0:T(2,128)(2,1)} %bitcast.27), calls=%async_computation.1 | async-start | bytes 1703936 | tf_op jit(solution)/shard_map/all_to_all | solution.py:40
  121.0 1.7 shard_map.105
  122.7 1.9 collective-permute-start.3
  124.6 2.8 %collective-permute-done.3.got_ref = bf16[2,3,256,384]{3,2,1,0:T(8,128)(2,1)S(1)} collective-permute-done((bf16[2,3,256,384]{3,2,1,0:T(8,128)(2,1)S(1)}, bf16[2,3,256,384]{3,2,1,0:T(8,128)(2,1)S(1)}, u32[]{:S(2)}, u32[]{:S(2)}) %collective-permute-start.3) | collective-permute-done | bytes 1179680 | tf_op jit(solution)/shard_map/ppermute | solution.py:359
  127.7 3.6 %collective-permute-start.4 = (bf16[3,256,384]{2,1,0:T(8,128)(2,1)S(1)}, bf16[3,256,384]{2,1,0:T(8,128)(2,1)S(1)}, u32[]{:S(2)}, u32[]{:S(2)}) collective-permute-start(bf16[3,256,384]{2,1,0:T(8,128)(2,1)S(1)} %get-tuple-element.30), channel_id=1, source_target_pairs={{0,2},{2,0},{1,3},{3,1},{4,6},{6,4},{5,7},{7,5},{8,10},{10,8},{9,1... | collective-permute-start | bytes 1769480 | tf_op jit(solution)/shard_map/ppermute | solution.py:361
  131.3 18.8 %collective-permute-done.4 = bf16[3,256,384]{2,1,0:T(8,128)(2,1)S(1)} collective-permute-done((bf16[3,256,384]{2,1,0:T(8,128)(2,1)S(1)}, bf16[3,256,384]{2,1,0:T(8,128)(2,1)S(1)}, u32[]{:S(2)}, u32[]{:S(2)}) %collective-permute-start.4) | collective-permute-done | bytes 589856 | tf_op jit(solution)/shard_map/ppermute | solution.py:361
  150.1 1.4 shard_map.107
  151.5 12.8 %all-to-all-done.1 = bf16[128,13,2,128]{3,2,1,0:T(2,128)(2,1)S(1)} async-done(((bf16[128,13,2,128]{3,2,1,0:T(2,128)(2,1)}), bf16[128,13,2,128]{3,2,1,0:T(2,128)(2,1)S(1)}, u32[]{:S(2)}, u32[]{:S(2)}) %all-to-all-start.1) | async-done | bytes 852000 | tf_op jit(solution)/shard_map/all_to_all | solution.py:40
  164.3 43.4 %all_to_all.20.in_ref = bf16[128,9,2,128]{3,2,1,0:T(2,128)(2,1)S(1)} all-to-all(bf16[128,9,2,128]{3,2,1,0:T(2,128)(2,1)S(1)} %bitcast.17), channel_id=1, replica_groups=mesh['expert'=128,'dp'=4] {'expert'}, dimensions={0} | all-to-all | bytes 1179648 | tf_op jit(solution)/shard_map/all_to_all | solution.py:40
  207.7 1.6 shard_map.109
  209.3 6.6 %all-to-all-start.3 = ((bf16[128,9,2,128]{3,2,1,0:T(2,128)(2,1)}), bf16[128,9,2,128]{3,2,1,0:T(2,128)(2,1)S(1)}, u32[]{:S(2)}, u32[]{:S(2)}) async-start(bf16[128,9,2,128]{3,2,1,0:T(2,128)(2,1)} %shard_map.109), calls=%async_computation.3 | async-start | bytes 1179648 | tf_op jit(solution)/shard_map/all_to_all | solution.py:40
  215.9 1.3 shard_map.108
  217.7 34.4 %all-to-all-done.3 = bf16[128,9,2,128]{3,2,1,0:T(2,128)(2,1)S(1)} async-done(((bf16[128,9,2,128]{3,2,1,0:T(2,128)(2,1)}), bf16[128,9,2,128]{3,2,1,0:T(2,128)(2,1)S(1)}, u32[]{:S(2)}, u32[]{:S(2)}) %all-to-all-start.3) | async-done | bytes 589856 | tf_op jit(solution)/shard_map/all_to_all | solution.py:40
  252.1 1.0 shard_map.110
  (31 shorter events, 4.3 us)
Async XLA Ops:
  4.2 20.7 %copy-start.11 = (bf16[1,3,256,384]{3,2,1,0:T(8,128)(2,1)S(1)}, bf16[1,3,256,384]{3,2,1,0:T(8,128)(2,1)}, u32[]{:S(2)}) copy-start(bf16[1,3,256,384]{3,2,1,0:T(8,128)(2,1)} %param.13) | copy-start | bytes 1769476
  4.2 98.0 %all-to-all-start = ((bf16[128,3,16,128]{3,2,1,0:T(8,128)(2,1)}), bf16[128,3,16,128]{3,2,1,0:T(8,128)(2,1)S(1)}, u32[]{:S(2)}, u32[]{:S(2)}) async-start(bf16[128,3,16,128]{3,2,1,0:T(8,128)(2,1)} %shard_map.103), calls=%async_computation | async-start | bytes 3145728 | tf_op jit(solution)/shard_map/all_to_all | solution.py:40
  24.9 21.8 %collective-permute-start = (bf16[3,256,384]{2,1,0:T(8,128)(2,1)S(1)}, bf16[3,256,384]{2,1,0:T(8,128)(2,1)S(1)}, u32[]{:S(2)}, u32[]{:S(2)}) collective-permute-start(bf16[3,256,384]{2,1,0:T(8,128)(2,1)S(1)} %bitcast.30), channel_id=1, source_target_pairs={{0,2},{2,0},{1,3},{3,1},{4,6},{6,4},{5,7},{7,5},{8,10},{10,8},{9,1... | collective-permute-start | bytes 1769480 | tf_op jit(solution)/shard_map/ppermute | solution.py:353
  28.2 21.0 %collective-permute-start.1 = (bf16[3,256,384]{2,1,0:T(8,128)(2,1)S(1)}, bf16[3,256,384]{2,1,0:T(8,128)(2,1)S(1)}, u32[]{:S(2)}, u32[]{:S(2)}) collective-permute-start(bf16[3,256,384]{2,1,0:T(8,128)(2,1)S(1)} %bitcast.31), channel_id=1, source_target_pairs={{0,1},{1,0},{2,3},{3,2},{4,5},{5,4},{6,7},{7,6},{8,9},{9,8},{10,11... | collective-permute-start | bytes 1769480 | tf_op jit(solution)/shard_map/ppermute | solution.py:354
  46.7 55.5 %copy-start.12 = (bf16[3,256,384]{2,1,0:T(8,128)(2,1)}, bf16[3,256,384]{2,1,0:T(8,128)(2,1)S(1)}, u32[]{:S(2)}) copy-start(bf16[3,256,384]{2,1,0:T(8,128)(2,1)S(1)} %collective-permute-done.w1_hbm) | copy-start | bytes 1769476
  46.7 4.0 %collective-permute-start.2 = (bf16[3,256,384]{2,1,0:T(8,128)(2,1)S(1)}, bf16[3,256,384]{2,1,0:T(8,128)(2,1)}, u32[]{:S(2)}, u32[]{:S(2)}) collective-permute-start(bf16[3,256,384]{2,1,0:T(8,128)(2,1)S(1)} %collective-permute-done.w1_hbm), channel_id=1, source_target_pairs={{0,1},{1,0},{2,3},{3,2},{4,5},{5,4},{6,7},{7,6},{8,9},{9,8},{10,11... | collective-permute-start | bytes 1769480 | tf_op jit(solution)/shard_map/ppermute | solution.py:354
  49.3 53.0 %copy-start.13 = (bf16[3,256,384]{2,1,0:T(8,128)(2,1)}, bf16[3,256,384]{2,1,0:T(8,128)(2,1)S(1)}, u32[]{:S(2)}) copy-start(bf16[3,256,384]{2,1,0:T(8,128)(2,1)S(1)} %collective-permute-done.1.w2_hbm) | copy-start | bytes 1769476
  102.2 1.2 copy-start.10
  109.9 8.2 %copy-start.5 = (bf16[384,1024]{1,0:T(8,128)(2,1)S(1)}, bf16[384,1024]{1,0:T(8,128)(2,1)}, u32[]{:S(2)}) copy-start(bf16[384,1024]{1,0:T(8,128)(2,1)} %get-tuple-element.22.x_ref) | copy-start | bytes 2359300
  109.9 8.2 %copy-start.6 = (bf16[384,1024]{1,0:T(8,128)(2,1)S(1)}, bf16[384,1024]{1,0:T(8,128)(2,1)}, u32[]{:S(2)}) copy-start(bf16[384,1024]{1,0:T(8,128)(2,1)} %get-tuple-element.23.q_ref) | copy-start | bytes 2359300
  109.9 54.4 %all-to-all-start.1 = ((bf16[128,13,2,128]{3,2,1,0:T(2,128)(2,1)}), bf16[128,13,2,128]{3,2,1,0:T(2,128)(2,1)S(1)}, u32[]{:S(2)}, u32[]{:S(2)}) async-start(bf16[128,13,2,128]{3,2,1,0:T(2,128)(2,1)} %bitcast.27), calls=%async_computation.1 | async-start | bytes 1703936 | tf_op jit(solution)/shard_map/all_to_all | solution.py:40
  118.1 1.0 copy-start.7
  119.1 1.0 copy-start.8
  120.0 1.0 copy-start.9
  122.7 4.7 %collective-permute-start.3 = (bf16[2,3,256,384]{3,2,1,0:T(8,128)(2,1)S(1)}, bf16[2,3,256,384]{3,2,1,0:T(8,128)(2,1)S(1)}, u32[]{:S(2)}, u32[]{:S(2)}) collective-permute-start(bf16[2,3,256,384]{3,2,1,0:T(8,128)(2,1)S(1)} %get-tuple-element.28), channel_id=1, source_target_pairs={{0,1},{1,0},{2,3},{3,2},{4,5},{5,4},{6,7},{7,6},{8,9},{9,8},{10,11... | collective-permute-start | bytes 3538952 | tf_op jit(solution)/shard_map/ppermute | solution.py:359
  127.4 22.7 %copy-start = (f32[1,3,256,384]{3,2,1,0:T(8,128)S(1)}, f32[1,3,256,384]{3,2,1,0:T(8,128)}, u32[]{:S(2)}) copy-start(f32[1,3,256,384]{3,2,1,0:T(8,128)} %param.14) | copy-start | bytes 3538948
  127.4 22.7 %copy-start.1 = (f32[1,3,256,384]{3,2,1,0:T(8,128)S(1)}, f32[1,3,256,384]{3,2,1,0:T(8,128)}, u32[]{:S(2)}) copy-start(f32[1,3,256,384]{3,2,1,0:T(8,128)} %param.15) | copy-start | bytes 3538948
  127.7 22.4 %collective-permute-start.4 = (bf16[3,256,384]{2,1,0:T(8,128)(2,1)S(1)}, bf16[3,256,384]{2,1,0:T(8,128)(2,1)S(1)}, u32[]{:S(2)}, u32[]{:S(2)}) collective-permute-start(bf16[3,256,384]{2,1,0:T(8,128)(2,1)S(1)} %get-tuple-element.30), channel_id=1, source_target_pairs={{0,2},{2,0},{1,3},{3,1},{4,6},{6,4},{5,7},{7,5},{8,10},{10,8},{9,1... | collective-permute-start | bytes 1769480 | tf_op jit(solution)/shard_map/ppermute | solution.py:361
  151.5 56.2 %copy-start.4 = (s32[128]{0:T(128)S(1)}, s32[128]{0:T(128)}, u32[]{:S(2)}) copy-start(s32[128]{0:T(128)} %partner_ref.1) | copy-start | bytes 1540
  207.7 8.2 %copy-start.2 = (s32[128,2]{0,1:T(2,128)S(1)}, s32[128,2]{0,1:T(2,128)}, u32[]{:S(2)}) copy-start(s32[128,2]{0,1:T(2,128)} %param.10) | copy-start | bytes 3076
  207.7 8.2 %copy-start.3 = (bf16[128,2]{0,1:T(2,128)(2,1)S(1)}, bf16[128,2]{0,1:T(2,128)(2,1)}, u32[]{:S(2)}) copy-start(bf16[128,2]{0,1:T(2,128)(2,1)} %param.11) | copy-start | bytes 1540
  209.3 42.8 %all-to-all-start.3 = ((bf16[128,9,2,128]{3,2,1,0:T(2,128)(2,1)}), bf16[128,9,2,128]{3,2,1,0:T(2,128)(2,1)S(1)}, u32[]{:S(2)}, u32[]{:S(2)}) async-start(bf16[128,9,2,128]{3,2,1,0:T(2,128)(2,1)} %shard_map.109), calls=%async_computation.3 | async-start | bytes 1179648 | tf_op jit(solution)/shard_map/all_to_all | solution.py:40

commit v7 on v6

--- a/solution.py
+++ b/solution.py
@@ -25,11 +25,12 @@
     return lax.dot_general(a, b, dims, preferred_element_type=f32)
 
 
-def call(body, outs, scratch, flops, moved, ins=None, limit=16):
+def call(body, outs, scratch, flops, moved, ins=None, limit=16, out=None):
     return pl.pallas_call(
         body,
         out_shape=outs,
-        **({} if ins is None else {'in_specs': ins}),
+        **({} if ins is None else {"in_specs": ins}),
+        **({} if out is None else {"out_specs": out}),
         scratch_shapes=scratch,
         compiler_params=pltpu.CompilerParams(vmem_limit_bytes=limit * 2**20),
         cost_estimate=pl.CostEstimate(flops=flops, bytes_accessed=moved, transcendentals=0),
@@ -52,12 +53,17 @@
     return hots, [jnp.where(rank == r, named, 0.0) for r in range(CAP)]
 
 
-def dispatch_body(ids_hbm, prob_hbm, tok_hbm, cot_hbm, out_ref, ids_ref, prob_ref, tok_ref, cot_ref, stage, sems):
+def dispatch_body(
+    ids_hbm, prob_hbm, tok_hbm, cot_hbm, out_hbm, ids_ref, prob_ref, tok_ref, cot_ref, out_ref, stage, sems
+):
     pairs = ((ids_hbm, ids_ref), (prob_hbm, prob_ref), (tok_hbm, tok_ref), (cot_hbm, cot_ref))
     copies = [pltpu.make_async_copy(src, dst, sems.at[i]) for i, (src, dst) in enumerate(pairs)]
     for copy in copies:
         copy.start()
-    groups, _, sub, _ = out_ref.shape
+    leaving = [
+        pltpu.make_async_copy(out_ref.at[r], out_hbm.at[:, r], sems.at[len(pairs) + r]) for r in range(CAP)
+    ]
+    _, groups, sub, _ = out_ref.shape
     chunks = sub // 2
     copies[0].wait()
     hots, picks = routing(ids_ref[...], groups)
@@ -65,29 +71,36 @@
     prob = prob_ref[...].astype(f32)
     prob_at = jnp.where(hots[0], prob[0:1, :], jnp.where(hots[1], prob[1:2, :], 0.0))
     copies[2].wait()
+    for r in range(CAP):
+        x = mul(picks[r].astype(bf16), tok_ref[...], NN)
+        for c in range(chunks):
+            stage[r, pl.ds(c, groups, stride=sub), :] = x[:, c * LANES : (c + 1) * LANES]
     copies[3].wait()
     for r in range(CAP):
-        x = mul(picks[r].astype(bf16), tok_ref[...], NN)
         q = mul((picks[r] * prob_at).astype(bf16), cot_ref[...], NN)
         for c in range(chunks):
-            cols = slice(c * LANES, (c + 1) * LANES)
-            stage[pl.ds(c, groups, stride=sub), :] = x[:, cols]
-            stage[pl.ds(chunks + c, groups, stride=sub), :] = q[:, cols]
-        out_ref[:, r] = stage[...].reshape(groups, sub, LANES).astype(bf16)
+            stage[r, pl.ds(chunks + c, groups, stride=sub), :] = q[:, c * LANES : (c + 1) * LANES]
+        out_ref[r] = stage[r].reshape(groups, sub, LANES).astype(bf16)
+        leaving[r].start()
+    for copy in leaving:
+        copy.wait()
 
 
 def dispatch(ids_t, prob_t, tokens, cotangent, groups):
     sub = 2 * tokens.shape[1] // LANES
+    arrays = (ids_t, prob_t, tokens, cotangent)
     return call(
         dispatch_body,
-        jax.ShapeDtypeStruct((groups, CAP, sub, LANES), bf16),
-        [pltpu.VMEM(a.shape, a.dtype) for a in (ids_t, prob_t, tokens, cotangent)]
-        + [pltpu.VMEM((groups * sub, LANES), f32), pltpu.SemaphoreType.DMA((4,))],
+        pltpu.HBM((groups, CAP, sub, LANES), bf16),
+        [pltpu.VMEM(a.shape, a.dtype) for a in arrays]
+        + [pltpu.VMEM((CAP, groups, sub, LANES), bf16), pltpu.VMEM((CAP, groups * sub, LANES), f32)]
+        + [pltpu.SemaphoreType.DMA((len(arrays) + CAP,))],
         2 * 2 * CAP * groups * tokens.size,
         4 * 2**20,
-        [pl.BlockSpec(memory_space=pl.ANY)] * 4,
+        [pl.BlockSpec(memory_space=pl.ANY)] * len(arrays),
         60,
-    )(ids_t, prob_t, tokens, cotangent)
+        pl.BlockSpec(memory_space=pl.ANY),
+    )(*arrays)
 
 
 def rows_body(
@@ -167,14 +180,14 @@
     anywhere = pl.BlockSpec(memory_space=pl.ANY)
     return pl.pallas_call(
         rows_body,
-        out_shape=[jax.ShapeDtypeStruct(s, bf16) for s in made],
+        out_shape=[pltpu.HBM(s, bf16) for s in made],
         in_specs=[pl.BlockSpec(memory_space=pltpu.SMEM), pl.BlockSpec(memory_space=pltpu.VMEM)]
         + [anywhere] * len(pieces),
         out_specs=[anywhere] * len(made),
         scratch_shapes=[pltpu.VMEM(s, bf16) for s in [(three, width, hidden)] + made]
         + [pltpu.VMEM((groups * sub, LANES), f32), pltpu.VMEM((groups * lines, LANES), f32)]
         + [pltpu.SemaphoreType.DMA((len(pieces) + len(made),))],
-        compiler_params=pltpu.CompilerParams(vmem_limit_bytes=55 * 2**20),
+        compiler_params=pltpu.CompilerParams(vmem_limit_bytes=44 * 2**20),
         cost_estimate=pl.CostEstimate(
             flops=10 * rows * width * hidden, bytes_accessed=8 * 2**20, transcendentals=0
         ),

time: 254 us -> 251 us (0.988)
  no operation moved by 1% of the time
where the time goes in v7:
time: 251 us; the launch traced here: 250 us
  waiting for transfers between devices  139 us (55%)
  starting transfers between devices  48.2 us (19%)
  blocking collectives  43.4 us (17%)
  Pallas kernels  15.7 us (6%)
  local copies, waits for them, and re-layouts  2.91 us (1%)
    all_to_all x3, waiting for transfers between devices, exchange(): return lax.all_to_all(x, 'expert', split_axis=0, concat_axis=0, tiled=True)  98.7 us
    all_to_all x1, blocking collectives, exchange(): return lax.all_to_all(x, 'expert', split_axis=0, concat_axis=0, tiled=True)  43.4 us
    all_to_all x3, starting transfers between devices, exchange(): return lax.all_to_all(x, 'expert', split_axis=0, concat_axis=0, tiled=True)  35.5 us
    ppermute x1, waiting for transfers between devices, on_device(): other = lax.ppermute(sent, 'dp', ACROSS)  18.8 us
    ppermute x1, waiting for transfers between devices, on_device(): far = lax.ppermute(mine, 'dp', ACROSS)  16.6 us
    pallas_call x1, Pallas kernels, rows_step(): pl.pallas_call(rows_body, out_shape=[pltpu.HBM(s, bf16) for s in made], i...  5.29 us
  transfers between devices with their start and end apart: 8, of which 7 were waited for; matrix products, arithmetic and copies ran while one was open for 0% of the time, Pallas kernels for 2%

profile of v7, /device:TPU:6, one launch (start us, length us, event | category | flops | bytes accessed | tf_op | source)
XLA Modules:
  0.0 250.5 jit_solution(14429839644320047000)
XLA Ops:
  0.6 3.2 %shard_map.103 = bf16[128,3,16,128]{3,2,1,0:T(8,128)(2,1)} custom-call(s32[2,128]{1,0:T(2,128)} %bitcast.23, bf16[2,128]{1,0:T(2,128)(2,1)} %bitcast.25, bf16[128,1024]{1,0:T(8,128)(2,1)} %tok_hbm.1, bf16[128,1024]{1,0:T(8,128)(2,1)} %cot_hbm.1), custom_call_target="tpu_custom_call" | custom-call | flops 201326592 | bytes 4194304 | tf_op jit(solution)/shard_map/pallas_call | solution.py:92
  3.9 20.7 %all-to-all-start = ((bf16[128,3,16,128]{3,2,1,0:T(8,128)(2,1)}), bf16[128,3,16,128]{3,2,1,0:T(8,128)(2,1)S(1)}, u32[]{:S(2)}, u32[]{:S(2)}) async-start(bf16[128,3,16,128]{3,2,1,0:T(8,128)(2,1)} %shard_map.103), calls=%async_computation | async-start | bytes 3145728 | tf_op jit(solution)/shard_map/all_to_all | solution.py:41
  24.6 3.3 %collective-permute-start = (bf16[3,256,384]{2,1,0:T(8,128)(2,1)S(1)}, bf16[3,256,384]{2,1,0:T(8,128)(2,1)S(1)}, u32[]{:S(2)}, u32[]{:S(2)}) collective-permute-start(bf16[3,256,384]{2,1,0:T(8,128)(2,1)S(1)} %bitcast.27), channel_id=1, source_target_pairs={{0,2},{2,0},{1,3},{3,1},{4,6},{6,4},{5,7},{7,5},{8,10},{10,8},{9,1... | collective-permute-start | bytes 1769480 | tf_op jit(solution)/shard_map/ppermute | solution.py:366
  27.9 1.9 collective-permute-start.1
  29.8 16.6 %collective-permute-done.w1_hbm = bf16[3,256,384]{2,1,0:T(8,128)(2,1)S(1)} collective-permute-done((bf16[3,256,384]{2,1,0:T(8,128)(2,1)S(1)}, bf16[3,256,384]{2,1,0:T(8,128)(2,1)S(1)}, u32[]{:S(2)}, u32[]{:S(2)}) %collective-permute-start) | collective-permute-done | bytes 589856 | tf_op jit(solution)/shard_map/ppermute | solution.py:366
  46.4 1.9 collective-permute-start.2
  48.4 2.0 collective-permute-done.2.w3_hbm
  50.4 51.5 %all-to-all-done.got_ref = bf16[128,3,16,128]{3,2,1,0:T(8,128)(2,1)S(1)} async-done(((bf16[128,3,16,128]{3,2,1,0:T(8,128)(2,1)}), bf16[128,3,16,128]{3,2,1,0:T(8,128)(2,1)S(1)}, u32[]{:S(2)}, u32[]{:S(2)}) %all-to-all-start) | async-done | bytes 1572896 | tf_op jit(solution)/shard_map/all_to_all | solution.py:41
  101.9 5.3 %shard_map.104 = (bf16[416,8,128]{2,1,0:T(8,128)(2,1)}, bf16[384,1024]{1,0:T(8,128)(2,1)}, bf16[384,1024]{1,0:T(8,128)(2,1)}, bf16[384,384]{1,0:T(8,128)(2,1)}, ...) custom-call(s32[4]{0:T(128)S(1)} %pad_add_fusion.place_ref, bf16[128,3,16,128]{3,2,1,0:T(8,128)(2,1)S(1)} %all-to-all-done.got_ref, ...), custom_call_target="tpu_custom_call" | custom-call | flops 1509949440 | bytes 8388608 | tf_op jit(solution)/shard_map/pallas_call | solution.py:181
  107.2 8.2 %all-to-all-start.1 = ((bf16[128,13,2,128]{3,2,1,0:T(2,128)(2,1)}), bf16[128,13,2,128]{3,2,1,0:T(2,128)(2,1)S(1)}, u32[]{:S(2)}, u32[]{:S(2)}) async-start(bf16[128,13,2,128]{3,2,1,0:T(2,128)(2,1)} %bitcast.30), calls=%async_computation.1 | async-start | bytes 1703936 | tf_op jit(solution)/shard_map/all_to_all | solution.py:41
  116.4 1.0 copy-done.9
  118.4 1.6 shard_map.105
  120.0 1.9 collective-permute-start.3
  121.9 2.8 %collective-permute-done.3.got_ref = bf16[2,3,256,384]{3,2,1,0:T(8,128)(2,1)S(1)} collective-permute-done((bf16[2,3,256,384]{3,2,1,0:T(8,128)(2,1)S(1)}, bf16[2,3,256,384]{3,2,1,0:T(8,128)(2,1)S(1)}, u32[]{:S(2)}, u32[]{:S(2)}) %collective-permute-start.3) | collective-permute-done | bytes 1179680 | tf_op jit(solution)/shard_map/ppermute | solution.py:372
  125.0 3.6 %collective-permute-start.4 = (bf16[3,256,384]{2,1,0:T(8,128)(2,1)S(1)}, bf16[3,256,384]{2,1,0:T(8,128)(2,1)S(1)}, u32[]{:S(2)}, u32[]{:S(2)}) collective-permute-start(bf16[3,256,384]{2,1,0:T(8,128)(2,1)S(1)} %get-tuple-element.30), channel_id=1, source_target_pairs={{0,2},{2,0},{1,3},{3,1},{4,6},{6,4},{5,7},{7,5},{8,10},{10,8},{9,1... | collective-permute-start | bytes 1769480 | tf_op jit(solution)/shard_map/ppermute | solution.py:374
  128.7 18.8 %collective-permute-done.4 = bf16[3,256,384]{2,1,0:T(8,128)(2,1)S(1)} collective-permute-done((bf16[3,256,384]{2,1,0:T(8,128)(2,1)S(1)}, bf16[3,256,384]{2,1,0:T(8,128)(2,1)S(1)}, u32[]{:S(2)}, u32[]{:S(2)}) %collective-permute-start.4) | collective-permute-done | bytes 589856 | tf_op jit(solution)/shard_map/ppermute | solution.py:374
  147.5 1.4 shard_map.107
  148.9 12.8 %all-to-all-done.1 = bf16[128,13,2,128]{3,2,1,0:T(2,128)(2,1)S(1)} async-done(((bf16[128,13,2,128]{3,2,1,0:T(2,128)(2,1)}), bf16[128,13,2,128]{3,2,1,0:T(2,128)(2,1)S(1)}, u32[]{:S(2)}, u32[]{:S(2)}) %all-to-all-start.1) | async-done | bytes 852000 | tf_op jit(solution)/shard_map/all_to_all | solution.py:41
  161.7 43.4 %all_to_all.20.in_ref = bf16[128,9,2,128]{3,2,1,0:T(2,128)(2,1)S(1)} all-to-all(bf16[128,9,2,128]{3,2,1,0:T(2,128)(2,1)S(1)} %bitcast.17), channel_id=1, replica_groups=mesh['expert'=128,'dp'=4] {'expert'}, dimensions={0} | all-to-all | bytes 1179648 | tf_op jit(solution)/shard_map/all_to_all | solution.py:41
  205.1 1.6 shard_map.109
  206.7 6.6 %all-to-all-start.3 = ((bf16[128,9,2,128]{3,2,1,0:T(2,128)(2,1)}), bf16[128,9,2,128]{3,2,1,0:T(2,128)(2,1)S(1)}, u32[]{:S(2)}, u32[]{:S(2)}) async-start(bf16[128,9,2,128]{3,2,1,0:T(2,128)(2,1)} %shard_map.109), calls=%async_computation.3 | async-start | bytes 1179648 | tf_op jit(solution)/shard_map/all_to_all | solution.py:41
  213.3 1.3 shard_map.108
  215.1 34.4 %all-to-all-done.3 = bf16[128,9,2,128]{3,2,1,0:T(2,128)(2,1)S(1)} async-done(((bf16[128,9,2,128]{3,2,1,0:T(2,128)(2,1)}), bf16[128,9,2,128]{3,2,1,0:T(2,128)(2,1)S(1)}, u32[]{:S(2)}, u32[]{:S(2)}) %all-to-all-start.3) | async-done | bytes 589856 | tf_op jit(solution)/shard_map/all_to_all | solution.py:41
  249.5 1.0 shard_map.110
  (25 shorter events, 2.8 us)
Async XLA Ops:
  3.9 20.7 %copy-start.5 = (bf16[1,3,256,384]{3,2,1,0:T(8,128)(2,1)S(1)}, bf16[1,3,256,384]{3,2,1,0:T(8,128)(2,1)}, u32[]{:S(2)}) copy-start(bf16[1,3,256,384]{3,2,1,0:T(8,128)(2,1)} %param.13) | copy-start | bytes 1769476
  3.9 98.0 %all-to-all-start = ((bf16[128,3,16,128]{3,2,1,0:T(8,128)(2,1)}), bf16[128,3,16,128]{3,2,1,0:T(8,128)(2,1)S(1)}, u32[]{:S(2)}, u32[]{:S(2)}) async-start(bf16[128,3,16,128]{3,2,1,0:T(8,128)(2,1)} %shard_map.103), calls=%async_computation | async-start | bytes 3145728 | tf_op jit(solution)/shard_map/all_to_all | solution.py:41
  24.6 21.8 %collective-permute-start = (bf16[3,256,384]{2,1,0:T(8,128)(2,1)S(1)}, bf16[3,256,384]{2,1,0:T(8,128)(2,1)S(1)}, u32[]{:S(2)}, u32[]{:S(2)}) collective-permute-start(bf16[3,256,384]{2,1,0:T(8,128)(2,1)S(1)} %bitcast.27), channel_id=1, source_target_pairs={{0,2},{2,0},{1,3},{3,1},{4,6},{6,4},{5,7},{7,5},{8,10},{10,8},{9,1... | collective-permute-start | bytes 1769480 | tf_op jit(solution)/shard_map/ppermute | solution.py:366
  27.9 20.5 %collective-permute-start.1 = (bf16[3,256,384]{2,1,0:T(8,128)(2,1)S(1)}, bf16[3,256,384]{2,1,0:T(8,128)(2,1)S(1)}, u32[]{:S(2)}, u32[]{:S(2)}) collective-permute-start(bf16[3,256,384]{2,1,0:T(8,128)(2,1)S(1)} %bitcast.28), channel_id=1, source_target_pairs={{0,1},{1,0},{2,3},{3,2},{4,5},{5,4},{6,7},{7,6},{8,9},{9,8},{10,11... | collective-permute-start | bytes 1769480 | tf_op jit(solution)/shard_map/ppermute | solution.py:367
  46.4 4.0 %collective-permute-start.2 = (bf16[3,256,384]{2,1,0:T(8,128)(2,1)S(1)}, bf16[3,256,384]{2,1,0:T(8,128)(2,1)}, u32[]{:S(2)}, u32[]{:S(2)}) collective-permute-start(bf16[3,256,384]{2,1,0:T(8,128)(2,1)S(1)} %collective-permute-done.w1_hbm), channel_id=1, source_target_pairs={{0,1},{1,0},{2,3},{3,2},{4,5},{5,4},{6,7},{7,6},{8,9},{9,8},{10,11... | collective-permute-start | bytes 1769480 | tf_op jit(solution)/shard_map/ppermute | solution.py:367
  107.2 8.2 %copy-start.6 = (bf16[384,1024]{1,0:T(8,128)(2,1)S(1)}, bf16[384,1024]{1,0:T(8,128)(2,1)}, u32[]{:S(2)}) copy-start(bf16[384,1024]{1,0:T(8,128)(2,1)} %get-tuple-element.22.x_ref) | copy-start | bytes 2359300
  107.2 8.2 %copy-start.7 = (bf16[384,1024]{1,0:T(8,128)(2,1)S(1)}, bf16[384,1024]{1,0:T(8,128)(2,1)}, u32[]{:S(2)}) copy-start(bf16[384,1024]{1,0:T(8,128)(2,1)} %get-tuple-element.23.q_ref) | copy-start | bytes 2359300
  107.2 54.4 %all-to-all-start.1 = ((bf16[128,13,2,128]{3,2,1,0:T(2,128)(2,1)}), bf16[128,13,2,128]{3,2,1,0:T(2,128)(2,1)S(1)}, u32[]{:S(2)}, u32[]{:S(2)}) async-start(bf16[128,13,2,128]{3,2,1,0:T(2,128)(2,1)} %bitcast.30), calls=%async_computation.1 | async-start | bytes 1703936 | tf_op jit(solution)/shard_map/all_to_all | solution.py:41
  115.5 1.0 copy-start.8
  116.4 1.0 copy-start.9
  117.4 1.0 copy-start.10
  120.0 4.7 %collective-permute-start.3 = (bf16[2,3,256,384]{3,2,1,0:T(8,128)(2,1)S(1)}, bf16[2,3,256,384]{3,2,1,0:T(8,128)(2,1)S(1)}, u32[]{:S(2)}, u32[]{:S(2)}) collective-permute-start(bf16[2,3,256,384]{3,2,1,0:T(8,128)(2,1)S(1)} %get-tuple-element.28), channel_id=1, source_target_pairs={{0,1},{1,0},{2,3},{3,2},{4,5},{5,4},{6,7},{7,6},{8,9},{9,8},{10,11... | collective-permute-start | bytes 3538952 | tf_op jit(solution)/shard_map/ppermute | solution.py:372
  124.8 22.7 %copy-start = (f32[1,3,256,384]{3,2,1,0:T(8,128)S(1)}, f32[1,3,256,384]{3,2,1,0:T(8,128)}, u32[]{:S(2)}) copy-start(f32[1,3,256,384]{3,2,1,0:T(8,128)} %param.14) | copy-start | bytes 3538948
  124.8 22.7 %copy-start.1 = (f32[1,3,256,384]{3,2,1,0:T(8,128)S(1)}, f32[1,3,256,384]{3,2,1,0:T(8,128)}, u32[]{:S(2)}) copy-start(f32[1,3,256,384]{3,2,1,0:T(8,128)} %param.15) | copy-start | bytes 3538948
  125.0 22.4 %collective-permute-start.4 = (bf16[3,256,384]{2,1,0:T(8,128)(2,1)S(1)}, bf16[3,256,384]{2,1,0:T(8,128)(2,1)S(1)}, u32[]{:S(2)}, u32[]{:S(2)}) collective-permute-start(bf16[3,256,384]{2,1,0:T(8,128)(2,1)S(1)} %get-tuple-element.30), channel_id=1, source_target_pairs={{0,2},{2,0},{1,3},{3,1},{4,6},{6,4},{5,7},{7,5},{8,10},{10,8},{9,1... | collective-permute-start | bytes 1769480 | tf_op jit(solution)/shard_map/ppermute | solution.py:374
  148.9 56.2 %copy-start.4 = (s32[128]{0:T(128)S(1)}, s32[128]{0:T(128)}, u32[]{:S(2)}) copy-start(s32[128]{0:T(128)} %partner_ref.1) | copy-start | bytes 1540
  205.1 8.2 %copy-start.2 = (s32[128,2]{0,1:T(2,128)S(1)}, s32[128,2]{0,1:T(2,128)}, u32[]{:S(2)}) copy-start(s32[128,2]{0,1:T(2,128)} %param.10) | copy-start | bytes 3076
  205.1 8.2 %copy-start.3 = (bf16[128,2]{0,1:T(2,128)(2,1)S(1)}, bf16[128,2]{0,1:T(2,128)(2,1)}, u32[]{:S(2)}) copy-start(bf16[128,2]{0,1:T(2,128)(2,1)} %param.11) | copy-start | bytes 1540
  206.7 42.8 %all-to-all-start.3 = ((bf16[128,9,2,128]{3,2,1,0:T(2,128)(2,1)}), bf16[128,9,2,128]{3,2,1,0:T(2,128)(2,1)S(1)}, u32[]{:S(2)}, u32[]{:S(2)}) async-start(bf16[128,9,2,128]{3,2,1,0:T(2,128)(2,1)} %shard_map.109), calls=%async_computation.3 | async-start | bytes 1179648 | tf_op jit(solution)/shard_map/all_to_all | solution.py:41

commit v8 on v7

--- a/solution.py
+++ b/solution.py
@@ -11,7 +11,6 @@
 ADAM_EPS = 1e-08
 CAP = 3
 LANES = 128
-SLOTS = 128
 BESIDE = [(0, 1), (1, 0), (2, 3), (3, 2)]
 ACROSS = [(0, 2), (2, 0), (1, 3), (3, 1)]
 f32, bf16 = jnp.float32, jnp.bfloat16
@@ -240,11 +239,11 @@
     )(side, keep, got)
 
 
-def adam_body(own_ref, other_ref, one_ref, two_ref, out_ref, stage):
-    blocks = own_ref.shape[1] // LANES
-    lines = own_ref.shape[0] * blocks // SLOTS
-    for p in range(lines // blocks):
-        at = slice(p * SLOTS, (p + 1) * SLOTS)
+def adam_body(own_ref, other_ref, one_ref, two_ref, out_ref):
+    bands, blocks, sub, _ = out_ref.shape
+    step = 16
+    for p in range(0, bands, step):
+        at = slice(p * sub, (p + step) * sub)
         grad = own_ref[at, :] + other_ref[at, :].astype(f32)
         first_new = BETA_ONE * one_ref[at, :] + (1.0 - BETA_ONE) * grad
         second_new = BETA_TWO * two_ref[at, :] + (1.0 - BETA_TWO) * grad * grad
@@ -252,15 +251,16 @@
         second_hat = second_new * (1.0 / (1.0 - BETA_TWO**STEP))
         update = first_hat / (jnp.sqrt(second_hat) + ADAM_EPS)
         for b in range(blocks):
-            stage[pl.ds(p * blocks + b, SLOTS, stride=lines), :] = update[:, b * LANES : (b + 1) * LANES]
-    out_ref[...] = stage[...].reshape(out_ref.shape).astype(bf16)
+            tiles = update[:, b * LANES : (b + 1) * LANES].reshape(step, sub, LANES)
+            out_ref[p : p + step, b] = tiles.astype(bf16)
 
 
 def adam_update(own, other, moment_one, moment_two):
+    rows, hidden = own.shape
     return call(
         adam_body,
-        jax.ShapeDtypeStruct((own.size // (8 * LANES), 8, LANES), bf16),
-        [pltpu.VMEM((own.size // LANES, LANES), f32)],
+        jax.ShapeDtypeStruct((rows // 8, hidden // LANES, 8, LANES), bf16),
+        [],
         12 * own.size,
         14 * own.size,
     )(own, other, moment_one, moment_two)
@@ -284,27 +284,6 @@
         4 * spread.size,
         [pl.BlockSpec(memory_space=pltpu.SMEM), vmem],
     )(partner, spread)
-
-
-def collect_body(in_ref, out_ref, stage):
-    stage[...] = in_ref[...].astype(f32).reshape(stage.shape)
-    blocks = out_ref.shape[1] // LANES
-    lines = stage.shape[0] // SLOTS
-    for p in range(lines // blocks):
-        for b in range(blocks):
-            out_ref[p * SLOTS : (p + 1) * SLOTS, b * LANES : (b + 1) * LANES] = stage[
-                pl.ds(p * blocks + b, SLOTS, stride=lines), :
-            ].astype(bf16)
-
-
-def collect(routed, shape):
-    return call(
-        collect_body,
-        jax.ShapeDtypeStruct(shape, bf16),
-        [pltpu.VMEM((routed.size // LANES, LANES), f32)],
-        0,
-        4 * routed.size,
-    )(routed)
 
 
 def combine_body(ids_ref, prob_ref, back_ref, tok_ref, gate_ref, stage, rows):
@@ -379,7 +358,7 @@
     spread = exchange(staged.reshape(pairs))
     routed = exchange(swap_slots(swap_partner, spread))
     token_grad, gate_grad = combine(ids_t, prob_t, back.reshape(tiles), tokens.shape[1], groups)
-    update = collect(routed.reshape(tiles), flat)
+    update = routed.reshape(staged.shape).transpose(0, 2, 1, 3)
     return (token_grad, gate_grad.T.astype(bf16), update.reshape(expert_weights.shape))
 
 

time: 251 us -> 251 us (level)
  no operation moved by 1% of the time
where the time goes in v8:
time: 251 us; the launch traced here: 250 us
  waiting for transfers between devices  139 us (55%)
  starting transfers between devices  48.2 us (19%)
  blocking collectives  43.4 us (17%)
  Pallas kernels  14.1 us (6%)
  local copies, waits for them, and re-layouts  3.73 us (1%)
    all_to_all x3, waiting for transfers between devices, exchange(): return lax.all_to_all(x, 'expert', split_axis=0, concat_axis=0, tiled=True)  99.2 us
    all_to_all x1, blocking collectives, exchange(): return lax.all_to_all(x, 'expert', split_axis=0, concat_axis=0, tiled=True)  43.4 us
    all_to_all x3, starting transfers between devices, exchange(): return lax.all_to_all(x, 'expert', split_axis=0, concat_axis=0, tiled=True)  35.5 us
    ppermute x1, waiting for transfers between devices, on_device(): other = lax.ppermute(sent, 'dp', ACROSS)  18.8 us
    ppermute x1, waiting for transfers between devices, on_device(): far = lax.ppermute(mine, 'dp', ACROSS)  16.6 us
    pallas_call x1, Pallas kernels, rows_step(): pl.pallas_call(rows_body, out_shape=[pltpu.HBM(s, bf16) for s in made], i...  5.29 us
  transfers between devices with their start and end apart: 8, of which 7 were waited for; matrix products, arithmetic and copies ran while one was open for 0% of the time, Pallas kernels for 2%

profile of v8, /device:TPU:6, one launch (start us, length us, event | category | flops | bytes accessed | tf_op | source)
XLA Modules:
  0.0 250.3 jit_solution(15219116284341294668)
XLA Ops:
  0.6 3.2 %shard_map.103 = bf16[128,3,16,128]{3,2,1,0:T(8,128)(2,1)} custom-call(s32[2,128]{1,0:T(2,128)} %bitcast.25, bf16[2,128]{1,0:T(2,128)(2,1)} %bitcast.27, bf16[128,1024]{1,0:T(8,128)(2,1)} %tok_hbm.1, bf16[128,1024]{1,0:T(8,128)(2,1)} %cot_hbm.1), custom_call_target="tpu_custom_call" | custom-call | flops 201326592 | bytes 4194304 | tf_op jit(solution)/shard_map/pallas_call | solution.py:91
  3.9 20.7 %all-to-all-start = ((bf16[128,3,16,128]{3,2,1,0:T(8,128)(2,1)}), bf16[128,3,16,128]{3,2,1,0:T(8,128)(2,1)S(1)}, u32[]{:S(2)}, u32[]{:S(2)}) async-start(bf16[128,3,16,128]{3,2,1,0:T(8,128)(2,1)} %shard_map.103), calls=%async_computation | async-start | bytes 3145728 | tf_op jit(solution)/shard_map/all_to_all | solution.py:40
  24.6 3.3 %collective-permute-start = (bf16[3,256,384]{2,1,0:T(8,128)(2,1)S(1)}, bf16[3,256,384]{2,1,0:T(8,128)(2,1)S(1)}, u32[]{:S(2)}, u32[]{:S(2)}) collective-permute-start(bf16[3,256,384]{2,1,0:T(8,128)(2,1)S(1)} %bitcast.29), channel_id=1, source_target_pairs={{0,2},{2,0},{1,3},{3,1},{4,6},{6,4},{5,7},{7,5},{8,10},{10,8},{9,1... | collective-permute-start | bytes 1769480 | tf_op jit(solution)/shard_map/ppermute | solution.py:345
  27.9 1.9 collective-permute-start.1
  29.8 16.6 %collective-permute-done.w1_hbm = bf16[3,256,384]{2,1,0:T(8,128)(2,1)S(1)} collective-permute-done((bf16[3,256,384]{2,1,0:T(8,128)(2,1)S(1)}, bf16[3,256,384]{2,1,0:T(8,128)(2,1)S(1)}, u32[]{:S(2)}, u32[]{:S(2)}) %collective-permute-start) | collective-permute-done | bytes 589856 | tf_op jit(solution)/shard_map/ppermute | solution.py:345
  46.4 1.9 collective-permute-start.2
  48.4 2.0 collective-permute-done.2.w3_hbm
  50.4 51.5 %all-to-all-done.got_ref = bf16[128,3,16,128]{3,2,1,0:T(8,128)(2,1)S(1)} async-done(((bf16[128,3,16,128]{3,2,1,0:T(8,128)(2,1)}), bf16[128,3,16,128]{3,2,1,0:T(8,128)(2,1)S(1)}, u32[]{:S(2)}, u32[]{:S(2)}) %all-to-all-start) | async-done | bytes 1572896 | tf_op jit(solution)/shard_map/all_to_all | solution.py:40
  101.9 5.3 %shard_map.104 = (bf16[416,8,128]{2,1,0:T(8,128)(2,1)}, bf16[384,1024]{1,0:T(8,128)(2,1)}, bf16[384,1024]{1,0:T(8,128)(2,1)}, bf16[384,384]{1,0:T(8,128)(2,1)}, ...) custom-call(s32[4]{0:T(128)S(1)} %pad_add_fusion.place_ref, bf16[128,3,16,128]{3,2,1,0:T(8,128)(2,1)S(1)} %all-to-all-done.got_ref, ...), custom_call_target="tpu_custom_call" | custom-call | flops 1509949440 | bytes 8388608 | tf_op jit(solution)/shard_map/pallas_call | solution.py:180
  107.2 8.2 %all-to-all-start.1 = ((bf16[128,13,2,128]{3,2,1,0:T(2,128)(2,1)}), bf16[128,13,2,128]{3,2,1,0:T(2,128)(2,1)S(1)}, u32[]{:S(2)}, u32[]{:S(2)}) async-start(bf16[128,13,2,128]{3,2,1,0:T(2,128)(2,1)} %bitcast.33), calls=%async_computation.1 | async-start | bytes 1703936 | tf_op jit(solution)/shard_map/all_to_all | solution.py:40
  115.5 1.0 copy-done.8
  116.4 1.0 copy-done.9
  117.4 1.0 copy-done.10
  118.4 1.6 shard_map.105
  120.0 1.9 collective-permute-start.3
  121.9 2.8 %collective-permute-done.3.got_ref = bf16[2,3,256,384]{3,2,1,0:T(8,128)(2,1)S(1)} collective-permute-done((bf16[2,3,256,384]{3,2,1,0:T(8,128)(2,1)S(1)}, bf16[2,3,256,384]{3,2,1,0:T(8,128)(2,1)S(1)}, u32[]{:S(2)}, u32[]{:S(2)}) %collective-permute-start.3) | collective-permute-done | bytes 1179680 | tf_op jit(solution)/shard_map/ppermute | solution.py:351
  125.0 3.6 %collective-permute-start.4 = (bf16[3,256,384]{2,1,0:T(8,128)(2,1)S(1)}, bf16[3,256,384]{2,1,0:T(8,128)(2,1)S(1)}, u32[]{:S(2)}, u32[]{:S(2)}) collective-permute-start(bf16[3,256,384]{2,1,0:T(8,128)(2,1)S(1)} %get-tuple-element.30), channel_id=1, source_target_pairs={{0,2},{2,0},{1,3},{3,1},{4,6},{6,4},{5,7},{7,5},{8,10},{10,8},{9,1... | collective-permute-start | bytes 1769480 | tf_op jit(solution)/shard_map/ppermute | solution.py:353
  128.7 18.8 %collective-permute-done.4 = bf16[3,256,384]{2,1,0:T(8,128)(2,1)S(1)} collective-permute-done((bf16[3,256,384]{2,1,0:T(8,128)(2,1)S(1)}, bf16[3,256,384]{2,1,0:T(8,128)(2,1)S(1)}, u32[]{:S(2)}, u32[]{:S(2)}) %collective-permute-start.4) | collective-permute-done | bytes 589856 | tf_op jit(solution)/shard_map/ppermute | solution.py:353
  148.3 13.3 %all-to-all-done.1 = bf16[128,13,2,128]{3,2,1,0:T(2,128)(2,1)S(1)} async-done(((bf16[128,13,2,128]{3,2,1,0:T(2,128)(2,1)}), bf16[128,13,2,128]{3,2,1,0:T(2,128)(2,1)S(1)}, u32[]{:S(2)}, u32[]{:S(2)}) %all-to-all-start.1) | async-done | bytes 852000 | tf_op jit(solution)/shard_map/all_to_all | solution.py:40
  161.7 43.4 %all_to_all.20.in_ref = bf16[128,9,2,128]{3,2,1,0:T(2,128)(2,1)S(1)} all-to-all(bf16[128,9,2,128]{3,2,1,0:T(2,128)(2,1)S(1)} %bitcast.20), channel_id=1, replica_groups=mesh['expert'=128,'dp'=4] {'expert'}, dimensions={0} | all-to-all | bytes 1179648 | tf_op jit(solution)/shard_map/all_to_all | solution.py:40
  205.1 1.6 shard_map.109
  206.7 6.6 %all-to-all-start.3 = ((bf16[128,9,2,128]{3,2,1,0:T(2,128)(2,1)}), bf16[128,9,2,128]{3,2,1,0:T(2,128)(2,1)S(1)}, u32[]{:S(2)}, u32[]{:S(2)}) async-start(bf16[128,9,2,128]{3,2,1,0:T(2,128)(2,1)} %shard_map.109), calls=%async_computation.3 | async-start | bytes 1179648 | tf_op jit(solution)/shard_map/all_to_all | solution.py:40
  213.3 1.3 shard_map.108
  215.1 34.4 %all-to-all-done.3 = bf16[128,9,2,128]{3,2,1,0:T(2,128)(2,1)S(1)} async-done(((bf16[128,9,2,128]{3,2,1,0:T(2,128)(2,1)}), bf16[128,9,2,128]{3,2,1,0:T(2,128)(2,1)S(1)}, u32[]{:S(2)}, u32[]{:S(2)}) %all-to-all-start.3) | async-done | bytes 589856 | tf_op jit(solution)/shard_map/all_to_all | solution.py:40
  (25 shorter events, 2.6 us)
Async XLA Ops:
  3.9 20.7 %copy-start.5 = (bf16[1,3,256,384]{3,2,1,0:T(8,128)(2,1)S(1)}, bf16[1,3,256,384]{3,2,1,0:T(8,128)(2,1)}, u32[]{:S(2)}) copy-start(bf16[1,3,256,384]{3,2,1,0:T(8,128)(2,1)} %param.13) | copy-start | bytes 1769476
  3.9 98.0 %all-to-all-start = ((bf16[128,3,16,128]{3,2,1,0:T(8,128)(2,1)}), bf16[128,3,16,128]{3,2,1,0:T(8,128)(2,1)S(1)}, u32[]{:S(2)}, u32[]{:S(2)}) async-start(bf16[128,3,16,128]{3,2,1,0:T(8,128)(2,1)} %shard_map.103), calls=%async_computation | async-start | bytes 3145728 | tf_op jit(solution)/shard_map/all_to_all | solution.py:40
  24.6 21.8 %collective-permute-start = (bf16[3,256,384]{2,1,0:T(8,128)(2,1)S(1)}, bf16[3,256,384]{2,1,0:T(8,128)(2,1)S(1)}, u32[]{:S(2)}, u32[]{:S(2)}) collective-permute-start(bf16[3,256,384]{2,1,0:T(8,128)(2,1)S(1)} %bitcast.29), channel_id=1, source_target_pairs={{0,2},{2,0},{1,3},{3,1},{4,6},{6,4},{5,7},{7,5},{8,10},{10,8},{9,1... | collective-permute-start | bytes 1769480 | tf_op jit(solution)/shard_map/ppermute | solution.py:345
  27.9 20.5 %collective-permute-start.1 = (bf16[3,256,384]{2,1,0:T(8,128)(2,1)S(1)}, bf16[3,256,384]{2,1,0:T(8,128)(2,1)S(1)}, u32[]{:S(2)}, u32[]{:S(2)}) collective-permute-start(bf16[3,256,384]{2,1,0:T(8,128)(2,1)S(1)} %bitcast.30), channel_id=1, source_target_pairs={{0,1},{1,0},{2,3},{3,2},{4,5},{5,4},{6,7},{7,6},{8,9},{9,8},{10,11... | collective-permute-start | bytes 1769480 | tf_op jit(solution)/shard_map/ppermute | solution.py:346
  46.4 4.0 %collective-permute-start.2 = (bf16[3,256,384]{2,1,0:T(8,128)(2,1)S(1)}, bf16[3,256,384]{2,1,0:T(8,128)(2,1)}, u32[]{:S(2)}, u32[]{:S(2)}) collective-permute-start(bf16[3,256,384]{2,1,0:T(8,128)(2,1)S(1)} %collective-permute-done.w1_hbm), channel_id=1, source_target_pairs={{0,1},{1,0},{2,3},{3,2},{4,5},{5,4},{6,7},{7,6},{8,9},{9,8},{10,11... | collective-permute-start | bytes 1769480 | tf_op jit(solution)/shard_map/ppermute | solution.py:346
  107.2 8.2 %copy-start.6 = (bf16[384,1024]{1,0:T(8,128)(2,1)S(1)}, bf16[384,1024]{1,0:T(8,128)(2,1)}, u32[]{:S(2)}) copy-start(bf16[384,1024]{1,0:T(8,128)(2,1)} %get-tuple-element.22.x_ref) | copy-start | bytes 2359300
  107.2 8.2 %copy-start.7 = (bf16[384,1024]{1,0:T(8,128)(2,1)S(1)}, bf16[384,1024]{1,0:T(8,128)(2,1)}, u32[]{:S(2)}) copy-start(bf16[384,1024]{1,0:T(8,128)(2,1)} %get-tuple-element.23.q_ref) | copy-start | bytes 2359300
  107.2 54.4 %all-to-all-start.1 = ((bf16[128,13,2,128]{3,2,1,0:T(2,128)(2,1)}), bf16[128,13,2,128]{3,2,1,0:T(2,128)(2,1)S(1)}, u32[]{:S(2)}, u32[]{:S(2)}) async-start(bf16[128,13,2,128]{3,2,1,0:T(2,128)(2,1)} %bitcast.33), calls=%async_computation.1 | async-start | bytes 1703936 | tf_op jit(solution)/shard_map/all_to_all | solution.py:40
  115.5 1.0 copy-start.8
  116.4 1.0 copy-start.9
  117.4 1.0 copy-start.10
  120.0 4.7 %collective-permute-start.3 = (bf16[2,3,256,384]{3,2,1,0:T(8,128)(2,1)S(1)}, bf16[2,3,256,384]{3,2,1,0:T(8,128)(2,1)S(1)}, u32[]{:S(2)}, u32[]{:S(2)}) collective-permute-start(bf16[2,3,256,384]{3,2,1,0:T(8,128)(2,1)S(1)} %get-tuple-element.28), channel_id=1, source_target_pairs={{0,1},{1,0},{2,3},{3,2},{4,5},{5,4},{6,7},{7,6},{8,9},{9,8},{10,11... | collective-permute-start | bytes 3538952 | tf_op jit(solution)/shard_map/ppermute | solution.py:351
  124.8 22.7 %copy-start = (f32[1,3,256,384]{3,2,1,0:T(8,128)S(1)}, f32[1,3,256,384]{3,2,1,0:T(8,128)}, u32[]{:S(2)}) copy-start(f32[1,3,256,384]{3,2,1,0:T(8,128)} %param.14) | copy-start | bytes 3538948
  124.8 22.7 %copy-start.1 = (f32[1,3,256,384]{3,2,1,0:T(8,128)S(1)}, f32[1,3,256,384]{3,2,1,0:T(8,128)}, u32[]{:S(2)}) copy-start(f32[1,3,256,384]{3,2,1,0:T(8,128)} %param.15) | copy-start | bytes 3538948
  125.0 22.4 %collective-permute-start.4 = (bf16[3,256,384]{2,1,0:T(8,128)(2,1)S(1)}, bf16[3,256,384]{2,1,0:T(8,128)(2,1)S(1)}, u32[]{:S(2)}, u32[]{:S(2)}) collective-permute-start(bf16[3,256,384]{2,1,0:T(8,128)(2,1)S(1)} %get-tuple-element.30), channel_id=1, source_target_pairs={{0,2},{2,0},{1,3},{3,1},{4,6},{6,4},{5,7},{7,5},{8,10},{10,8},{9,1... | collective-permute-start | bytes 1769480 | tf_op jit(solution)/shard_map/ppermute | solution.py:353
  148.3 56.8 %copy-start.4 = (s32[128]{0:T(128)S(1)}, s32[128]{0:T(128)}, u32[]{:S(2)}) copy-start(s32[128]{0:T(128)} %partner_ref.1) | copy-start | bytes 1540
  205.1 8.2 %copy-start.2 = (s32[128,2]{0,1:T(2,128)S(1)}, s32[128,2]{0,1:T(2,128)}, u32[]{:S(2)}) copy-start(s32[128,2]{0,1:T(2,128)} %param.10) | copy-start | bytes 3076
  205.1 8.2 %copy-start.3 = (bf16[128,2]{0,1:T(2,128)(2,1)S(1)}, bf16[128,2]{0,1:T(2,128)(2,1)}, u32[]{:S(2)}) copy-start(bf16[128,2]{0,1:T(2,128)(2,1)} %param.11) | copy-start | bytes 1540
  206.7 42.8 %all-to-all-start.3 = ((bf16[128,9,2,128]{3,2,1,0:T(2,128)(2,1)}), bf16[128,9,2,128]{3,2,1,0:T(2,128)(2,1)S(1)}, u32[]{:S(2)}, u32[]{:S(2)}) async-start(bf16[128,9,2,128]{3,2,1,0:T(2,128)(2,1)} %shard_map.109), calls=%async_computation.3 | async-start | bytes 1179648 | tf_op jit(solution)/shard_map/all_to_all | solution.py:40

commit v9 on v8

--- a/solution.py
+++ b/solution.py
@@ -11,6 +11,7 @@
 ADAM_EPS = 1e-08
 CAP = 3
 LANES = 128
+PORTIONS = 4
 BESIDE = [(0, 1), (1, 0), (2, 3), (3, 2)]
 ACROSS = [(0, 2), (2, 0), (1, 3), (3, 1)]
 f32, bf16 = jnp.float32, jnp.bfloat16
@@ -118,8 +119,10 @@
         (h_ref, h_hbm),
         (da_ref, da_hbm),
         (du_ref, du_hbm),
-        (back_ref, back_hbm),
     ]
+    portion = back_ref.shape[0] // PORTIONS
+    cuts = [pl.ds(k * portion, portion) for k in range(PORTIONS)]
+    pairs += [(back_ref.at[cut], back_hbm.at[cut]) for cut in cuts]
     copies = [pltpu.make_async_copy(src, dst, sems.at[i]) for i, (src, dst) in enumerate(pairs)]
     for copy in copies[:parts]:
         copy.start()
@@ -163,8 +166,10 @@
     stage_back[pl.ds(CAP * chunks, groups, stride=lines), :] = gates
     for spare in range(CAP * chunks + 1, lines):
         stage_back[pl.ds(spare, groups, stride=lines), :] = jnp.zeros((groups, LANES), f32)
-    back_ref[...] = stage_back[...].reshape(back_ref.shape).astype(bf16)
-    copies[parts + 5].start()
+    for k, cut in enumerate(cuts):
+        packed = stage_back[k * portion * 8 : (k + 1) * portion * 8, :]
+        back_ref[cut] = packed.reshape(portion, 8, LANES).astype(bf16)
+        copies[parts + 5 + k].start()
     for copy in copies[parts:]:
         copy.wait()
 
@@ -185,7 +190,7 @@
         out_specs=[anywhere] * len(made),
         scratch_shapes=[pltpu.VMEM(s, bf16) for s in [(three, width, hidden)] + made]
         + [pltpu.VMEM((groups * sub, LANES), f32), pltpu.VMEM((groups * lines, LANES), f32)]
-        + [pltpu.SemaphoreType.DMA((len(pieces) + len(made),))],
+        + [pltpu.SemaphoreType.DMA((len(pieces) + len(made) - 1 + PORTIONS,))],
         compiler_params=pltpu.CompilerParams(vmem_limit_bytes=44 * 2**20),
         cost_estimate=pl.CostEstimate(
             flops=10 * rows * width * hidden, bytes_accessed=8 * 2**20, transcendentals=0

time: 251 us -> 251 us (level)
  no operation moved by 1% of the time
where the time goes in v9:
time: 251 us; the launch traced here: 250 us
  waiting for transfers between devices  139 us (55%)
  starting transfers between devices  48.2 us (19%)
  blocking collectives  43.4 us (17%)
  Pallas kernels  14.1 us (6%)
  local copies, waits for them, and re-layouts  3.73 us (1%)
    all_to_all x3, waiting for transfers between devices, exchange(): return lax.all_to_all(x, 'expert', split_axis=0, concat_axis=0, tiled=True)  99.2 us
    all_to_all x1, blocking collectives, exchange(): return lax.all_to_all(x, 'expert', split_axis=0, concat_axis=0, tiled=True)  43.4 us
    all_to_all x3, starting transfers between devices, exchange(): return lax.all_to_all(x, 'expert', split_axis=0, concat_axis=0, tiled=True)  35.4 us
    ppermute x1, waiting for transfers between devices, on_device(): other = lax.ppermute(sent, 'dp', ACROSS)  18.8 us
    ppermute x1, waiting for transfers between devices, on_device(): far = lax.ppermute(mine, 'dp', ACROSS)  16.6 us
    pallas_call x1, Pallas kernels, rows_step(): pl.pallas_call(rows_body, out_shape=[pltpu.HBM(s, bf16) for s in made], i...  5.24 us
  transfers between devices with their start and end apart: 8, of which 7 were waited for; matrix products, arithmetic and copies ran while one was open for 0% of the time, Pallas kernels for 2%

profile of v9, /device:TPU:6, one launch (start us, length us, event | category | flops | bytes accessed | tf_op | source)
XLA Modules:
  0.0 250.2 jit_solution(9712323642748880569)
XLA Ops:
  0.6 3.2 %shard_map.103 = bf16[128,3,16,128]{3,2,1,0:T(8,128)(2,1)} custom-call(s32[2,128]{1,0:T(2,128)} %bitcast.25, bf16[2,128]{1,0:T(2,128)(2,1)} %bitcast.27, bf16[128,1024]{1,0:T(8,128)(2,1)} %tok_hbm.1, bf16[128,1024]{1,0:T(8,128)(2,1)} %cot_hbm.1), custom_call_target="tpu_custom_call" | custom-call | flops 201326592 | bytes 4194304 | tf_op jit(solution)/shard_map/pallas_call | solution.py:92
  3.9 20.7 %all-to-all-start = ((bf16[128,3,16,128]{3,2,1,0:T(8,128)(2,1)}), bf16[128,3,16,128]{3,2,1,0:T(8,128)(2,1)S(1)}, u32[]{:S(2)}, u32[]{:S(2)}) async-start(bf16[128,3,16,128]{3,2,1,0:T(8,128)(2,1)} %shard_map.103), calls=%async_computation | async-start | bytes 3145728 | tf_op jit(solution)/shard_map/all_to_all | solution.py:41
  24.6 3.3 %collective-permute-start = (bf16[3,256,384]{2,1,0:T(8,128)(2,1)S(1)}, bf16[3,256,384]{2,1,0:T(8,128)(2,1)S(1)}, u32[]{:S(2)}, u32[]{:S(2)}) collective-permute-start(bf16[3,256,384]{2,1,0:T(8,128)(2,1)S(1)} %bitcast.29), channel_id=1, source_target_pairs={{0,2},{2,0},{1,3},{3,1},{4,6},{6,4},{5,7},{7,5},{8,10},{10,8},{9,1... | collective-permute-start | bytes 1769480 | tf_op jit(solution)/shard_map/ppermute | solution.py:350
  27.9 1.9 collective-permute-start.1
  29.8 16.6 %collective-permute-done.w1_hbm = bf16[3,256,384]{2,1,0:T(8,128)(2,1)S(1)} collective-permute-done((bf16[3,256,384]{2,1,0:T(8,128)(2,1)S(1)}, bf16[3,256,384]{2,1,0:T(8,128)(2,1)S(1)}, u32[]{:S(2)}, u32[]{:S(2)}) %collective-permute-start) | collective-permute-done | bytes 589856 | tf_op jit(solution)/shard_map/ppermute | solution.py:350
  46.4 1.9 collective-permute-start.2
  48.4 2.0 collective-permute-done.2.w3_hbm
  50.4 51.5 %all-to-all-done.got_ref = bf16[128,3,16,128]{3,2,1,0:T(8,128)(2,1)S(1)} async-done(((bf16[128,3,16,128]{3,2,1,0:T(8,128)(2,1)}), bf16[128,3,16,128]{3,2,1,0:T(8,128)(2,1)S(1)}, u32[]{:S(2)}, u32[]{:S(2)}) %all-to-all-start) | async-done | bytes 1572896 | tf_op jit(solution)/shard_map/all_to_all | solution.py:41
  101.9 5.2 %shard_map.104 = (bf16[416,8,128]{2,1,0:T(8,128)(2,1)}, bf16[384,1024]{1,0:T(8,128)(2,1)}, bf16[384,1024]{1,0:T(8,128)(2,1)}, bf16[384,384]{1,0:T(8,128)(2,1)}, ...) custom-call(s32[4]{0:T(128)S(1)} %pad_add_fusion.place_ref, bf16[128,3,16,128]{3,2,1,0:T(8,128)(2,1)S(1)} %all-to-all-done.got_ref, ...), custom_call_target="tpu_custom_call" | custom-call | flops 1509949440 | bytes 8388608 | tf_op jit(solution)/shard_map/pallas_call | solution.py:185
  107.2 8.2 %all-to-all-start.1 = ((bf16[128,13,2,128]{3,2,1,0:T(2,128)(2,1)}), bf16[128,13,2,128]{3,2,1,0:T(2,128)(2,1)S(1)}, u32[]{:S(2)}, u32[]{:S(2)}) async-start(bf16[128,13,2,128]{3,2,1,0:T(2,128)(2,1)} %bitcast.33), calls=%async_computation.1 | async-start | bytes 1703936 | tf_op jit(solution)/shard_map/all_to_all | solution.py:41
  115.4 1.0 copy-done.8
  116.4 1.0 copy-done.9
  117.4 1.0 copy-done.10
  118.3 1.7 shard_map.105
  120.0 1.9 collective-permute-start.3
  121.9 2.8 %collective-permute-done.3.got_ref = bf16[2,3,256,384]{3,2,1,0:T(8,128)(2,1)S(1)} collective-permute-done((bf16[2,3,256,384]{3,2,1,0:T(8,128)(2,1)S(1)}, bf16[2,3,256,384]{3,2,1,0:T(8,128)(2,1)S(1)}, u32[]{:S(2)}, u32[]{:S(2)}) %collective-permute-start.3) | collective-permute-done | bytes 1179680 | tf_op jit(solution)/shard_map/ppermute | solution.py:356
  125.0 3.6 %collective-permute-start.4 = (bf16[3,256,384]{2,1,0:T(8,128)(2,1)S(1)}, bf16[3,256,384]{2,1,0:T(8,128)(2,1)S(1)}, u32[]{:S(2)}, u32[]{:S(2)}) collective-permute-start(bf16[3,256,384]{2,1,0:T(8,128)(2,1)S(1)} %get-tuple-element.30), channel_id=1, source_target_pairs={{0,2},{2,0},{1,3},{3,1},{4,6},{6,4},{5,7},{7,5},{8,10},{10,8},{9,1... | collective-permute-start | bytes 1769480 | tf_op jit(solution)/shard_map/ppermute | solution.py:358
  128.6 18.8 %collective-permute-done.4 = bf16[3,256,384]{2,1,0:T(8,128)(2,1)S(1)} collective-permute-done((bf16[3,256,384]{2,1,0:T(8,128)(2,1)S(1)}, bf16[3,256,384]{2,1,0:T(8,128)(2,1)S(1)}, u32[]{:S(2)}, u32[]{:S(2)}) %collective-permute-start.4) | collective-permute-done | bytes 589856 | tf_op jit(solution)/shard_map/ppermute | solution.py:358
  148.3 13.3 %all-to-all-done.1 = bf16[128,13,2,128]{3,2,1,0:T(2,128)(2,1)S(1)} async-done(((bf16[128,13,2,128]{3,2,1,0:T(2,128)(2,1)}), bf16[128,13,2,128]{3,2,1,0:T(2,128)(2,1)S(1)}, u32[]{:S(2)}, u32[]{:S(2)}) %all-to-all-start.1) | async-done | bytes 852000 | tf_op jit(solution)/shard_map/all_to_all | solution.py:41
  161.6 43.4 %all_to_all.20.in_ref = bf16[128,9,2,128]{3,2,1,0:T(2,128)(2,1)S(1)} all-to-all(bf16[128,9,2,128]{3,2,1,0:T(2,128)(2,1)S(1)} %bitcast.20), channel_id=1, replica_groups=mesh['expert'=128,'dp'=4] {'expert'}, dimensions={0} | all-to-all | bytes 1179648 | tf_op jit(solution)/shard_map/all_to_all | solution.py:41
  205.0 1.6 shard_map.109
  206.6 6.6 %all-to-all-start.3 = ((bf16[128,9,2,128]{3,2,1,0:T(2,128)(2,1)}), bf16[128,9,2,128]{3,2,1,0:T(2,128)(2,1)S(1)}, u32[]{:S(2)}, u32[]{:S(2)}) async-start(bf16[128,9,2,128]{3,2,1,0:T(2,128)(2,1)} %shard_map.109), calls=%async_computation.3 | async-start | bytes 1179648 | tf_op jit(solution)/shard_map/all_to_all | solution.py:41
  213.2 1.3 shard_map.108
  215.0 34.4 %all-to-all-done.3 = bf16[128,9,2,128]{3,2,1,0:T(2,128)(2,1)S(1)} async-done(((bf16[128,9,2,128]{3,2,1,0:T(2,128)(2,1)}), bf16[128,9,2,128]{3,2,1,0:T(2,128)(2,1)S(1)}, u32[]{:S(2)}, u32[]{:S(2)}) %all-to-all-start.3) | async-done | bytes 589856 | tf_op jit(solution)/shard_map/all_to_all | solution.py:41
  (25 shorter events, 2.6 us)
Async XLA Ops:
  3.9 20.7 %copy-start.5 = (bf16[1,3,256,384]{3,2,1,0:T(8,128)(2,1)S(1)}, bf16[1,3,256,384]{3,2,1,0:T(8,128)(2,1)}, u32[]{:S(2)}) copy-start(bf16[1,3,256,384]{3,2,1,0:T(8,128)(2,1)} %param.13) | copy-start | bytes 1769476
  3.9 98.0 %all-to-all-start = ((bf16[128,3,16,128]{3,2,1,0:T(8,128)(2,1)}), bf16[128,3,16,128]{3,2,1,0:T(8,128)(2,1)S(1)}, u32[]{:S(2)}, u32[]{:S(2)}) async-start(bf16[128,3,16,128]{3,2,1,0:T(8,128)(2,1)} %shard_map.103), calls=%async_computation | async-start | bytes 3145728 | tf_op jit(solution)/shard_map/all_to_all | solution.py:41
  24.6 21.8 %collective-permute-start = (bf16[3,256,384]{2,1,0:T(8,128)(2,1)S(1)}, bf16[3,256,384]{2,1,0:T(8,128)(2,1)S(1)}, u32[]{:S(2)}, u32[]{:S(2)}) collective-permute-start(bf16[3,256,384]{2,1,0:T(8,128)(2,1)S(1)} %bitcast.29), channel_id=1, source_target_pairs={{0,2},{2,0},{1,3},{3,1},{4,6},{6,4},{5,7},{7,5},{8,10},{10,8},{9,1... | collective-permute-start | bytes 1769480 | tf_op jit(solution)/shard_map/ppermute | solution.py:350
  27.9 20.5 %collective-permute-start.1 = (bf16[3,256,384]{2,1,0:T(8,128)(2,1)S(1)}, bf16[3,256,384]{2,1,0:T(8,128)(2,1)S(1)}, u32[]{:S(2)}, u32[]{:S(2)}) collective-permute-start(bf16[3,256,384]{2,1,0:T(8,128)(2,1)S(1)} %bitcast.30), channel_id=1, source_target_pairs={{0,1},{1,0},{2,3},{3,2},{4,5},{5,4},{6,7},{7,6},{8,9},{9,8},{10,11... | collective-permute-start | bytes 1769480 | tf_op jit(solution)/shard_map/ppermute | solution.py:351
  46.4 4.0 %collective-permute-start.2 = (bf16[3,256,384]{2,1,0:T(8,128)(2,1)S(1)}, bf16[3,256,384]{2,1,0:T(8,128)(2,1)}, u32[]{:S(2)}, u32[]{:S(2)}) collective-permute-start(bf16[3,256,384]{2,1,0:T(8,128)(2,1)S(1)} %collective-permute-done.w1_hbm), channel_id=1, source_target_pairs={{0,1},{1,0},{2,3},{3,2},{4,5},{5,4},{6,7},{7,6},{8,9},{9,8},{10,11... | collective-permute-start | bytes 1769480 | tf_op jit(solution)/shard_map/ppermute | solution.py:351
  107.2 8.2 %copy-start.6 = (bf16[384,1024]{1,0:T(8,128)(2,1)S(1)}, bf16[384,1024]{1,0:T(8,128)(2,1)}, u32[]{:S(2)}) copy-start(bf16[384,1024]{1,0:T(8,128)(2,1)} %get-tuple-element.22.x_ref) | copy-start | bytes 2359300
  107.2 8.2 %copy-start.7 = (bf16[384,1024]{1,0:T(8,128)(2,1)S(1)}, bf16[384,1024]{1,0:T(8,128)(2,1)}, u32[]{:S(2)}) copy-start(bf16[384,1024]{1,0:T(8,128)(2,1)} %get-tuple-element.23.q_ref) | copy-start | bytes 2359300
  107.2 54.4 %all-to-all-start.1 = ((bf16[128,13,2,128]{3,2,1,0:T(2,128)(2,1)}), bf16[128,13,2,128]{3,2,1,0:T(2,128)(2,1)S(1)}, u32[]{:S(2)}, u32[]{:S(2)}) async-start(bf16[128,13,2,128]{3,2,1,0:T(2,128)(2,1)} %bitcast.33), calls=%async_computation.1 | async-start | bytes 1703936 | tf_op jit(solution)/shard_map/all_to_all | solution.py:41
  115.4 1.0 copy-start.8
  116.4 1.0 copy-start.9
  117.3 1.0 copy-start.10
  120.0 4.7 %collective-permute-start.3 = (bf16[2,3,256,384]{3,2,1,0:T(8,128)(2,1)S(1)}, bf16[2,3,256,384]{3,2,1,0:T(8,128)(2,1)S(1)}, u32[]{:S(2)}, u32[]{:S(2)}) collective-permute-start(bf16[2,3,256,384]{3,2,1,0:T(8,128)(2,1)S(1)} %get-tuple-element.28), channel_id=1, source_target_pairs={{0,1},{1,0},{2,3},{3,2},{4,5},{5,4},{6,7},{7,6},{8,9},{9,8},{10,11... | collective-permute-start | bytes 3538952 | tf_op jit(solution)/shard_map/ppermute | solution.py:356
  124.7 22.7 %copy-start = (f32[1,3,256,384]{3,2,1,0:T(8,128)S(1)}, f32[1,3,256,384]{3,2,1,0:T(8,128)}, u32[]{:S(2)}) copy-start(f32[1,3,256,384]{3,2,1,0:T(8,128)} %param.14) | copy-start | bytes 3538948
  124.7 22.7 %copy-start.1 = (f32[1,3,256,384]{3,2,1,0:T(8,128)S(1)}, f32[1,3,256,384]{3,2,1,0:T(8,128)}, u32[]{:S(2)}) copy-start(f32[1,3,256,384]{3,2,1,0:T(8,128)} %param.15) | copy-start | bytes 3538948
  125.0 22.4 %collective-permute-start.4 = (bf16[3,256,384]{2,1,0:T(8,128)(2,1)S(1)}, bf16[3,256,384]{2,1,0:T(8,128)(2,1)S(1)}, u32[]{:S(2)}, u32[]{:S(2)}) collective-permute-start(bf16[3,256,384]{2,1,0:T(8,128)(2,1)S(1)} %get-tuple-element.30), channel_id=1, source_target_pairs={{0,2},{2,0},{1,3},{3,1},{4,6},{6,4},{5,7},{7,5},{8,10},{10,8},{9,1... | collective-permute-start | bytes 1769480 | tf_op jit(solution)/shard_map/ppermute | solution.py:358
  148.3 56.8 %copy-start.4 = (s32[128]{0:T(128)S(1)}, s32[128]{0:T(128)}, u32[]{:S(2)}) copy-start(s32[128]{0:T(128)} %partner_ref.1) | copy-start | bytes 1540
  205.0 8.2 %copy-start.2 = (s32[128,2]{0,1:T(2,128)S(1)}, s32[128,2]{0,1:T(2,128)}, u32[]{:S(2)}) copy-start(s32[128,2]{0,1:T(2,128)} %param.10) | copy-start | bytes 3076
  205.0 8.2 %copy-start.3 = (bf16[128,2]{0,1:T(2,128)(2,1)S(1)}, bf16[128,2]{0,1:T(2,128)(2,1)}, u32[]{:S(2)}) copy-start(bf16[128,2]{0,1:T(2,128)(2,1)} %param.11) | copy-start | bytes 1540
  206.6 42.8 %all-to-all-start.3 = ((bf16[128,9,2,128]{3,2,1,0:T(2,128)(2,1)}), bf16[128,9,2,128]{3,2,1,0:T(2,128)(2,1)S(1)}, u32[]{:S(2)}, u32[]{:S(2)}) async-start(bf16[128,9,2,128]{3,2,1,0:T(2,128)(2,1)} %shard_map.109), calls=%async_computation.3 | async-start | bytes 1179648 | tf_op jit(solution)/shard_map/all_to_all | solution.py:41
